TPU v7x, 32 devices: a whole 2x2x4 slice. The times are simulated.
32 devices in a mesh: seq: 8 (over z, core), tp: 4 (over y, x).
Axes of the slice: x: 2, y: 2, z: 4, core: 2. Of those that a mesh axis runs over, the one named last changes fastest.
Arguments:
- tokens: bfloat16 [4096, 2048], P(('seq', 'tp')), may hold values from -6 to 6
- mixer_gain: bfloat16 [2048], P('tp'), may hold values from 0.5 to 1.5
- in_proj: bfloat16 [2048, 2816], P(None, 'tp'), may hold values from -0.125 to 0.125
- branch_proj: bfloat16 [2048, 2816], P(None, 'tp'), may hold values from -0.125 to 0.125
- conv_taps: float32 [4, 2816], P(None, 'tp'), may hold values from -3 to 3
- conv_bias: float32 [2816], P('tp'), may hold values from -3 to 3
- rate_blocks: bfloat16 [16, 176, 176], P('tp'), may hold values from -0.4375 to 0.4375
- rate_bias: float32 [2816], P('tp'), may hold values from -4 to 4
- input_blocks: bfloat16 [16, 176, 176], P('tp'), may hold values from -0.4375 to 0.4375
- input_bias: float32 [2816], P('tp'), may hold values from -4 to 4
- decay_param: float32 [2816], P('tp')
- out_proj: bfloat16 [2816, 2048], P('tp'), may hold values from -0.4375 to 0.4375
- dense_gain: bfloat16 [2048], P('tp'), may hold values from 0.5 to 1.5
- gate_proj: bfloat16 [2048, 6144], P(None, 'tp'), may hold values from -0.125 to 0.125
- up_proj: bfloat16 [2048, 6144], P(None, 'tp'), may hold values from -0.125 to 0.125
- down_proj: bfloat16 [6144, 2048], P('tp'), may hold values from -0.15625 to 0.15625
- segment_ids: int32 [4096], P('seq'), may hold values from 0 to 6, as said below
- cotangent: bfloat16 [4096, 2048], P(('seq', 'tp')), may hold values from -6 to 6
Outputs:
- output: bfloat16 [4096, 2048], P(('seq', 'tp'))
- tokens_grad: float32 [4096, 2048], P(('seq', 'tp'))
- mixer_gain_grad: float32 [2048], P('tp')
- in_proj_grad: float32 [2048, 2816], P(None, 'tp')
- branch_proj_grad: float32 [2048, 2816], P(None, 'tp')
- conv_taps_grad: float32 [4, 2816], P(None, 'tp')
- conv_bias_grad: float32 [2816], P('tp')
- rate_blocks_grad: float32 [16, 176, 176], P('tp')
- rate_bias_grad: float32 [2816], P('tp')
- input_blocks_grad: float32 [16, 176, 176], P('tp')
- input_bias_grad: float32 [2816], P('tp')
- decay_grad: float32 [2816], P('tp')
- out_proj_grad: float32 [2816, 2048], P('tp')
- dense_gain_grad: float32 [2048], P('tp')
- gate_proj_grad: float32 [2048, 6144], P(None, 'tp')
- up_proj_grad: float32 [2048, 6144], P(None, 'tp')
- down_proj_grad: float32 [6144, 2048], P('tp')
Inputs may be any that keep to these rules, and one draw needn't show every extreme that they name: `segment_ids`: ids never fall along the stream, begin at 0 and end at 6; a new id marks a document start.
All inputs are finite; a program needn't handle non-finite values.
Results may differ from a plain program's by a relative error of at most 0.015.
Values may be sent and summed in bfloat16 or wider, within the bound.
No kernel may reach another device: no remote copies, remote signals or barrier semaphores. Data moves between devices by JAX's collectives and lax.ppermute only.
A program may use at most 320 MiB of HBM per device.

v0:
```python
import math

import jax
import jax.numpy as jnp
from jax import lax
from jax.sharding import PartitionSpec as P

epsilon = 1e-06
HIGHEST = lax.Precision.HIGHEST


def prefix(part, axis, combine, identity, reverse):
    count = lax.axis_size(axis)
    place = lax.axis_index(axis)
    ahead = count - 1 - place if reverse else place
    gathered = jax.tree.map(lambda a: lax.all_gather(a, axis), part)
    state = jax.tree.map(lambda a, e: jnp.zeros_like(a) + jnp.asarray(e, a.dtype), part, identity)

    def one(hop, state):
        source = count - 1 - hop if reverse else hop
        return combine(
            state, jax.tree.map(lambda a: lax.dynamic_index_in_dim(a, source, 0, False), gathered)
        )

    return lax.fori_loop(0, ahead, one, state)


def shifted(value, axis, by):
    peers = lax.axis_size(axis)
    pairs = [(i, i + by) for i in range(peers) if 0 <= i + by < peers]
    return lax.ppermute(value, axis, pairs)


def product(left, right):
    return jnp.dot(left, right, preferred_element_type=jnp.float32)


def product_left_t(left, right):
    return lax.dot_general(
        left, right, (((0,), (0,)), ((), ())), preferred_element_type=jnp.float32
    )


def product_right_t(left, right):
    return lax.dot_general(
        left, right, (((1,), (1,)), ((), ())), preferred_element_type=jnp.float32
    )


def rms_scale(values):
    return values * lax.rsqrt(jnp.mean(values * values, axis=-1, keepdims=True) + epsilon)


def gelu_tanh(values):
    return jax.nn.gelu(values, approximate=True)


def dense_act(gate_values, up_values):
    return gelu_tanh(gate_values) * up_values


def scaled_norm(values, scale):
    return rms_scale(values) * scale


def combine(earlier, later):
    return (earlier[0] * later[0], later[0] * earlier[1] + later[1])


def causal_conv(inner_values, rim_values, own_ids, rim_ids, taps, bias):
    rim_width = taps.shape[0] - 1
    length, width = inner_values.shape
    block_len = math.gcd(length, 128)
    block_count = length // block_len
    rows_three = inner_values.reshape(block_count, block_len, width)
    tails = jnp.concatenate([rim_values[None], rows_three[:-1, block_len - rim_width :]], axis=0)
    ext_ids = jnp.concatenate([rim_ids, own_ids], axis=0)
    target = jnp.arange(block_len, dtype=jnp.int32)
    source = jnp.arange(block_len, dtype=jnp.int32)
    rim_place = jnp.arange(rim_width, dtype=jnp.int32)
    result = jnp.broadcast_to(bias, (length, width))
    for offset in range(taps.shape[0]):
        inside = (target[:, None] - offset == source[None, :]).astype(jnp.float32)
        across = (target[:, None] - offset + rim_width == rim_place[None, :]).astype(jnp.float32)
        window = jnp.einsum("ts,bsc->btc", inside, rows_three, precision=HIGHEST)
        window = window + jnp.einsum("tj,bjc->btc", across, tails, precision=HIGHEST)
        same = (ext_ids[rim_width - offset : rim_width - offset + length] == own_ids).astype(
            jnp.float32
        )
        result = result + taps[offset] * window.reshape(length, width) * same[:, None]
    return result


def gate_terms(rate_raw, input_raw, conv_out, rate_bias, input_bias, decay_param, starts):
    log_decay = -8.0 * jax.nn.sigmoid(rate_raw + rate_bias) * jax.nn.softplus(-decay_param)
    keep = jnp.exp(log_decay) * (1.0 - starts)[:, None]
    drive = (
        jnp.sqrt(-jnp.expm1(2.0 * log_decay)) * jax.nn.sigmoid(input_raw + input_bias) * conv_out
    )
    return (keep, drive)


def dense_blocks(blocks):
    count, rows_in, cols_out = blocks.shape
    dense = jnp.zeros((count * rows_in, count * cols_out), blocks.dtype)
    for which in range(count):
        dense = dense.at[
            which * rows_in : (which + 1) * rows_in, which * cols_out : (which + 1) * cols_out
        ].set(blocks[which])
    return dense


def block_weight(values, grads, blocks):
    count, rows_in, cols_out = blocks.shape
    full = product_left_t(values, grads)
    return jnp.stack(
        [
            full[which * rows_in : (which + 1) * rows_in, which * cols_out : (which + 1) * cols_out]
            for which in range(count)
        ],
        axis=0,
    )


def carry_prefix(summary, backward):
    identity = (jnp.ones_like(summary[0]), jnp.zeros_like(summary[1]))
    return prefix(summary, "seq", combine, identity, backward)


def project_branch(normed, in_proj, branch_proj):
    return (product(normed, in_proj), product(normed, branch_proj))


def recur_local(
    inner_proj,
    rim_values,
    rim_ids,
    ids_float,
    conv_taps,
    conv_bias,
    rate_dense,
    rate_bias,
    input_dense,
    input_bias,
    decay_param,
):
    rim_width = conv_taps.shape[0] - 1
    ext_ids = jnp.concatenate([rim_ids, ids_float], axis=0)
    conv_out = causal_conv(inner_proj, rim_values, ids_float, rim_ids, conv_taps, conv_bias)
    starts = (ext_ids[rim_width:] != ext_ids[rim_width - 1 : -1]).astype(jnp.float32)
    conv_low = conv_out.astype(jnp.bfloat16)
    rate_raw = product(conv_low, rate_dense)
    input_raw = product(conv_low, input_dense)
    keep, drive = gate_terms(
        rate_raw, input_raw, conv_out, rate_bias, input_bias, decay_param, starts
    )
    prefix_keep, prefix_drive = lax.associative_scan(combine, (keep, drive), axis=0)
    return (
        inner_proj,
        ext_ids,
        starts,
        conv_out,
        conv_low,
        rate_raw,
        input_raw,
        keep,
        prefix_keep,
        prefix_drive,
    )


def shards(
    tokens,
    mixer_gain,
    in_proj,
    branch_proj,
    conv_taps,
    conv_bias,
    rate_blocks,
    rate_bias,
    input_blocks,
    input_bias,
    decay_param,
    out_proj,
    dense_gain,
    gate_proj,
    up_proj,
    down_proj,
    segment_ids,
    cotangent,
):
    tp_place = lax.axis_index("tp")
    gain_share = mixer_gain.shape[0]
    rim_width = conv_taps.shape[0] - 1
    rate_dense = dense_blocks(rate_blocks)
    input_dense = dense_blocks(input_blocks)
    gathered, cot_rows, mixer_full, dense_full = (
        lax.all_gather(tokens, "tp", axis=0, tiled=True),
        lax.all_gather(cotangent, "tp", axis=0, tiled=True),
        lax.all_gather(mixer_gain, "tp", axis=0, tiled=True),
        lax.all_gather(dense_gain, "tp", axis=0, tiled=True),
    )
    mixer_scale = mixer_full.astype(jnp.float32)
    dense_scale = dense_full.astype(jnp.float32)
    normed = (rms_scale(gathered.astype(jnp.float32)) * mixer_scale).astype(jnp.bfloat16)
    ids_float = segment_ids.astype(jnp.float32)
    inner_proj, branch_pre = project_branch(normed, in_proj, branch_proj)
    rim_values, rim_ids = shifted((inner_proj[-rim_width:], ids_float[-rim_width:]), "seq", 1)
    local_parts = recur_local(
        inner_proj,
        rim_values,
        rim_ids,
        ids_float,
        conv_taps,
        conv_bias,
        rate_dense,
        rate_bias,
        input_dense,
        input_bias,
        decay_param,
    )
    prefix_keep = local_parts[8]
    prefix_drive = local_parts[9]
    prior = carry_prefix((prefix_keep[-1], prefix_drive[-1]), False)
    state_in = prior[1]
    state = prefix_drive + prefix_keep * state_in
    branch = gelu_tanh(branch_pre)
    mixed = (state * branch).astype(jnp.bfloat16)
    mixer_out = lax.psum_scatter(product(mixed, out_proj), "tp", scatter_dimension=0, tiled=True)
    mid = tokens.astype(jnp.float32) + mixer_out
    normed_float, dense_pull = jax.vjp(scaled_norm, mid, dense_scale)
    normed_two = normed_float.astype(jnp.bfloat16)
    rows_two = lax.all_gather(normed_two, "tp", axis=0, tiled=True)
    gate_pre = product(rows_two, gate_proj)
    up_pre = product(rows_two, up_proj)
    hidden_float, act_pull = jax.vjp(dense_act, gate_pre, up_pre)
    hidden = hidden_float.astype(jnp.bfloat16)
    dense_out = lax.psum_scatter(
        product(hidden, down_proj).astype(jnp.bfloat16), "tp", scatter_dimension=0, tiled=True
    ).astype(jnp.float32)
    output = (mid + dense_out).astype(jnp.bfloat16)
    down_grad = product_left_t(hidden, cot_rows)
    hidden_grad = product_right_t(cot_rows, down_proj)
    gate_float, up_float = act_pull(hidden_grad)
    gate_grad = gate_float.astype(jnp.bfloat16)
    up_grad = up_float.astype(jnp.bfloat16)
    gate_w_grad = product_left_t(rows_two, gate_grad)
    up_w_grad = product_left_t(rows_two, up_grad)
    normed_two_grad = lax.psum_scatter(
        (product_right_t(gate_grad, gate_proj) + product_right_t(up_grad, up_proj)).astype(
            jnp.bfloat16
        ),
        "tp",
        scatter_dimension=0,
        tiled=True,
    ).astype(jnp.float32)
    mid_from_norm, dense_gain_part = dense_pull(normed_two_grad)
    mid_grad = cotangent.astype(jnp.float32) + mid_from_norm
    mid_rows = lax.all_gather(mid_grad.astype(jnp.bfloat16), "tp", axis=0, tiled=True)
    out_w_grad = product_left_t(mixed, mid_rows)
    mixed_grad = product_right_t(mid_rows, out_proj)
    normed_again, rim_values_again, rim_ids_again, state_again = lax.optimization_barrier(
        (normed, rim_values, rim_ids, state_in)
    )
    inner_again, branch_pre_again = project_branch(normed_again, in_proj, branch_proj)
    parts_again = recur_local(
        inner_again,
        rim_values_again,
        rim_ids_again,
        ids_float,
        conv_taps,
        conv_bias,
        rate_dense,
        rate_bias,
        input_dense,
        input_bias,
        decay_param,
    )
    work_state = parts_again[9] + parts_again[8] * state_again
    (
        work_inner,
        ext_ids,
        starts,
        conv_out,
        conv_low,
        rate_raw,
        input_raw,
        keep,
        unused_keep,
        unused_drive,
    ) = parts_again
    work_branch, branch_pull = jax.vjp(gelu_tanh, branch_pre_again)
    state_direct = mixed_grad * work_branch
    branch_grad = mixed_grad * work_state
    shifted_keep = jnp.concatenate([keep[1:], jnp.ones_like(keep[:1])], axis=0)
    back_keep, back_grad = lax.associative_scan(
        combine, (jnp.flip(shifted_keep, 0), jnp.flip(state_direct, 0)), axis=0
    )
    suffix_keep = jnp.flip(back_keep, 0)
    suffix_grad = jnp.flip(back_grad, 0)
    after = carry_prefix((keep[0] * suffix_keep[0], keep[0] * suffix_grad[0]), True)
    state_grad = suffix_grad + suffix_keep * after[1]
    state_prev = jnp.concatenate([state_in[None], work_state[:-1]], axis=0)
    keep_grad = state_grad * state_prev

    def gate_six(rate_values, input_values, conv_values, rate_offset, input_offset, decay_values):
        return gate_terms(
            rate_values, input_values, conv_values, rate_offset, input_offset, decay_values, starts
        )

    unused_gates, gate_pull = jax.vjp(
        gate_six, rate_raw, input_raw, conv_out, rate_bias, input_bias, decay_param
    )
    rate_float, input_float, conv_direct, rate_bias_grad, input_bias_grad, decay_grad = gate_pull(
        (keep_grad, state_grad)
    )
    rate_low = rate_float.astype(jnp.bfloat16)
    input_low = input_float.astype(jnp.bfloat16)
    rate_w_grad = block_weight(conv_low, rate_low, rate_blocks)
    input_w_grad = block_weight(conv_low, input_low, input_blocks)
    conv_grad = (
        conv_direct
        + product_right_t(rate_low, rate_dense)
        + product_right_t(input_low, input_dense)
    )
    rim_id_part = ext_ids[:rim_width]

    def conv_local(inner_values, rim_part, taps, bias):
        return causal_conv(inner_values, rim_part, ids_float, rim_id_part, taps, bias)

    unused_conv, conv_pull = jax.vjp(conv_local, work_inner, rim_values_again, conv_taps, conv_bias)
    inner_direct, rim_part_grad, taps_grad, bias_grad = conv_pull(conv_grad)
    rim_grad = shifted(rim_part_grad, "seq", -1)
    length = inner_direct.shape[0]
    inner_grad = inner_direct.at[length - rim_width :].add(rim_grad).astype(jnp.bfloat16)
    branch_pre_grad = branch_pull(branch_grad)[0].astype(jnp.bfloat16)
    in_w_grad = product_left_t(normed, inner_grad)
    branch_w_grad = product_left_t(normed, branch_pre_grad)
    normed_grad = lax.psum_scatter(
        (
            product_right_t(inner_grad, in_proj) + product_right_t(branch_pre_grad, branch_proj)
        ).astype(jnp.bfloat16),
        "tp",
        scatter_dimension=0,
        tiled=True,
    ).astype(jnp.float32)
    unused_norm, mixer_pull = jax.vjp(scaled_norm, tokens.astype(jnp.float32), mixer_scale)
    rows_grad, mixer_gain_part = mixer_pull(normed_grad)
    tokens_grad = mid_grad + rows_grad
    mixer_total, dense_total = lax.psum((mixer_gain_part, dense_gain_part), ("seq", "tp"))
    mixer_gain_grad = lax.dynamic_slice_in_dim(mixer_total, tp_place * gain_share, gain_share, 0)
    dense_gain_grad = lax.dynamic_slice_in_dim(dense_total, tp_place * gain_share, gain_share, 0)
    summed = (
        lax.psum(in_w_grad.astype(jnp.bfloat16), "seq").astype(jnp.float32),
        lax.psum(branch_w_grad.astype(jnp.bfloat16), "seq").astype(jnp.float32),
        lax.psum(taps_grad.astype(jnp.bfloat16), "seq").astype(jnp.float32),
        lax.psum(bias_grad.astype(jnp.bfloat16), "seq").astype(jnp.float32),
        lax.psum(rate_w_grad.astype(jnp.bfloat16), "seq").astype(jnp.float32),
        lax.psum(rate_bias_grad.astype(jnp.bfloat16), "seq").astype(jnp.float32),
        lax.psum(input_w_grad.astype(jnp.bfloat16), "seq").astype(jnp.float32),
        lax.psum(input_bias_grad.astype(jnp.bfloat16), "seq").astype(jnp.float32),
        lax.psum(decay_grad.astype(jnp.bfloat16), "seq").astype(jnp.float32),
        lax.psum(out_w_grad.astype(jnp.bfloat16), "seq").astype(jnp.float32),
        lax.psum(gate_w_grad.astype(jnp.bfloat16), "seq").astype(jnp.float32),
        lax.psum(up_w_grad.astype(jnp.bfloat16), "seq").astype(jnp.float32),
        lax.psum(down_grad.astype(jnp.bfloat16), "seq").astype(jnp.float32),
    )
    return (
        output,
        tokens_grad,
        mixer_gain_grad,
        summed[0],
        summed[1],
        summed[2],
        summed[3],
        summed[4],
        summed[5],
        summed[6],
        summed[7],
        summed[8],
        summed[9],
        dense_gain_grad,
        summed[10],
        summed[11],
        summed[12],
    )


def solution(mesh):
    return jax.shard_map(
        shards,
        mesh=mesh,
        in_specs=(
            P(("seq", "tp"), None),
            P("tp"),
            P(None, "tp"),
            P(None, "tp"),
            P(None, "tp"),
            P("tp"),
            P("tp", None, None),
            P("tp"),
            P("tp", None, None),
            P("tp"),
            P("tp"),
            P("tp", None),
            P("tp"),
            P(None, "tp"),
            P(None, "tp"),
            P("tp", None),
            P("seq"),
            P(("seq", "tp"), None),
        ),
        out_specs=(
            P(("seq", "tp"), None),
            P(("seq", "tp"), None),
            P("tp"),
            P(None, "tp"),
            P(None, "tp"),
            P(None, "tp"),
            P("tp"),
            P("tp", None, None),
            P("tp"),
            P("tp", None, None),
            P("tp"),
            P("tp"),
            P("tp", None),
            P("tp"),
            P(None, "tp"),
            P(None, "tp"),
            P("tp", None),
        ),
        check_vma=False,
    )
```

profile of v0, /device:TPU:0, one launch (start us, length us, event | category | flops | bytes accessed | tf_op | source)
XLA Modules:
  0.0 3581.4 jit_solution(10300524862556435803)
XLA Ops:
  85.9 28.4 slice.1201
  114.3 28.3 slice.1139
  200.9 28.5 slice.1137
  766.6 28.8 pad.403
  795.5 28.7 pad.404
  842.0 28.6 pad.421
  870.6 28.9 pad.422
  934.0 44.4 %reduce-scatter.5.cloned.1.call-done = f32[128,2048]{1,0:T(8,128)} async-done(((f32[512,2048]{1,0:T(8,128)}), f32[128,2048]{1,0:T(8,128)}) %reduce-scatter.5.cloned.1.call-update) | async-done | bytes 1048592 | tf_op jit(solution)/shard_map/reduce_scatter | solution.py:229
  1084.9 28.5 slice.1322
  1170.0 28.3 slice.1320
  1608.5 28.3 slice.1236
  1636.8 28.4 slice.1229
  1665.2 28.3 slice.1227
  1904.2 28.6 pad.493
  1935.0 28.9 pad.475
  1963.8 28.8 pad.476
  1992.6 28.6 pad.494
  2666.2 28.8 pad.439
  2695.1 28.7 pad.440
  2723.8 28.7 pad.457
  2752.5 29.0 pad.458
  2944.2 29.5 all-reduce.118
  2978.3 37.9 %all-reduce.117 = (f32[2048]{0:T(1024)S(1)}, f32[2048]{0:T(1024)S(1)}) all-reduce(f32[2048]{0:T(1024)S(1)} %get-tuple-element.272, f32[2048]{0:T(1024)S(1)} %copy-done.198), channel_id=1, replica_groups=mesh['seq'=8,'tp'=4] {'seq','tp'}, use_global_device_ids=true, to_apply=%region_14.15 | all-reduce | flops 4096 | bytes 32768 | tf_op jit(solution)/shard_map/psum | solution.py:350
  3021.1 515.5 %all-reduce.122.cloned.1.call-done = (bf16[2048,704]{0,1:T(8,128)(2,1)}, bf16[2048,704]{0,1:T(8,128)(2,1)}, bf16[4,176,176]{2,1,0:T(8,128)(2,1)}, bf16[4,176,176...) async-done(((bf16[2048,704]{0,1:T(8,128)(2,1)}, ...) | async-done | bytes 28020752 | tf_op jit(solution)/shard_map/psum | solution.py:354
  (1143 shorter events, 2365.5 us)
Async XLA Ops:
  7.2 907.7 %copy-start = (bf16[2048,704]{0,1:T(8,128)(2,1)S(1)}, bf16[2048,704]{0,1:T(8,128)(2,1)}, u32[]{:S(2)}) copy-start(bf16[2048,704]{0,1:T(8,128)(2,1)} %param.43) | copy-start | bytes 8650756
  7.2 40.7 %all-gather.11.cloned.1.call-start = ((), (), s32[]{:S(2)}) async-start(), calls=%async_computation.4 | async-start | bytes 2621440 | tf_op jit(solution)/shard_map/all_gather | solution.py:198
  7.9 970.4 %reduce-scatter.5.cloned.1.call-start = ((), (), s32[]{:S(2)}) async-start(), calls=%async_computation.5 | async-start | bytes 5242880 | tf_op jit(solution)/shard_map/reduce_scatter | solution.py:229
  9.4 36.4 %collective-permute-start.1 = (f32[3]{0:T(128)}, f32[3]{0:T(128)}, u32[]{:S(2)}, u32[]{:S(2)}) collective-permute-start(f32[3]{0:T(128)} %slice.1121), channel_id=1, source_target_pairs={{0,4},{4,8},{8,12},{12,16},{16,20},{20,24},{24,28},{1,5},{5,9},{9,... | collective-permute-start | bytes 44 | tf_op jit(solution)/shard_map/ppermute | solution.py:31
  45.5 956.1 %copy-start.217 = (s32[128]{0:T(128)}, s32[128]{0:T(128)S(1)}, u32[]{:S(2)}) copy-start(s32[128]{0:T(128)S(1)} %iota_add_fusion.4) | copy-start | bytes 1540
  45.6 950.7 %copy-start.221 = (s32[128]{0:T(128)}, s32[128]{0:T(128)S(1)}, u32[]{:S(2)}) copy-start(s32[128]{0:T(128)S(1)} %iota_add_fusion.3) | copy-start | bytes 1540
  45.6 956.9 %copy-start.215 = (s32[128]{0:T(128)}, s32[128]{0:T(128)S(1)}, u32[]{:S(2)}) copy-start(s32[128]{0:T(128)S(1)} %iota_add_fusion.2) | copy-start | bytes 1540
  45.6 952.0 %copy-start.219 = (s32[128]{0:T(128)}, s32[128]{0:T(128)S(1)}, u32[]{:S(2)}) copy-start(s32[128]{0:T(128)S(1)} %iota_add_fusion.1) | copy-start | bytes 1540
  45.6 957.8 %copy-start.213 = (s32[128]{0:T(128)}, s32[128]{0:T(128)S(1)}, u32[]{:S(2)}) copy-start(s32[128]{0:T(128)S(1)} %iota_add_fusion) | copy-start | bytes 1540
  45.7 960.2 %copy-start.189 = (f32[704]{0:T(1024)}, f32[704]{0:T(1024)S(1)}, u32[]{:S(2)}) copy-start(f32[704]{0:T(1024)S(1)} %get-tuple-element.274) | copy-start | bytes 8452
  45.7 960.2 %copy-start.191 = (f32[704]{0:T(1024)}, f32[704]{0:T(1024)S(1)}, u32[]{:S(2)}) copy-start(f32[704]{0:T(1024)S(1)} %get-tuple-element.275) | copy-start | bytes 8452
  45.7 960.2 %copy-start.193 = (f32[704]{0:T(1024)}, f32[704]{0:T(1024)S(1)}, u32[]{:S(2)}) copy-start(f32[704]{0:T(1024)S(1)} %get-tuple-element.276) | copy-start | bytes 8452
  45.7 960.2 %copy-start.195 = (f32[704]{0:T(1024)}, f32[704]{0:T(1024)S(1)}, u32[]{:S(2)}) copy-start(f32[704]{0:T(1024)S(1)} %get-tuple-element.277) | copy-start | bytes 8452
  46.6 959.4 %copy-start.199 = (f32[512]{0:T(512)}, f32[512]{0:T(512)S(1)}, u32[]{:S(2)}) copy-start(f32[512]{0:T(512)S(1)} %get-tuple-element.486) | copy-start | bytes 6148
  54.8 17.6 collective-permute-start
  925.3 92.5 %all-gather.13.cloned.1.call-start = ((), (), s32[]{:S(2)}) async-start(), calls=%async_computation.6 | async-start | bytes 2621440 | tf_op jit(solution)/shard_map/all_gather | solution.py:233
  934.0 525.7 %copy-start.185 = (f32[4,1,512]{2,1,0:T(1,128)}, f32[4,1,512]{2,1,0:T(1,128)S(1)}, u32[]{:S(2)}) copy-start(f32[4,1,512]{2,1,0:T(1,128)S(1)} %convert_element_type.269) | copy-start | bytes 24580
  982.3 72.7 %all-gather.15.cloned.1.call-start = ((), (), s32[]{:S(2)}) async-start(), calls=%async_computation.8 | async-start | bytes 2621440 | tf_op jit(solution)/shard_map/all_gather | solution.py:199
  982.9 474.3 %reduce-scatter.9.cloned.1.call-start = ((), (), s32[]{:S(2)}) async-start(), calls=%async_computation.9 | async-start | bytes 2621440 | tf_op jit(solution)/shard_map/reduce_scatter | solution.py:249
  1078.5 942.8 %all-gather.17.cloned.1.call-start = ((), (), s32[]{:S(2)}) async-start(), calls=%async_computation.10 | async-start | bytes 2621440 | tf_op jit(solution)/shard_map/all_gather | solution.py:259
  1461.9 1514.8 %reduce-scatter.11.cloned.1.call-start = ((), (), s32[]{:S(2)}) async-start(), calls=%async_computation.11 | async-start | bytes 2621440 | tf_op jit(solution)/shard_map/reduce_scatter | solution.py:339
  2868.0 24.0 collective-permute-start.2
  2902.1 115.4 %reduce-scatter.7.cloned.1.call-start = ((), (), s32[]{:S(2)}) async-start(), calls=%async_computation.7 | async-start | bytes 2621440 | tf_op jit(solution)/shard_map/reduce_scatter | solution.py:238
  2910.2 626.4 %all-reduce.122.cloned.1.call-start = ((), (), s32[]{:S(2)}) async-start(), calls=%async_computation.12 | async-start | bytes 56492032 | tf_op jit(solution)/shard_map/psum | solution.py:354
  (235 other events, 2122.9 us)
Sparse Core Ops, SparseCore 0:
  9.9 38.0 all-gather.10
  925.4 52.8 reduce-scatter.4
  982.4 35.2 all-gather.12
  1019.6 35.2 all-gather.14
  1078.6 35.1 reduce-scatter.8
  1462.0 35.3 all-gather.16
  2902.2 35.3 reduce-scatter.10
  2940.8 35.1 reduce-scatter.6
  2981.2 555.3 all-reduce.121
where the time goes:
time: 3610 us; the launch traced here: 3580 us
  local copies, waits for them, and re-layouts  2340 us (65%)
  waiting for transfers between devices  590 us (16%)
  other arithmetic  322 us (9%)
  matrix products  166 us (5%)
  blocking collectives  140 us (4%)
    slice x101, local copies, waits for them, and re-layouts, recur_local(): lax.associative_scan(combine, (keep, drive), axis=0)  873 us
    pad x64, local copies, waits for them, and re-layouts, recur_local(): lax.associative_scan(combine, (keep, drive), axis=0)  556 us
    psum x1, waiting for transfers between devices, shards(): lax.psum(in_w_grad.astype(jnp.bfloat16), 'seq').astype(jnp.float32)  516 us
    slice x54, local copies, waits for them, and re-layouts, shards(): lax.associative_scan(combine, (jnp.flip(shifted_keep, 0), jnp.flip(state_...  470 us
    pad x32, local copies, waits for them, and re-layouts, shards(): lax.associative_scan(combine, (jnp.flip(shifted_keep, 0), jnp.flip(state_...  279 us
  transfers between devices with their start and end apart: 12, of which 5 were waited for; matrix products, arithmetic and copies ran while one was open for 31% of the time, Pallas kernels for 0%

commit v1 on v0

v1 whole, which is shorter than its diff:
```python
import functools

import jax
import jax.numpy as jnp
from jax import lax
from jax.experimental import pallas as pl
from jax.experimental.pallas import tpu as pltpu
from jax.sharding import PartitionSpec as P

epsilon = 1e-06
f32 = jnp.float32
bf16 = jnp.bfloat16
TILE = 8
VMEM_LIMIT = 50 * 1024 * 1024


def product(left, right):
    return jnp.dot(left, right, preferred_element_type=f32)


def product_left_t(left, right):
    return lax.dot_general(left, right, (((0,), (0,)), ((), ())), preferred_element_type=f32)


def product_right_t(left, right):
    return lax.dot_general(left, right, (((1,), (1,)), ((), ())), preferred_element_type=f32)


def gelu_tanh(values):
    return jax.nn.gelu(values, approximate=True)


def dense_act(gate_values, up_values):
    return gelu_tanh(gate_values) * up_values


def swap(value, axis, bit):
    count = lax.axis_size(axis)
    return lax.ppermute(value, axis, [(i, i ^ bit) for i in range(count)])


def gather_rel(rows):
    count = lax.axis_size("tp")
    return jnp.stack([rows] + [swap(rows, "tp", r) for r in range(1, count)], axis=0)


def scatter_rel(blocks):
    count = lax.axis_size("tp")
    total = blocks[0].astype(f32)
    for r in range(1, count):
        total = total + swap(blocks[r], "tp", r).astype(f32)
    return total


def carry_in(keep_total, value_total, backward):
    place = lax.axis_index("seq")
    total = jnp.stack([keep_total, value_total])
    before = jnp.stack([jnp.ones_like(keep_total), jnp.zeros_like(value_total)])
    bit = 1
    while bit < lax.axis_size("seq"):
        other = swap(total, "seq", bit)
        upper = (place & bit) != 0
        earlier = jnp.logical_not(upper) if backward else upper
        joined_before = jnp.stack([other[0] * before[0], before[0] * other[1] + before[1]])
        before = jnp.where(earlier, joined_before, before)
        first = jnp.where(earlier, other, total)
        second = jnp.where(earlier, total, other)
        total = jnp.stack([first[0] * second[0], second[0] * first[1] + second[1]])
        bit *= 2
    return before[1]


def sum_bits(value, axis):
    bit = 1
    while bit < lax.axis_size(axis):
        value = value + swap(value, axis, bit)
        bit *= 2
    return value


def line_pairs(kind):
    pairs = []
    for i in range(lax.axis_size("seq")):
        chip, core = i // 2, i % 2
        base, z = chip // 4 * 4, chip % 4
        to = {"in": {0: 1, 3: 2}, "mid": {1: 2, 2: 1}, "out": {1: 0, 2: 3}}[kind].get(z)
        if to is not None:
            pairs.append((i, (base + to) * 2 + core))
    return pairs


def line_sum(part):
    z = lax.axis_index("seq") // 2 % 4
    at_end = jnp.logical_or(z == 0, z == 3)
    half = part + lax.ppermute(part, "seq", line_pairs("in"))
    total = half + lax.ppermute(half, "seq", line_pairs("mid"))
    bit = 8
    while bit < lax.axis_size("seq"):
        total = total + swap(total, "seq", bit)
        bit *= 2
    return jnp.where(at_end, lax.ppermute(total, "seq", line_pairs("out")), total)


def both_halves(mine, theirs, core):
    first = jnp.where(core == 0, mine, theirs)
    second = jnp.where(core == 0, theirs, mine)
    return first, second


def summed_grad(left, right, core):
    width = left.shape[1] // 2
    theirs = lax.dynamic_slice_in_dim(left, (1 - core) * width, width, 1)
    ours = lax.dynamic_slice_in_dim(left, core * width, width, 1)
    away = product_left_t(theirs, right).astype(bf16)
    back = swap(away, "seq", 1)
    part = (product_left_t(ours, right) + back.astype(f32)).astype(bf16)
    total = line_sum(part)
    other = swap(total, "seq", 1)
    first, second = both_halves(total, other, core)
    return jnp.concatenate([first, second], axis=0).astype(f32)


def minus_expm1(x):
    series = 1.0 / 40320.0
    for term in (1.0 / 5040.0, 1.0 / 720.0, 1.0 / 120.0, 1.0 / 24.0, 1.0 / 6.0, 0.5, 1.0):
        series = series * x + term
    return jnp.where(x > -0.35, -x * series, 1.0 - jnp.exp(x))


def rows_of(shape):
    return lax.broadcasted_iota(jnp.int32, shape, 0)


def down(cur, prev, by, row):
    return jnp.where(row >= by, pltpu.roll(cur, by, 0), pltpu.roll(prev, by, 0))


def up(cur, after, by, row):
    return jnp.where(row < TILE - by, pltpu.roll(cur, TILE - by, 0), pltpu.roll(after, TILE - by, 0))


def last_row(tile):
    return jnp.broadcast_to(tile[TILE - 1 :, :], tile.shape)


def first_row(tile):
    return jnp.broadcast_to(tile[:1, :], tile.shape)


def forward_kernel(
    place_ref,
    inner_ref,
    mask_ref,
    rim_ref,
    taps_ref,
    vec_ref,
    rate_ref,
    input_ref,
    conv_ref,
    low_ref,
    sig_rate_ref,
    sig_input_ref,
    keep_ref,
    value_ref,
    end_ref,
    prev_ref,
    carry_ref,
    rate_raw_ref,
    input_raw_ref,
):
    step = pl.program_id(0)
    length, width = inner_ref.shape[1:]
    tiles = length // TILE
    taps_n = taps_ref.shape[0]

    @pl.when(step == 0)
    def _():
        prev_ref[...] = rim_ref[...]
        carry_ref[0] = jnp.ones((TILE, width), f32)
        carry_ref[1] = jnp.zeros((TILE, width), f32)

    row = rows_of((TILE, width))

    def conv_tile(i, prev):
        at = pl.ds(pl.multiple_of(i * TILE, TILE), TILE)
        cur = inner_ref[0, at, :]
        masks = mask_ref[at, :]
        total = vec_ref[0:1, :] + taps_ref[0:1, :] * cur
        for k in range(1, taps_n):
            total = total + taps_ref[k : k + 1, :] * (down(cur, prev, k, row) * masks[:, k : k + 1])
        conv_ref[0, at, :] = total
        return cur

    prev_ref[...] = lax.fori_loop(0, tiles, conv_tile, prev_ref[...])
    low = conv_ref[0].astype(bf16)
    low_ref[0] = low
    rate_raw_ref[...] = jnp.dot(low, rate_ref[...], preferred_element_type=f32)
    input_raw_ref[...] = jnp.dot(low, input_ref[...], preferred_element_type=f32)

    def gate_tile(i, carry):
        keep_in, value_in = carry
        at = pl.ds(pl.multiple_of(i * TILE, TILE), TILE)
        sig_rate = jax.nn.sigmoid(rate_raw_ref[at, :] + vec_ref[1:2, :])
        sig_input = jax.nn.sigmoid(input_raw_ref[at, :] + vec_ref[2:3, :])
        sig_rate_ref[0, at, :] = sig_rate
        sig_input_ref[0, at, :] = sig_input
        log_decay = sig_rate * vec_ref[3:4, :]
        a = jnp.exp(log_decay) * mask_ref[at, 0:1]
        b = jnp.sqrt(minus_expm1(2.0 * log_decay)) * sig_input * conv_ref[0, at, :]
        for d in (1, 2, 4):
            a_before = jnp.where(row >= d, pltpu.roll(a, d, 0), 1.0)
            b_before = jnp.where(row >= d, pltpu.roll(b, d, 0), 0.0)
            b = b + a * b_before
            a = a * a_before
        b = b + a * value_in
        a = a * keep_in
        keep_ref[0, at, :] = a
        value_ref[0, at, :] = b
        return last_row(a), last_row(b)

    keep_end, value_end = lax.fori_loop(0, tiles, gate_tile, (carry_ref[0], carry_ref[1]))
    carry_ref[0] = keep_end
    carry_ref[1] = value_end
    end_ref[0] = keep_end
    end_ref[1] = value_end


def backward_kernel(
    place_ref,
    direct_ref,
    state_ref,
    state_prev_ref,
    conv_ref,
    sig_rate_ref,
    sig_input_ref,
    inner_ref,
    inner_prev_ref,
    mask_ref,
    rim_ref,
    state_in_ref,
    after_ref,
    taps_ref,
    vec_ref,
    rate_ref,
    input_ref,
    rate_grad_ref,
    input_grad_ref,
    inner_grad_ref,
    tail_ref,
    rim_grad_ref,
    sums_ref,
    carry_ref,
    next_ref,
    acc_ref,
    rate_f_ref,
    input_f_ref,
    conv_f_ref,
):
    step = pl.program_id(0)
    steps = pl.num_programs(0)
    length, width = direct_ref.shape[1:]
    tiles = length // TILE
    taps_n = taps_ref.shape[0]
    row = rows_of((TILE, width))
    is_first_block = step == steps - 1

    @pl.when(step == 0)
    def _():
        carry_ref[...] = after_ref[...]
        next_ref[...] = jnp.zeros_like(next_ref)
        acc_ref[...] = jnp.zeros_like(acc_ref)

    edge_state = jnp.where(is_first_block, state_in_ref[...], state_prev_ref[0])
    edge_inner = jnp.where(is_first_block, rim_ref[...], inner_prev_ref[0])
    neg_rate = vec_ref[3:4, :]

    def gate_tile(n, carry):
        after, acc_rate, acc_input, acc_decay = carry
        i = tiles - 1 - n
        at = pl.ds(pl.multiple_of(i * TILE, TILE), TILE)
        before = pl.ds(pl.multiple_of(jnp.maximum(i - 1, 0) * TILE, TILE), TILE)
        direct = direct_ref[0, at, :]
        sig_rate = sig_rate_ref[0, at, :]
        sig_input = sig_input_ref[0, at, :]
        conv = conv_ref[0, at, :]
        log_decay = sig_rate * neg_rate
        decay = jnp.exp(log_decay)
        keep = decay * mask_ref[at, 0:1]
        room = minus_expm1(2.0 * log_decay)
        root = jnp.sqrt(room)
        a = keep
        b = keep * direct
        for d in (1, 2, 4):
            a_after = jnp.where(row < TILE - d, pltpu.roll(a, TILE - d, 0), 1.0)
            b_after = jnp.where(row < TILE - d, pltpu.roll(b, TILE - d, 0), 0.0)
            b = b + a * b_after
            a = a * a_after
        reach = b + a * after
        grad = direct + up(reach, after, 1, row)
        prev_tile = jnp.where(i == 0, edge_state, state_ref[0, before, :])
        state_prev = down(state_ref[0, at, :], prev_tile, 1, row)
        grad_root = grad * root
        gated = grad_root * sig_input
        decay_grad = grad * (keep * state_prev - sig_input * conv * (decay * decay) / root)
        rate_grad = decay_grad * neg_rate * (sig_rate * (1.0 - sig_rate))
        input_grad = gated * conv * (1.0 - sig_input)
        rate_f_ref[at, :] = rate_grad
        input_f_ref[at, :] = input_grad
        conv_f_ref[at, :] = gated
        return (
            first_row(reach),
            acc_rate + rate_grad,
            acc_input + input_grad,
            acc_decay + decay_grad * sig_rate,
        )

    after, acc_rate, acc_input, acc_decay = lax.fori_loop(
        0, tiles, gate_tile, (carry_ref[...], acc_ref[0], acc_ref[1], acc_ref[2])
    )
    carry_ref[...] = after
    acc_ref[0] = acc_rate
    acc_ref[1] = acc_input
    acc_ref[2] = acc_decay
    rate_low = rate_f_ref[...].astype(bf16)
    input_low = input_f_ref[...].astype(bf16)
    rate_grad_ref[0] = rate_low
    input_grad_ref[0] = input_low
    right_t = (((1,), (1,)), ((), ()))
    conv_f_ref[...] += lax.dot_general(
        rate_low, rate_ref[...], right_t, preferred_element_type=f32
    ) + lax.dot_general(input_low, input_ref[...], right_t, preferred_element_type=f32)

    def conv_tile(n, carry):
        acc_bias, acc_taps, nexts = carry
        i = tiles - 1 - n
        at = pl.ds(pl.multiple_of(i * TILE, TILE), TILE)
        before = pl.ds(pl.multiple_of(jnp.maximum(i - 1, 0) * TILE, TILE), TILE)
        grad = conv_f_ref[at, :]
        masks = mask_ref[at, :]
        cur = inner_ref[0, at, :]
        prev = jnp.where(i == 0, edge_inner, inner_ref[0, before, :])
        total = grad * taps_ref[0:1, :]
        new_taps = [acc_taps[0] + grad * cur]
        new_nexts = []
        for k in range(1, taps_n):
            masked = grad * masks[:, k : k + 1]
            part = masked * taps_ref[k : k + 1, :]
            total = total + up(part, nexts[k - 1], k, row)
            new_taps.append(acc_taps[k] + masked * down(cur, prev, k, row))
            new_nexts.append(part)
        rate_f_ref[at, :] = total
        return acc_bias + grad, tuple(new_taps), tuple(new_nexts)

    acc_bias, acc_taps, nexts = lax.fori_loop(
        0,
        tiles,
        conv_tile,
        (
            acc_ref[3],
            tuple(acc_ref[4 + k] for k in range(taps_n)),
            tuple(next_ref[k] for k in range(taps_n - 1)),
        ),
    )
    acc_ref[3] = acc_bias
    for k in range(taps_n):
        acc_ref[4 + k] = acc_taps[k]
    for k in range(taps_n - 1):
        next_ref[k] = nexts[k]
    inner_grad_ref[0] = rate_f_ref[...].astype(bf16)

    @pl.when(step == 0)
    def _():
        tail_ref[...] = rate_f_ref[length - TILE :, :]

    @pl.when(is_first_block)
    def _():
        zero = jnp.zeros((TILE, width), f32)
        total = zero
        for k in range(1, taps_n):
            total = total + up(zero, nexts[k - 1], k, row)
        rim_grad_ref[...] = total
        sums_ref[...] = jnp.sum(acc_ref[...], axis=1)


def recur_forward(place, inner, masks, rim, taps, vecs, rate_dense, input_dense):
    blocks, length, width = inner.shape
    whole = lambda *shape: pl.BlockSpec(shape, lambda j, p: (0,) * len(shape))
    block = pl.BlockSpec((1, length, width), lambda j, p: (j ^ p[0], 0, 0))
    full = jax.ShapeDtypeStruct((blocks, length, width), f32)
    return pl.pallas_call(
        forward_kernel,
        grid_spec=pltpu.PrefetchScalarGridSpec(
            num_scalar_prefetch=1,
            grid=(blocks,),
            in_specs=[
                block,
                pl.BlockSpec((length, masks.shape[1]), lambda j, p: (j, 0)),
                whole(*rim.shape),
                whole(*taps.shape),
                whole(*vecs.shape),
                whole(*rate_dense.shape),
                whole(*input_dense.shape),
            ],
            out_specs=[block, block, block, block, block, block, whole(2, TILE, width)],
            scratch_shapes=[
                pltpu.VMEM((TILE, width), f32),
                pltpu.VMEM((2, TILE, width), f32),
                pltpu.VMEM((length, width), f32),
                pltpu.VMEM((length, width), f32),
            ],
        ),
        out_shape=[
            full,
            jax.ShapeDtypeStruct((blocks, length, width), bf16),
            full,
            full,
            full,
            full,
            jax.ShapeDtypeStruct((2, TILE, width), f32),
        ],
        compiler_params=pltpu.CompilerParams(vmem_limit_bytes=VMEM_LIMIT),
        name="recur_forward",
    )(place, inner, masks, rim, taps, vecs, rate_dense, input_dense)


def recur_backward(
    place, direct, state, conv, sig_rate, sig_input, inner, masks, rim, state_in, after, taps, vecs, rate_dense, input_dense
):
    blocks, length, width = inner.shape
    last = length // TILE - 1
    whole = lambda *shape: pl.BlockSpec(shape, lambda j, p: (0,) * len(shape))
    block = pl.BlockSpec((1, length, width), lambda j, p: ((blocks - 1 - j) ^ p[0], 0, 0))
    edge = pl.BlockSpec(
        (1, TILE, width), lambda j, p: (jnp.maximum(blocks - 2 - j, 0) ^ p[0], last, 0)
    )
    low = jax.ShapeDtypeStruct((blocks, length, width), bf16)
    tile = jax.ShapeDtypeStruct((TILE, width), f32)
    count = 4 + taps.shape[0]
    return pl.pallas_call(
        backward_kernel,
        grid_spec=pltpu.PrefetchScalarGridSpec(
            num_scalar_prefetch=1,
            grid=(blocks,),
            in_specs=[
                block,
                block,
                edge,
                block,
                block,
                block,
                block,
                edge,
                pl.BlockSpec((length, masks.shape[1]), lambda j, p: (blocks - 1 - j, 0)),
                whole(*rim.shape),
                whole(*state_in.shape),
                whole(*after.shape),
                whole(*taps.shape),
                whole(*vecs.shape),
                whole(*rate_dense.shape),
                whole(*input_dense.shape),
            ],
            out_specs=[
                block,
                block,
                block,
                whole(TILE, width),
                whole(TILE, width),
                whole(count, width),
            ],
            scratch_shapes=[
                pltpu.VMEM((TILE, width), f32),
                pltpu.VMEM((taps.shape[0] - 1, TILE, width), f32),
                pltpu.VMEM((count, TILE, width), f32),
                pltpu.VMEM((length, width), f32),
                pltpu.VMEM((length, width), f32),
                pltpu.VMEM((length, width), f32),
            ],
        ),
        out_shape=[low, low, low, tile, tile, jax.ShapeDtypeStruct((count, width), f32)],
        compiler_params=pltpu.CompilerParams(vmem_limit_bytes=VMEM_LIMIT),
        name="recur_backward",
    )(
        place,
        direct,
        state,
        state,
        conv,
        sig_rate,
        sig_input,
        inner,
        inner,
        masks,
        rim,
        state_in,
        after,
        taps,
        vecs,
        rate_dense,
        input_dense,
    )


def dense_blocks(blocks):
    count, rows_in, cols_out = blocks.shape
    tall = blocks.reshape(count * rows_in, cols_out)
    wide = jnp.concatenate([tall] * count, axis=1)
    row = lax.broadcasted_iota(jnp.int32, wide.shape, 0) // rows_in
    col = lax.broadcasted_iota(jnp.int32, wide.shape, 1) // cols_out
    return jnp.where(row == col, wide, jnp.zeros_like(wide))


def diagonal_blocks(full, count):
    rows, cols = full.shape[0] // count, full.shape[1] // count
    return jnp.stack([full[i * rows : (i + 1) * rows, i * cols : (i + 1) * cols] for i in range(count)])


def rms(values):
    return lax.rsqrt(jnp.mean(values * values, axis=-1, keepdims=True) + epsilon)


def norm_back(grad, xhat, scale, root):
    e = grad * scale
    return root * (e - xhat * jnp.mean(e * xhat, axis=-1, keepdims=True)), jnp.sum(grad * xhat, axis=0)


def shards(
    tokens,
    mixer_gain,
    in_proj,
    branch_proj,
    conv_taps,
    conv_bias,
    rate_blocks,
    rate_bias,
    input_blocks,
    input_bias,
    decay_param,
    out_proj,
    dense_gain,
    gate_proj,
    up_proj,
    down_proj,
    segment_ids,
    cotangent,
):
    tp_place = lax.axis_index("tp")
    seq_place = lax.axis_index("seq")
    core = seq_place % 2
    tp_size = lax.axis_size("tp")
    seq_size = lax.axis_size("seq")
    place = tp_place.astype(jnp.int32)[None]
    gain_share = mixer_gain.shape[0]
    taps_n, width = conv_taps.shape
    rim_width = taps_n - 1
    length, model = tokens.shape
    group = length * tp_size
    blocks_n = rate_blocks.shape[0]
    hidden_n = gate_proj.shape[1]
    onward = [(i, i + 1) for i in range(seq_size - 1)]
    backward_pairs = [(i + 1, i) for i in range(seq_size - 1)]

    rows_rel = gather_rel(tokens)
    gains = gather_rel(jnp.stack([mixer_gain, dense_gain]))
    order = tp_place ^ jnp.arange(tp_size)
    gains = jnp.take(gains, order, axis=0).transpose(1, 0, 2).reshape(2, -1).astype(f32)
    mixer_scale, dense_scale = gains[0], gains[1]
    rim_ids = lax.ppermute(segment_ids[-rim_width:], "seq", onward)
    ext_ids = jnp.concatenate([rim_ids, segment_ids])
    same = [ext_ids[rim_width - k : rim_width - k + group] == segment_ids for k in range(1, taps_n)]
    masks = jnp.stack([same[0]] + same, axis=1).astype(f32)

    rate_dense = dense_blocks(rate_blocks)
    input_dense = dense_blocks(input_blocks)
    decay_rate = jax.nn.softplus(-decay_param)
    vecs = jnp.stack([conv_bias, rate_bias, input_bias, -8.0 * decay_rate])

    rows_f = rows_rel.reshape(group, model).astype(f32)
    normed = (rows_f * rms(rows_f) * mixer_scale).astype(bf16)
    inner = product(normed, in_proj).reshape(tp_size, length, width)
    last_block = lax.dynamic_index_in_dim(inner, (tp_size - 1) ^ tp_place, 0, False)
    rim = lax.ppermute(last_block[-TILE:], "seq", onward)
    branch_pre = product(normed, branch_proj)
    conv, conv_low, sig_rate, sig_input, keep_prefix, value_prefix, ends = recur_forward(
        place, inner, masks, rim, conv_taps, vecs, rate_dense, input_dense
    )
    state_in = carry_in(ends[0, 0], ends[1, 0], False)
    state = value_prefix + keep_prefix * state_in
    branch = gelu_tanh(branch_pre).reshape(state.shape)
    mixed = (state * branch).astype(bf16).reshape(group, width)
    mixer_out = scatter_rel(product(mixed, out_proj).astype(bf16).reshape(tp_size, length, model))
    mid = tokens.astype(f32) + mixer_out
    mid_root = rms(mid)
    xhat_dense = mid * mid_root
    normed_two = (xhat_dense * dense_scale).astype(bf16)

    rows_two = gather_rel(normed_two).reshape(group, model)
    cot_rows = gather_rel(cotangent).reshape(group, model)
    gate_pre = product(rows_two, gate_proj)
    up_pre = product(rows_two, up_proj)
    hidden_float, act_pull = jax.vjp(dense_act, gate_pre, up_pre)
    hidden = hidden_float.astype(bf16)
    hidden_grad = product_right_t(cot_rows, down_proj)
    gate_float, up_float = act_pull(hidden_grad)
    gate_grad = gate_float.astype(bf16)
    up_grad = up_float.astype(bf16)
    down_sum = summed_grad(hidden, cot_rows, core)
    gate_sum = summed_grad(rows_two, gate_grad, core)
    up_sum = summed_grad(rows_two, up_grad, core)
    normed_two_part = product_right_t(gate_grad, gate_proj) + product_right_t(up_grad, up_proj)
    normed_two_grad = scatter_rel(normed_two_part.astype(bf16).reshape(tp_size, length, model))
    dense_out = scatter_rel(product(hidden, down_proj).astype(bf16).reshape(tp_size, length, model))
    output = (mid + dense_out).astype(bf16)
    mid_from_norm, dense_gain_part = norm_back(normed_two_grad, xhat_dense, dense_scale, mid_root)
    mid_grad = cotangent.astype(f32) + mid_from_norm

    mid_rows = gather_rel(mid_grad.astype(bf16)).reshape(group, model)
    mixed_grad = product_right_t(mid_rows, out_proj).reshape(state.shape)
    work_branch, branch_pull = jax.vjp(gelu_tanh, branch_pre.reshape(state.shape))
    direct = mixed_grad * work_branch
    reach = jnp.sum(direct * keep_prefix, axis=(0, 1))
    out_sum = summed_grad(mixed, mid_rows, core)
    branch_pre_grad = branch_pull(mixed_grad * state)[0].astype(bf16).reshape(group, width)
    branch_sum = summed_grad(normed, branch_pre_grad, core)
    after = carry_in(ends[0, 0], reach, True)
    tile = lambda v: jnp.broadcast_to(v, (TILE, width))
    rate_low, input_low, inner_grad, tail, rim_grad, sums = recur_backward(
        place,
        direct,
        state,
        conv,
        sig_rate,
        sig_input,
        inner,
        masks,
        rim,
        tile(state_in),
        tile(after),
        conv_taps,
        vecs,
        rate_dense,
        input_dense,
    )
    fixed = tail + lax.ppermute(rim_grad, "seq", backward_pairs)
    inner_grad = lax.dynamic_update_slice(
        inner_grad, fixed.astype(bf16)[None], ((tp_size - 1) ^ tp_place, length - TILE, 0)
    ).reshape(group, width)
    in_sum = summed_grad(normed, inner_grad, core)
    low_rows = conv_low.reshape(group, width)
    rate_w = diagonal_blocks(product_left_t(low_rows, rate_low.reshape(group, width)), blocks_n)
    input_w = diagonal_blocks(product_left_t(low_rows, input_low.reshape(group, width)), blocks_n)
    rate_w, input_w = rate_w.astype(bf16), input_w.astype(bf16)
    ours, theirs = both_halves(rate_w, input_w, core)
    block_total = line_sum((ours.astype(f32) + swap(theirs, "seq", 1).astype(f32)).astype(bf16))
    rate_sum, input_sum = both_halves(block_total, swap(block_total, "seq", 1), core)
    normed_part = product_right_t(inner_grad, in_proj) + product_right_t(branch_pre_grad, branch_proj)
    normed_grad = scatter_rel(normed_part.astype(bf16).reshape(tp_size, length, model))
    own = tokens.astype(f32)
    own_root = rms(own)
    rows_grad, mixer_gain_part = norm_back(normed_grad, own * own_root, mixer_scale, own_root)
    tokens_grad = mid_grad + rows_grad

    gain_parts = sum_bits(jnp.stack([mixer_gain_part, dense_gain_part]), "tp")
    gain_own = lax.dynamic_slice_in_dim(gain_parts, tp_place * gain_share, gain_share, 1)
    gain_sum = sum_bits(gain_own, "seq")
    sums = sum_bits(sums, "seq")
    decay_sum = 8.0 * jax.nn.sigmoid(-decay_param) * sums[2]
    return (
        output,
        tokens_grad,
        gain_sum[0],
        in_sum,
        branch_sum,
        sums[4 : 4 + taps_n],
        sums[3],
        rate_sum.astype(f32),
        sums[0],
        input_sum.astype(f32),
        sums[1],
        decay_sum,
        out_sum,
        gain_sum[1],
        gate_sum,
        up_sum,
        down_sum,
    )


def solution(mesh):
    return jax.shard_map(
        shards,
        mesh=mesh,
        in_specs=(
            P(("seq", "tp"), None),
            P("tp"),
            P(None, "tp"),
            P(None, "tp"),
            P(None, "tp"),
            P("tp"),
            P("tp", None, None),
            P("tp"),
            P("tp", None, None),
            P("tp"),
            P("tp"),
            P("tp", None),
            P("tp"),
            P(None, "tp"),
            P(None, "tp"),
            P("tp", None),
            P("seq"),
            P(("seq", "tp"), None),
        ),
        out_specs=(
            P(("seq", "tp"), None),
            P(("seq", "tp"), None),
            P("tp"),
            P(None, "tp"),
            P(None, "tp"),
            P(None, "tp"),
            P("tp"),
            P("tp", None, None),
            P("tp"),
            P("tp", None, None),
            P("tp"),
            P("tp"),
            P("tp", None),
            P("tp"),
            P(None, "tp"),
            P(None, "tp"),
            P("tp", None),
        ),
        check_vma=False,
    )
```

time: 3610 us -> 1060 us (0.29)
  local copies, waits for them, and re-layouts: 2340 us -> 18.5 us
  other arithmetic: 322 us -> 116 us
  blocking collectives: 140 us -> 0 us
  starting transfers between devices: 6.81 us -> 108 us
  waiting for transfers between devices: 590 us -> 668 us
  matrix products: 166 us -> 103 us
    slice x162 -> x10, local copies, waits for them, and re-layouts: 1350 us -> 4.11 us  [the longest x4 1.51 us: scatter_rel(): total = total + swap(blocks[r], 'tp', r).astype(f32)]
    pad x96 -> x0, local copies, waits for them, and re-layouts: 835 us -> none  [the longest x64 556 us: recur_local(): lax.associative_scan(combine, (keep, drive), axis=0)]
    ppermute x3 -> x79, waiting for transfers between devices: 0.01 us -> 668 us  [the longest x7 275 us: line_sum(): lax.ppermute(total, 'seq', line_pairs('out'))]
    psum x1 -> x0, waiting for transfers between devices: 516 us -> none  [shards(): lax.psum(in_w_grad.astype(jnp.bfloat16), 'seq').astype(jnp.float32)]
    add x112 -> x22, other arithmetic: 164 us -> 34.7 us  [the longest x7 17.8 us: line_sum(): half = part + lax.ppermute(part, 'seq', line_pairs('in'))]
    ppermute x3 -> x79, starting transfers between devices: 5.87 us -> 108 us  [the longest x55 58.4 us: swap(): return lax.ppermute(value, axis, [(i, i ^ bit) for i in range(count)])]
    all_gather x6 -> x0, blocking collectives: 72.7 us -> none  [the longest x4 55.8 us: prefix(): gathered = jax.tree.map(lambda a: lax.all_gather(a, axis), part)]
    psum x2 -> x0, blocking collectives: 67.4 us -> none  [the longest x1 37.9 us: shards(): lax.psum((mixer_gain_part, dense_gain_part), ('seq', 'tp'))]
  transfers between devices with their start and end apart: 12 -> 79, of which waited for: 5 -> 36; matrix products, arithmetic and copies ran while one was open for 31% -> 16% of each run, Pallas kernels for 0% -> 2%
where the time goes in v1:
time: 1060 us; the launch traced here: 1050 us
  waiting for transfers between devices  668 us (63%)
  other arithmetic  116 us (11%)
  starting transfers between devices  108 us (10%)
  matrix products  103 us (10%)
  Pallas kernels  35.3 us (3%)
  local copies, waits for them, and re-layouts  18.5 us (2%)
    ppermute x7, waiting for transfers between devices, line_sum(): lax.ppermute(total, 'seq', line_pairs('out'))  275 us
    ppermute x55, waiting for transfers between devices, swap(): return lax.ppermute(value, axis, [(i, i ^ bit) for i in range(count)])  210 us
    ppermute x7, waiting for transfers between devices, line_sum(): half = part + lax.ppermute(part, 'seq', line_pairs('in'))  183 us
    ppermute x55, starting transfers between devices, swap(): return lax.ppermute(value, axis, [(i, i ^ bit) for i in range(count)])  58.4 us
    dot_general x14, matrix products, product_left_t(): lax.dot_general(left, right, (((0,), (0,)), ((), ())), preferred_element_...  39.8 us
    dot_general x6, matrix products, product_right_t(): lax.dot_general(left, right, (((1,), (1,)), ((), ())), preferred_element_...  33.7 us
    dot_general x6, matrix products, product(): return jnp.dot(left, right, preferred_element_type=f32)  30 us
    convert_element_type x6, other arithmetic, summed_grad(): return jnp.concatenate([first, second], axis=0).astype(f32)  29.4 us
  transfers between devices with their start and end apart: 79, of which 36 were waited for; matrix products, arithmetic and copies ran while one was open for 16% of the time, Pallas kernels for 2%

profile of v1, /device:TPU:0, one launch (start us, length us, event | category | flops | bytes accessed | tf_op | source)
XLA Modules:
  0.0 1051.3 jit_solution(6708864605200600247)
XLA Ops:
  22.2 13.2 %collective-permute-done.2 = bf16[128,2048]{1,0:T(8,128)(2,1)} collective-permute-done((bf16[128,2048]{1,0:T(8,128)(2,1)}, bf16[128,2048]{1,0:T(8,128)(2,1)}, u32[]{:S(2)}, u32[]{:S(2)}) %collective-permute-start.2) | collective-permute-done | bytes 524320 | tf_op jit(solution)/shard_map/ppermute | solution.py:39
  35.4 11.3 %collective-permute-done.1 = bf16[128,2048]{1,0:T(8,128)(2,1)} collective-permute-done((bf16[128,2048]{1,0:T(8,128)(2,1)}, bf16[128,2048]{1,0:T(8,128)(2,1)}, u32[]{:S(2)}, u32[]{:S(2)}) %collective-permute-start.1) | collective-permute-done | bytes 524320 | tf_op jit(solution)/shard_map/ppermute | solution.py:39
  57.3 15.8 %recur_forward.1 = (f32[4,128,704]{2,1,0:T(8,128)}, bf16[4,128,704]{2,1,0:T(8,128)(2,1)S(1)}, f32[4,128,704]{2,1,0:T(8,128)}, f32[4,128,704]{2,1,0:T(8,128)}, f3...) custom-call(s32[1]{0:T(128)} %bitcast.place_ref, f32[4,128,704]{2,1,0:T(8,128)} %copy-done.10, ...), custom_call_target="tpu_custom_call" | custom-call | tf_op jit(solution)/shard_map/recur_forward/pallas_call | solution.py:390
  103.0 9.6 collective-permute-done.11
  113.2 10.7 %collective-permute-done.13 = bf16[128,2048]{1,0:T(8,128)(2,1)} collective-permute-done((bf16[128,2048]{1,0:T(8,128)(2,1)}, bf16[128,2048]{1,0:T(8,128)(2,1)}, u32[]{:S(2)}, u32[]{:S(2)}) %collective-permute-start.13) | collective-permute-done | bytes 524320 | tf_op jit(solution)/shard_map/ppermute | solution.py:39
  136.5 9.9 collective-permute-done.22
  155.0 13.2 %collective-permute-done.15 = bf16[128,2048]{1,0:T(8,128)(2,1)} collective-permute-done((bf16[128,2048]{1,0:T(8,128)(2,1)}, bf16[128,2048]{1,0:T(8,128)(2,1)}, u32[]{:S(2)}, u32[]{:S(2)}) %collective-permute-start.15) | collective-permute-done | bytes 524320 | tf_op jit(solution)/shard_map/ppermute | solution.py:39
  169.9 8.6 fusion.95
  183.7 9.7 multiply_convert_fusion.1
  220.9 10.7 %collective-permute-done.25 = bf16[128,2048]{1,0:T(8,128)(2,1)S(1)} collective-permute-done((bf16[128,2048]{1,0:T(8,128)(2,1)S(1)}, bf16[128,2048]{1,0:T(8,128)(2,1)S(1)}, u32[]{:S(2)}, u32[]{:S(2)}) %collective-permute-start.25) | collective-permute-done | bytes 524320 | tf_op jit(solution)/shard_map/ppermute | solution.py:39
  231.6 9.8 collective-permute-done.24
  241.9 9.0 collective-permute-done.19
  303.6 19.5 %recur_backward.1 = (bf16[4,128,704]{2,1,0:T(8,128)(2,1)S(1)}, bf16[4,128,704]{2,1,0:T(8,128)(2,1)S(1)}, bf16[4,128,704]{2,1,0:T(8,128)(2,1)S(1)}, f32[8,704]{1,...) custom-call(s32[1]{0:T(128)} %bitcast.place_ref, f32[4,128,704]{2,1,0:T(8,128)} %get-tuple-element.52.direct_ref, ...), custom_call_target="tpu_custom_call" | custom-call | tf_op jit(solution)/shard_map/recur_backward/pallas_call | solution.py:439
  335.7 10.7 %collective-permute-done.33 = bf16[128,2048]{1,0:T(8,128)(2,1)S(1)} collective-permute-done((bf16[128,2048]{1,0:T(8,128)(2,1)S(1)}, bf16[128,2048]{1,0:T(8,128)(2,1)S(1)}, u32[]{:S(2)}, u32[]{:S(2)}) %collective-permute-start.33) | collective-permute-done | bytes 524320 | tf_op jit(solution)/shard_map/ppermute | solution.py:39
  346.8 11.0 %collective-permute-done.35 = bf16[128,2048]{1,0:T(8,128)(2,1)S(1)} collective-permute-done((bf16[128,2048]{1,0:T(8,128)(2,1)S(1)}, bf16[128,2048]{1,0:T(8,128)(2,1)S(1)}, u32[]{:S(2)}, u32[]{:S(2)}) %collective-permute-start.35) | collective-permute-done | bytes 524320 | tf_op jit(solution)/shard_map/ppermute | solution.py:39
  405.7 53.1 %collective-permute-done.53 = f32[8,704]{1,0:T(8,128)S(1)} collective-permute-done((f32[8,704]{1,0:T(8,128)S(1)}, f32[8,704]{1,0:T(8,128)S(1)}, u32[]{:S(2)}, u32[]{:S(2)}) %collective-permute-start.53) | collective-permute-done | bytes 22560 | tf_op jit(solution)/shard_map/ppermute | solution.py:39
  498.1 66.1 %collective-permute-done.60 = bf16[352,2048]{1,0:T(8,128)(2,1)S(1)} collective-permute-done((bf16[352,2048]{1,0:T(8,128)(2,1)S(1)}, bf16[352,2048]{1,0:T(8,128)(2,1)S(1)}, u32[]{:S(2)}, u32[]{:S(2)}) %collective-permute-start.60) | collective-permute-done | bytes 1441824 | tf_op jit(solution)/shard_map/ppermute | solution.py:95
  573.8 88.8 %collective-permute-done.47 = bf16[1024,704]{0,1:T(8,128)(2,1)S(1)} collective-permute-done((bf16[1024,704]{0,1:T(8,128)(2,1)S(1)}, bf16[1024,704]{0,1:T(8,128)(2,1)S(1)}, u32[]{:S(2)}, u32[]{:S(2)}) %collective-permute-start.47) | collective-permute-done | bytes 1441824 | tf_op jit(solution)/shard_map/ppermute | solution.py:95
  666.6 24.5 %collective-permute-done.42 = bf16[1024,704]{0,1:T(8,128)(2,1)S(1)} collective-permute-done((bf16[1024,704]{0,1:T(8,128)(2,1)S(1)}, bf16[1024,704]{0,1:T(8,128)(2,1)S(1)}, u32[]{:S(2)}, u32[]{:S(2)}) %collective-permute-start.42) | collective-permute-done | bytes 1441824 | tf_op jit(solution)/shard_map/ppermute | solution.py:95
  719.6 14.1 %collective-permute-done.62 = bf16[352,2048]{1,0:T(8,128)(2,1)} collective-permute-done((bf16[352,2048]{1,0:T(8,128)(2,1)}, bf16[352,2048]{1,0:T(8,128)(2,1)}, u32[]{:S(2)}, u32[]{:S(2)}) %collective-permute-start.62) | collective-permute-done | bytes 1441824 | tf_op jit(solution)/shard_map/ppermute | solution.py:101
  742.8 127.4 %collective-permute-done.49 = bf16[1024,704]{0,1:T(8,128)(2,1)S(1)} collective-permute-done((bf16[1024,704]{0,1:T(8,128)(2,1)S(1)}, bf16[1024,704]{0,1:T(8,128)(2,1)S(1)}, u32[]{:S(2)}, u32[]{:S(2)}) %collective-permute-start.49) | collective-permute-done | bytes 1441824 | tf_op jit(solution)/shard_map/ppermute | solution.py:101
  872.8 28.3 %collective-permute-done.44 = bf16[1024,704]{0,1:T(8,128)(2,1)S(1)} collective-permute-done((bf16[1024,704]{0,1:T(8,128)(2,1)S(1)}, bf16[1024,704]{0,1:T(8,128)(2,1)S(1)}, u32[]{:S(2)}, u32[]{:S(2)}) %collective-permute-start.44) | collective-permute-done | bytes 1441824 | tf_op jit(solution)/shard_map/ppermute | solution.py:101
  914.4 54.2 %collective-permute-done.72 = bf16[1024,1536]{1,0:T(8,128)(2,1)} collective-permute-done((bf16[1024,1536]{1,0:T(8,128)(2,1)S(1)}, bf16[1024,1536]{1,0:T(8,128)(2,1)}, u32[]{:S(2)}, u32[]{:S(2)}) %collective-permute-start.72) | collective-permute-done | bytes 3145760 | tf_op jit(solution)/shard_map/ppermute | solution.py:101
  974.5 49.6 %collective-permute-done.67 = bf16[1024,1536]{1,0:T(8,128)(2,1)S(1)} collective-permute-done((bf16[1024,1536]{1,0:T(8,128)(2,1)S(1)}, bf16[1024,1536]{1,0:T(8,128)(2,1)S(1)}, u32[]{:S(2)}, u32[]{:S(2)}) %collective-permute-start.67) | collective-permute-done | bytes 3145760 | tf_op jit(solution)/shard_map/ppermute | solution.py:101
  (422 shorter events, 370.1 us)
Async XLA Ops:
  293.1 103.4 %collective-permute-start.69 = (bf16[1024,1536]{1,0:T(8,128)(2,1)}, bf16[1024,1536]{1,0:T(8,128)(2,1)}, u32[]{:S(2)}, u32[]{:S(2)}) collective-permute-start(bf16[1024,1536]{1,0:T(8,128)(2,1)} %convolution_convert_fusion), channel_id=1, source_target_pairs={{0,4},{4,0},{8,12},{12,8},{16,20},{20,16},{24,28},{28,24},{1,5},{5... | collective-permute-start | bytes 9437192 | tf_op jit(solution)/shard_map/ppermute | solution.py:39
  293.6 84.9 %collective-permute-start.74 = (bf16[768,2048]{1,0:T(8,128)(2,1)}, bf16[768,2048]{1,0:T(8,128)(2,1)}, u32[]{:S(2)}, u32[]{:S(2)}) collective-permute-start(bf16[768,2048]{1,0:T(8,128)(2,1)} %convolution_convert_fusion.2), channel_id=1, source_target_pairs={{0,4},{4,0},{8,12},{12,8},{16,20},{20,16},{24,28},{28,24},{1,5},{5... | collective-permute-start | bytes 9437192 | tf_op jit(solution)/shard_map/ppermute | solution.py:39
  346.3 130.0 %collective-permute-start.64 = (bf16[1024,1536]{1,0:T(8,128)(2,1)}, bf16[1024,1536]{1,0:T(8,128)(2,1)}, u32[]{:S(2)}, u32[]{:S(2)}) collective-permute-start(bf16[1024,1536]{1,0:T(8,128)(2,1)} %convolution_convert_fusion.1), channel_id=1, source_target_pairs={{0,4},{4,0},{8,12},{12,8},{16,20},{20,16},{24,28},{28,24},{1,5},{5... | collective-permute-start | bytes 9437192 | tf_op jit(solution)/shard_map/ppermute | solution.py:39
  388.6 98.7 %collective-permute-start.75 = (bf16[768,2048]{1,0:T(8,128)(2,1)}, bf16[768,2048]{1,0:T(8,128)(2,1)}, u32[]{:S(2)}, u32[]{:S(2)}) collective-permute-start(bf16[768,2048]{1,0:T(8,128)(2,1)} %add_convert_fusion), channel_id=1, source_target_pairs={{0,8},{4,12},{24,16},{28,20},{1,9},{5,13},{25,17},{29,21},{2,10},{... | collective-permute-start | bytes 9437192 | tf_op jit(solution)/shard_map/ppermute | solution.py:95
  394.4 78.6 %collective-permute-start.59 = (bf16[352,2048]{1,0:T(8,128)(2,1)}, bf16[352,2048]{1,0:T(8,128)(2,1)}, u32[]{:S(2)}, u32[]{:S(2)}) collective-permute-start(bf16[352,2048]{1,0:T(8,128)(2,1)} %convolution_convert_fusion.5), channel_id=1, source_target_pairs={{0,4},{4,0},{8,12},{12,8},{16,20},{20,16},{24,28},{28,24},{1,5},{5... | collective-permute-start | bytes 4325384 | tf_op jit(solution)/shard_map/ppermute | solution.py:39
  395.2 63.5 %collective-permute-start.53 = (f32[8,704]{1,0:T(8,128)S(1)}, f32[8,704]{1,0:T(8,128)S(1)}, u32[]{:S(2)}, u32[]{:S(2)}) collective-permute-start(f32[8,704]{1,0:T(8,128)S(1)} %add.363), channel_id=1, source_target_pairs={{0,16},{4,20},{8,24},{12,28},{16,0},{20,4},{24,8},{28,12},{1,17},{... | collective-permute-start | bytes 67592 | tf_op jit(solution)/shard_map/ppermute | solution.py:39
  396.5 63.5 %collective-permute-start.40 = (f32[2,512]{1,0:T(2,128)S(1)}, f32[2,512]{1,0:T(2,128)S(1)}, u32[]{:S(2)}, u32[]{:S(2)}) collective-permute-start(f32[2,512]{1,0:T(2,128)S(1)} %add.350), channel_id=1, source_target_pairs={{0,16},{4,20},{8,24},{12,28},{16,0},{20,4},{24,8},{28,12},{1,17},{... | collective-permute-start | bytes 12296 | tf_op jit(solution)/shard_map/ppermute | solution.py:39
  460.1 109.3 %collective-permute-start.70 = (bf16[1024,1536]{1,0:T(8,128)(2,1)}, bf16[1024,1536]{1,0:T(8,128)(2,1)}, u32[]{:S(2)}, u32[]{:S(2)}) collective-permute-start(bf16[1024,1536]{1,0:T(8,128)(2,1)} %add_convert_fusion.1), channel_id=1, source_target_pairs={{0,8},{4,12},{24,16},{28,20},{1,9},{5,13},{25,17},{29,21},{2,10},{... | collective-permute-start | bytes 9437192 | tf_op jit(solution)/shard_map/ppermute | solution.py:95
  476.3 88.0 %collective-permute-start.60 = (bf16[352,2048]{1,0:T(8,128)(2,1)S(1)}, bf16[352,2048]{1,0:T(8,128)(2,1)S(1)}, u32[]{:S(2)}, u32[]{:S(2)}) collective-permute-start(bf16[352,2048]{1,0:T(8,128)(2,1)S(1)} %fusion.13), channel_id=1, source_target_pairs={{0,8},{4,12},{24,16},{28,20},{1,9},{5,13},{25,17},{29,21},{2,10},{... | collective-permute-start | bytes 4325384 | tf_op jit(solution)/shard_map/ppermute | solution.py:95
  481.9 216.4 %collective-permute-start.65 = (bf16[1024,1536]{1,0:T(8,128)(2,1)S(1)}, bf16[1024,1536]{1,0:T(8,128)(2,1)}, u32[]{:S(2)}, u32[]{:S(2)}) collective-permute-start(bf16[1024,1536]{1,0:T(8,128)(2,1)S(1)} %add_convert_fusion.2), channel_id=1, source_target_pairs={{0,8},{4,12},{24,16},{28,20},{1,9},{5,13},{25,17},{29,21},{2,10},{... | collective-permute-start | bytes 9437192 | tf_op jit(solution)/shard_map/ppermute | solution.py:95
  487.3 175.3 %collective-permute-start.47 = (bf16[1024,704]{0,1:T(8,128)(2,1)S(1)}, bf16[1024,704]{0,1:T(8,128)(2,1)S(1)}, u32[]{:S(2)}, u32[]{:S(2)}) collective-permute-start(bf16[1024,704]{0,1:T(8,128)(2,1)S(1)} %add_convert_fusion.5), channel_id=1, source_target_pairs={{0,8},{4,12},{24,16},{28,20},{1,9},{5,13},{25,17},{29,21},{2,10},{... | collective-permute-start | bytes 4325384 | tf_op jit(solution)/shard_map/ppermute | solution.py:95
  494.8 205.9 %collective-permute-start.76 = (bf16[768,2048]{1,0:T(8,128)(2,1)}, bf16[768,2048]{1,0:T(8,128)(2,1)}, u32[]{:S(2)}, u32[]{:S(2)}) collective-permute-start(bf16[768,2048]{1,0:T(8,128)(2,1)} %add.383), channel_id=1, source_target_pairs={{8,16},{12,20},{16,8},{20,12},{9,17},{13,21},{17,9},{21,13},{10,18... | collective-permute-start | bytes 9437192 | tf_op jit(solution)/shard_map/ppermute | solution.py:96
  564.3 126.9 %collective-permute-start.42 = (bf16[1024,704]{0,1:T(8,128)(2,1)S(1)}, bf16[1024,704]{0,1:T(8,128)(2,1)S(1)}, u32[]{:S(2)}, u32[]{:S(2)}) collective-permute-start(bf16[1024,704]{0,1:T(8,128)(2,1)S(1)} %add_convert_fusion.6), channel_id=1, source_target_pairs={{0,8},{4,12},{24,16},{28,20},{1,9},{5,13},{25,17},{29,21},{2,10},{... | collective-permute-start | bytes 4325384 | tf_op jit(solution)/shard_map/ppermute | solution.py:95
  569.4 125.3 %collective-permute-start.61 = (bf16[352,2048]{1,0:T(8,128)(2,1)S(1)}, bf16[352,2048]{1,0:T(8,128)(2,1)S(1)}, u32[]{:S(2)}, u32[]{:S(2)}) collective-permute-start(bf16[352,2048]{1,0:T(8,128)(2,1)S(1)} %add.372), channel_id=1, source_target_pairs={{8,16},{12,20},{16,8},{20,12},{9,17},{13,21},{17,9},{21,13},{10,18... | collective-permute-start | bytes 4325384 | tf_op jit(solution)/shard_map/ppermute | solution.py:96
  662.6 73.9 %collective-permute-start.71 = (bf16[1024,1536]{1,0:T(8,128)(2,1)S(1)}, bf16[1024,1536]{1,0:T(8,128)(2,1)}, u32[]{:S(2)}, u32[]{:S(2)}) collective-permute-start(bf16[1024,1536]{1,0:T(8,128)(2,1)S(1)} %add.378), channel_id=1, source_target_pairs={{8,16},{12,20},{16,8},{20,12},{9,17},{13,21},{17,9},{21,13},{10,18... | collective-permute-start | bytes 9437192 | tf_op jit(solution)/shard_map/ppermute | solution.py:96
  710.0 193.4 %collective-permute-start.66 = (bf16[1024,1536]{1,0:T(8,128)(2,1)S(1)}, bf16[1024,1536]{1,0:T(8,128)(2,1)S(1)}, u32[]{:S(2)}, u32[]{:S(2)}) collective-permute-start(bf16[1024,1536]{1,0:T(8,128)(2,1)S(1)} %add.375), channel_id=1, source_target_pairs={{8,16},{12,20},{16,8},{20,12},{9,17},{13,21},{17,9},{21,13},{10,18... | collective-permute-start | bytes 9437192 | tf_op jit(solution)/shard_map/ppermute | solution.py:96
  710.9 194.9 %collective-permute-start.77 = (bf16[768,2048]{1,0:T(8,128)(2,1)S(1)}, bf16[768,2048]{1,0:T(8,128)(2,1)S(1)}, u32[]{:S(2)}, u32[]{:S(2)}) collective-permute-start(bf16[768,2048]{1,0:T(8,128)(2,1)S(1)} %add.384), channel_id=1, source_target_pairs={{8,0},{12,4},{16,24},{20,28},{9,1},{13,5},{17,25},{21,29},{10,2},{... | collective-permute-start | bytes 9437192 | tf_op jit(solution)/shard_map/ppermute | solution.py:101
  715.8 154.3 %collective-permute-start.49 = (bf16[1024,704]{0,1:T(8,128)(2,1)S(1)}, bf16[1024,704]{0,1:T(8,128)(2,1)S(1)}, u32[]{:S(2)}, u32[]{:S(2)}) collective-permute-start(bf16[1024,704]{0,1:T(8,128)(2,1)S(1)} %add.361), channel_id=1, source_target_pairs={{8,0},{12,4},{16,24},{20,28},{9,1},{13,5},{17,25},{21,29},{10,2},{... | collective-permute-start | bytes 4325384 | tf_op jit(solution)/shard_map/ppermute | solution.py:101
  733.7 167.3 %collective-permute-start.44 = (bf16[1024,704]{0,1:T(8,128)(2,1)S(1)}, bf16[1024,704]{0,1:T(8,128)(2,1)S(1)}, u32[]{:S(2)}, u32[]{:S(2)}) collective-permute-start(bf16[1024,704]{0,1:T(8,128)(2,1)S(1)} %add.358), channel_id=1, source_target_pairs={{8,0},{12,4},{16,24},{20,28},{9,1},{13,5},{17,25},{21,29},{10,2},{... | collective-permute-start | bytes 4325384 | tf_op jit(solution)/shard_map/ppermute | solution.py:101
  736.5 164.7 %collective-permute-start.63 = (bf16[352,2048]{1,0:T(8,128)(2,1)S(1)}, bf16[352,2048]{1,0:T(8,128)(2,1)}, u32[]{:S(2)}, u32[]{:S(2)}) collective-permute-start(bf16[352,2048]{1,0:T(8,128)(2,1)S(1)} %broadcast_select_fusion.9), channel_id=1, source_target_pairs={{0,4},{4,0},{8,12},{12,8},{16,20},{20,16},{24,28},{28,24},{1,5},{5... | collective-permute-start | bytes 4325384 | tf_op jit(solution)/shard_map/ppermute | solution.py:39
  870.2 98.4 %collective-permute-start.72 = (bf16[1024,1536]{1,0:T(8,128)(2,1)S(1)}, bf16[1024,1536]{1,0:T(8,128)(2,1)}, u32[]{:S(2)}, u32[]{:S(2)}) collective-permute-start(bf16[1024,1536]{1,0:T(8,128)(2,1)S(1)} %add.379), channel_id=1, source_target_pairs={{8,0},{12,4},{16,24},{20,28},{9,1},{13,5},{17,25},{21,29},{10,2},{... | collective-permute-start | bytes 9437192 | tf_op jit(solution)/shard_map/ppermute | solution.py:101
  901.2 69.7 %collective-permute-start.45 = (bf16[1024,704]{0,1:T(8,128)(2,1)S(1)}, bf16[1024,704]{0,1:T(8,128)(2,1)S(1)}, u32[]{:S(2)}, u32[]{:S(2)}) collective-permute-start(bf16[1024,704]{0,1:T(8,128)(2,1)S(1)} %broadcast_select_fusion.13), channel_id=1, source_target_pairs={{0,4},{4,0},{8,12},{12,8},{16,20},{20,16},{24,28},{28,24},{1,5},{5... | collective-permute-start | bytes 4325384 | tf_op jit(solution)/shard_map/ppermute | solution.py:39
  904.2 119.9 %collective-permute-start.67 = (bf16[1024,1536]{1,0:T(8,128)(2,1)S(1)}, bf16[1024,1536]{1,0:T(8,128)(2,1)S(1)}, u32[]{:S(2)}, u32[]{:S(2)}) collective-permute-start(bf16[1024,1536]{1,0:T(8,128)(2,1)S(1)} %add.376), channel_id=1, source_target_pairs={{8,0},{12,4},{16,24},{20,28},{9,1},{13,5},{17,25},{21,29},{10,2},{... | collective-permute-start | bytes 9437192 | tf_op jit(solution)/shard_map/ppermute | solution.py:101
  906.1 118.5 %collective-permute-start.78 = (bf16[768,2048]{1,0:T(8,128)(2,1)S(1)}, bf16[768,2048]{1,0:T(8,128)(2,1)}, u32[]{:S(2)}, u32[]{:S(2)}) collective-permute-start(bf16[768,2048]{1,0:T(8,128)(2,1)S(1)} %broadcast_select_fusion), channel_id=1, source_target_pairs={{0,4},{4,0},{8,12},{12,8},{16,20},{20,16},{24,28},{28,24},{1,5},{5... | collective-permute-start | bytes 9437192 | tf_op jit(solution)/shard_map/ppermute | solution.py:39
  (118 other events, 2406.9 us)

commit v2 on v1

--- a/solution.py
+++ b/solution.py
@@ -1,4 +1,4 @@
-import functools
+import math
 
 import jax
 import jax.numpy as jnp
@@ -30,8 +30,8 @@
     return jax.nn.gelu(values, approximate=True)
 
 
-def dense_act(gate_values, up_values):
-    return gelu_tanh(gate_values) * up_values
+def tied(*values):
+    return lax.optimization_barrier(values)
 
 
 def swap(value, axis, bit):
@@ -39,16 +39,22 @@
     return lax.ppermute(value, axis, [(i, i ^ bit) for i in range(count)])
 
 
-def gather_rel(rows):
+def gather_rows(rows):
     count = lax.axis_size("tp")
-    return jnp.stack([rows] + [swap(rows, "tp", r) for r in range(1, count)], axis=0)
-
-
-def scatter_rel(blocks):
-    count = lax.axis_size("tp")
-    total = blocks[0].astype(f32)
-    for r in range(1, count):
-        total = total + swap(blocks[r], "tp", r).astype(f32)
+    place = lax.axis_index("tp")
+    whole = jnp.zeros((count,) + rows.shape, rows.dtype)
+    for r in range(count):
+        block = rows if r == 0 else swap(rows, "tp", r)
+        whole = lax.dynamic_update_index_in_dim(whole, block, place ^ r, 0)
+    return whole
+
+
+def scatter_rows(blocks):
+    place = lax.axis_index("tp")
+    block = lambda r: lax.dynamic_index_in_dim(blocks, place ^ r, 0, False)
+    total = block(0).astype(f32)
+    for r in range(1, lax.axis_size("tp")):
+        total = total + swap(block(r), "tp", r).astype(f32)
     return total
 
 
@@ -70,6 +76,15 @@
     return before[1]
 
 
+def from_neighbour(value, step):
+    count = lax.axis_size("seq")
+    place = lax.axis_index("seq")
+    inside = lax.ppermute(value, "seq", [(i, i ^ 1) for i in range(count)])
+    pairs = [(i, i + 1) for i in range(1, count - 1, 2)] + [(i + 1, i) for i in range(1, count - 1, 2)]
+    across = lax.ppermute(value, "seq", pairs)
+    return jnp.where((place % 2 == 0) == (step == 1), inside, across)
+
+
 def sum_bits(value, axis):
     bit = 1
     while bit < lax.axis_size(axis):
@@ -78,46 +93,336 @@
     return value
 
 
-def line_pairs(kind):
-    pairs = []
-    for i in range(lax.axis_size("seq")):
-        chip, core = i // 2, i % 2
-        base, z = chip // 4 * 4, chip % 4
-        to = {"in": {0: 1, 3: 2}, "mid": {1: 2, 2: 1}, "out": {1: 0, 2: 3}}[kind].get(z)
-        if to is not None:
-            pairs.append((i, (base + to) * 2 + core))
-    return pairs
-
-
-def line_sum(part):
-    z = lax.axis_index("seq") // 2 % 4
-    at_end = jnp.logical_or(z == 0, z == 3)
-    half = part + lax.ppermute(part, "seq", line_pairs("in"))
-    total = half + lax.ppermute(half, "seq", line_pairs("mid"))
-    bit = 8
-    while bit < lax.axis_size("seq"):
-        total = total + swap(total, "seq", bit)
-        bit *= 2
-    return jnp.where(at_end, lax.ppermute(total, "seq", line_pairs("out")), total)
-
-
 def both_halves(mine, theirs, core):
     first = jnp.where(core == 0, mine, theirs)
     second = jnp.where(core == 0, theirs, mine)
     return first, second
 
 
-def summed_grad(left, right, core):
-    width = left.shape[1] // 2
-    theirs = lax.dynamic_slice_in_dim(left, (1 - core) * width, width, 1)
-    ours = lax.dynamic_slice_in_dim(left, core * width, width, 1)
-    away = product_left_t(theirs, right).astype(bf16)
-    back = swap(away, "seq", 1)
-    part = (product_left_t(ours, right) + back.astype(f32)).astype(bf16)
-    total = line_sum(part)
-    other = swap(total, "seq", 1)
-    first, second = both_halves(total, other, core)
-    return jnp.concatenate([first, second], axis=0).astype(f32)
+def gelu_grads(gate_pre, up_pre, hidden_grad):
+    square = gate_pre * gate_pre
+    inner = math.sqrt(2.0 / math.pi) * gate_pre * (1.0 + 0.044715 * square)
+    half = 0.5 * (1.0 + jnp.tanh(inner))
+    act = gate_pre * half
+    slope = half + 2.0 * math.sqrt(2.0 / math.pi) * act * (1.0 - half) * (1.0 + 3.0 * 0.044715 * square)
+    return act * up_pre, hidden_grad * up_pre * slope, hidden_grad * act
+
+
+def dense_weight_grads(mine, theirs, cot_all, gate_proj, up_proj, down_proj, places):
+    tp_size, chips, block, model = mine.shape
+    half = gate_proj.shape[1] // 2
+    cot_all = cot_all.reshape(chips, 2, tp_size, block, model)
+    part = math.gcd(chips, 4)
+    length = part * block
+    per_core = tp_size * chips // part
+    steps, outs = 2 * per_core, 4
+    tile = math.gcd(half, 256)
+    left_t = (((0,), (0,)), ((), ()))
+    right_t = (((1,), (1,)), ((), ()))
+
+    def kernel(core_ref, mine_ref, theirs_ref, cot_ref, gate_ref, up_ref, down_ref, *rest):
+        gate_out, up_out, down_out, acc_g, acc_u, acc_d, hid, gg, ug, x_ref = rest
+        i = pl.program_id(0)
+
+        @pl.when(i < per_core)
+        def _():
+            x_ref[...] = mine_ref[...].reshape(length, model)
+
+        @pl.when(jnp.logical_and(i >= per_core, i < steps))
+        def _():
+            x_ref[...] = theirs_ref[...].reshape(length, model)
+
+        @pl.when(i == 0)
+        def _():
+            acc_g[...] = jnp.zeros_like(acc_g)
+            acc_u[...] = jnp.zeros_like(acc_u)
+            acc_d[...] = jnp.zeros_like(acc_d)
+
+        @pl.when(i < steps)
+        def _():
+            cots = cot_ref[...].reshape(length, model)
+            for n in range(half // tile):
+                cols = slice(n * tile, (n + 1) * tile)
+                gate_pre = jnp.dot(x_ref[...], gate_ref[:, cols], preferred_element_type=f32)
+                up_pre = jnp.dot(x_ref[...], up_ref[:, cols], preferred_element_type=f32)
+                hidden_grad = lax.dot_general(cots, down_ref[cols, :], right_t, preferred_element_type=f32)
+                a, b, c = gelu_grads(gate_pre, up_pre, hidden_grad)
+                hid[:, cols] = a.astype(bf16)
+                gg[:, cols] = b.astype(bf16)
+                ug[:, cols] = c.astype(bf16)
+            acc_g[...] += lax.dot_general(x_ref[...], gg[...], left_t, preferred_element_type=f32)
+            acc_u[...] += lax.dot_general(x_ref[...], ug[...], left_t, preferred_element_type=f32)
+            acc_d[...] += lax.dot_general(hid[...], cots, left_t, preferred_element_type=f32)
+
+        @pl.when(i >= steps)
+        def _():
+            wide = pl.ds(pl.multiple_of((i - steps) * (model // outs), model // outs), model // outs)
+            low = pl.ds(pl.multiple_of((i - steps) * (half // outs), half // outs), half // outs)
+            gate_out[...] = acc_g[wide, :].astype(bf16)
+            up_out[...] = acc_u[wide, :].astype(bf16)
+            down_out[...] = acc_d[low, :].astype(bf16)
+
+    once = pl.Buffered(1)
+    groups = chips // part
+    out_index = lambda i, c: (jnp.maximum(i - steps, 0), 0)
+
+    def cot_index(i, c):
+        i = jnp.minimum(i, steps - 1)
+        n = i % per_core
+        return n % groups, c[0] ^ (i // per_core), n // groups, 0, 0
+
+    def rows_index(first):
+        def index(i, c):
+            n = jnp.clip(i - first, 0, per_core - 1)
+            return n // groups, n % groups, 0, 0
+
+        return pl.BlockSpec((1, part, block, model), index)
+
+    return pl.pallas_call(
+        kernel,
+        grid_spec=pltpu.PrefetchScalarGridSpec(
+            num_scalar_prefetch=1,
+            grid=(steps + outs,),
+            in_specs=[
+                rows_index(0),
+                rows_index(per_core),
+                pl.BlockSpec((part, 1, 1, block, model), cot_index),
+                pl.BlockSpec((model, half), lambda i, c: (0, c[0]), pipeline_mode=once),
+                pl.BlockSpec((model, half), lambda i, c: (0, c[0]), pipeline_mode=once),
+                pl.BlockSpec((half, model), lambda i, c: (c[0], 0), pipeline_mode=once),
+            ],
+            out_specs=[
+                pl.BlockSpec((model // outs, half), out_index),
+                pl.BlockSpec((model // outs, half), out_index),
+                pl.BlockSpec((half // outs, model), out_index),
+            ],
+            scratch_shapes=[
+                pltpu.VMEM((model, half), f32),
+                pltpu.VMEM((model, half), f32),
+                pltpu.VMEM((half, model), f32),
+                pltpu.VMEM((length, half), bf16),
+                pltpu.VMEM((length, half), bf16),
+                pltpu.VMEM((length, half), bf16),
+                pltpu.VMEM((length, model), bf16),
+            ],
+        ),
+        out_shape=[
+            jax.ShapeDtypeStruct((model, half), bf16),
+            jax.ShapeDtypeStruct((model, half), bf16),
+            jax.ShapeDtypeStruct((half, model), bf16),
+        ],
+        compiler_params=pltpu.CompilerParams(vmem_limit_bytes=60 * 1024 * 1024),
+        cost_estimate=pl.CostEstimate(flops=1000, bytes_accessed=1000, transcendentals=0),
+        name="dense_weight_grads",
+    )(places, mine, theirs, cot_all, gate_proj, up_proj, down_proj)
+
+
+def joined(mine, theirs, core, axis):
+    rows, cols = mine.shape
+    block = math.gcd(rows, 256)
+    steps = rows // block
+
+    def kernel(core_ref, mine_ref, theirs_ref, out_ref):
+        for low in range(2):
+
+            @pl.when(core_ref[0] == low)
+            def _(low=low):
+                pair = (mine_ref, theirs_ref) if low == 0 else (theirs_ref, mine_ref)
+                if axis == 1:
+                    out_ref[:, :cols] = pair[0][...].astype(f32)
+                    out_ref[:, cols:] = pair[1][...].astype(f32)
+                else:
+                    out_ref[0] = pair[0][...].astype(f32)
+                    out_ref[1] = pair[1][...].astype(f32)
+
+    half = pl.BlockSpec((block, cols), lambda i, c: (i, 0))
+    if axis == 1:
+        out_spec = pl.BlockSpec((block, 2 * cols), lambda i, c: (i, 0))
+        out_shape = jax.ShapeDtypeStruct((rows, 2 * cols), f32)
+    else:
+        out_spec = pl.BlockSpec((2, block, cols), lambda i, c: (0, i, 0))
+        out_shape = jax.ShapeDtypeStruct((2, rows, cols), f32)
+    out = pl.pallas_call(
+        kernel,
+        grid_spec=pltpu.PrefetchScalarGridSpec(
+            num_scalar_prefetch=1, grid=(steps,), in_specs=[half, half], out_specs=out_spec
+        ),
+        out_shape=out_shape,
+        compiler_params=pltpu.CompilerParams(vmem_limit_bytes=VMEM_LIMIT),
+        cost_estimate=pl.CostEstimate(flops=1000, bytes_accessed=1000, transcendentals=0),
+        name="joined",
+    )(core, mine, theirs)
+    return out if axis == 1 else out.reshape(2 * rows, cols)
+
+
+def dense_rows(rows, cot_all, group_place, gate_proj, up_proj, down_proj):
+    length, model = rows.shape
+    width = gate_proj.shape[1]
+    tile = math.gcd(width, 256)
+    out_tile = math.gcd(model, 256)
+    first, second = width // tile, model // out_tile
+    right_t = (((1,), (1,)), ((), ()))
+
+    def kernel(place_ref, x_ref, c_ref, gate_ref, up_ref, down_ref, hidden_ref, grad_ref, gates, ups, gate_grads, up_grads):
+        j = pl.program_id(0)
+
+        @pl.when(j < first)
+        def _():
+            gate_pre = jnp.dot(x_ref[...], gate_ref[...], preferred_element_type=f32)
+            up_pre = jnp.dot(x_ref[...], up_ref[...], preferred_element_type=f32)
+            hidden_grad = lax.dot_general(c_ref[...], down_ref[...], right_t, preferred_element_type=f32)
+            hidden, gate_grad, up_grad = gelu_grads(gate_pre, up_pre, hidden_grad)
+            hidden_ref[...] = hidden.astype(bf16)
+            at = pl.ds(pl.multiple_of(j * tile, tile), tile)
+            gates[:, at] = gate_ref[...]
+            ups[:, at] = up_ref[...]
+            gate_grads[:, at] = gate_grad.astype(bf16)
+            up_grads[:, at] = up_grad.astype(bf16)
+
+        @pl.when(j >= first)
+        def _():
+            at = pl.ds(pl.multiple_of((j - first) * out_tile, out_tile), out_tile)
+            part = lax.dot_general(gate_grads[...], gates[at, :], right_t, preferred_element_type=f32)
+            part = part + lax.dot_general(up_grads[...], ups[at, :], right_t, preferred_element_type=f32)
+            grad_ref[...] = part.astype(bf16)
+
+    clamp = lambda j: jnp.minimum(j, first - 1)
+    wide = pl.BlockSpec((model, tile), lambda j, p: (0, clamp(j)))
+    return pl.pallas_call(
+        kernel,
+        grid_spec=pltpu.PrefetchScalarGridSpec(
+            num_scalar_prefetch=1,
+            grid=(first + second,),
+            in_specs=[
+                pl.BlockSpec((length, model), lambda j, p: (0, 0)),
+                pl.BlockSpec((length, model), lambda j, p: (p[0], 0)),
+                wide,
+                wide,
+                pl.BlockSpec((tile, model), lambda j, p: (clamp(j), 0)),
+            ],
+            out_specs=[
+                pl.BlockSpec((length, tile), lambda j, p: (0, clamp(j))),
+                pl.BlockSpec((length, out_tile), lambda j, p: (0, jnp.maximum(j - first, 0))),
+            ],
+            scratch_shapes=[
+                pltpu.VMEM((model, width), bf16),
+                pltpu.VMEM((model, width), bf16),
+                pltpu.VMEM((length, width), bf16),
+                pltpu.VMEM((length, width), bf16),
+            ],
+        ),
+        out_shape=[
+            jax.ShapeDtypeStruct((length, width), bf16),
+            jax.ShapeDtypeStruct((length, model), bf16),
+        ],
+        compiler_params=pltpu.CompilerParams(vmem_limit_bytes=VMEM_LIMIT),
+        name="dense_rows",
+    )(group_place, rows, cot_all, gate_proj, up_proj, down_proj)
+
+
+def project_t(rows, weight_t):
+    total, model = rows.shape
+    width = weight_t.shape[0]
+    length = math.gcd(total, 256)
+
+    def kernel(rows_ref, weight_ref, out_ref):
+        out_ref[...] = lax.dot_general(
+            rows_ref[...], weight_ref[...], (((1,), (1,)), ((), ())), preferred_element_type=f32
+        )
+
+    return pl.pallas_call(
+        kernel,
+        grid=(total // length,),
+        in_specs=[
+            pl.BlockSpec((length, model), lambda j: (j, 0)),
+            pl.BlockSpec((width, model), lambda j: (0, 0)),
+        ],
+        out_specs=pl.BlockSpec((length, width), lambda j: (j, 0)),
+        out_shape=jax.ShapeDtypeStruct((total, width), f32),
+        compiler_params=pltpu.CompilerParams(vmem_limit_bytes=VMEM_LIMIT),
+        name="project_t",
+    )(rows, weight_t)
+
+
+def mix_out(value_prefix, keep_prefix, branch_pre, state_in, out_proj):
+    blocks, length, width = value_prefix.shape
+    model = out_proj.shape[1]
+
+    def kernel(value_ref, keep_ref, branch_ref, in_ref, out_ref, state_ref, mixed_ref, part_ref):
+        state = value_ref[0] + keep_ref[0] * in_ref[...]
+        state_ref[0] = state
+        mixed = (state * gelu_tanh(branch_ref[0])).astype(bf16)
+        mixed_ref[0] = mixed
+        part_ref[0] = jnp.dot(mixed, out_ref[...], preferred_element_type=f32).astype(bf16)
+
+    block = pl.BlockSpec((1, length, width), lambda j: (j, 0, 0))
+    whole = lambda *shape: pl.BlockSpec(shape, lambda j: (0,) * len(shape))
+    return pl.pallas_call(
+        kernel,
+        grid=(blocks,),
+        in_specs=[block, block, block, whole(1, width), whole(width, model)],
+        out_specs=[block, block, pl.BlockSpec((1, length, model), lambda j: (j, 0, 0))],
+        out_shape=[
+            jax.ShapeDtypeStruct((blocks, length, width), f32),
+            jax.ShapeDtypeStruct((blocks, length, width), bf16),
+            jax.ShapeDtypeStruct((blocks, length, model), bf16),
+        ],
+        compiler_params=pltpu.CompilerParams(vmem_limit_bytes=VMEM_LIMIT),
+        name="mix_out",
+    )(value_prefix, keep_prefix, branch_pre, state_in, out_proj)
+
+
+def mix_back(mid_rows, out_proj, branch_pre, state, keep_prefix):
+    blocks, length, width = state.shape
+    model = out_proj.shape[1]
+    tiles = length // 16
+
+    def kernel(mid_ref, out_ref, branch_ref, state_ref, keep_ref, direct_ref, branch_grad_ref, reach_ref, mixed, acc):
+        j = pl.program_id(0)
+        mixed[...] = lax.dot_general(
+            mid_ref[0], out_ref[...], (((1,), (1,)), ((), ())), preferred_element_type=f32
+        )
+
+        @pl.when(j == 0)
+        def _():
+            acc[...] = jnp.zeros_like(acc)
+
+        def tile(i, total):
+            at = pl.ds(pl.multiple_of(i * 16, 16), 16)
+            grad = mixed[at, :]
+            pre = branch_ref[0, at, :]
+            square = pre * pre
+            inner = math.sqrt(2.0 / math.pi) * pre * (1.0 + 0.044715 * square)
+            half = 0.5 * (1.0 + jnp.tanh(inner))
+            act = pre * half
+            slope = half + 2.0 * math.sqrt(2.0 / math.pi) * act * (1.0 - half) * (1.0 + 3.0 * 0.044715 * square)
+            direct = grad * act
+            direct_ref[0, at, :] = direct
+            branch_grad_ref[0, at, :] = (grad * state_ref[0, at, :] * slope).astype(bf16)
+            return total + direct * keep_ref[0, at, :]
+
+        acc[...] = lax.fori_loop(0, tiles, tile, acc[...])
+
+        @pl.when(j == blocks - 1)
+        def _():
+            reach_ref[...] = jnp.sum(acc[...], axis=0, keepdims=True)
+
+    block = pl.BlockSpec((1, length, width), lambda j: (j, 0, 0))
+    whole = lambda *shape: pl.BlockSpec(shape, lambda j: (0,) * len(shape))
+    return pl.pallas_call(
+        kernel,
+        grid=(blocks,),
+        in_specs=[pl.BlockSpec((1, length, model), lambda j: (j, 0, 0)), whole(width, model), block, block, block],
+        out_specs=[block, block, whole(1, width)],
+        out_shape=[
+            jax.ShapeDtypeStruct((blocks, length, width), f32),
+            jax.ShapeDtypeStruct((blocks, length, width), bf16),
+            jax.ShapeDtypeStruct((1, width), f32),
+        ],
+        scratch_shapes=[pltpu.VMEM((length, width), f32), pltpu.VMEM((16, width), f32)],
+        compiler_params=pltpu.CompilerParams(vmem_limit_bytes=VMEM_LIMIT),
+        name="mix_back",
+    )(mid_rows, out_proj, branch_pre, state, keep_prefix)
 
 
 def minus_expm1(x):
@@ -148,7 +453,6 @@
 
 
 def forward_kernel(
-    place_ref,
     inner_ref,
     mask_ref,
     rim_ref,
@@ -226,7 +530,6 @@
 
 
 def backward_kernel(
-    place_ref,
     direct_ref,
     state_ref,
     state_prev_ref,
@@ -382,19 +685,60 @@
         sums_ref[...] = jnp.sum(acc_ref[...], axis=1)
 
 
-def recur_forward(place, inner, masks, rim, taps, vecs, rate_dense, input_dense):
+def norm_project(blocks, place, gain, weight_t):
+    count = len(blocks)
+    length, model = blocks[0].shape
+    width = weight_t.shape[0]
+
+    def kernel(place_ref, *refs):
+        ins, gain_ref, weight_ref, normed_ref, out_ref = refs[:count], *refs[count:]
+        j = pl.program_id(0)
+        for r in range(count):
+
+            @pl.when((j ^ place_ref[0]) == r)
+            def _(source=ins[r]):
+                x = source[...].astype(f32)
+                root = lax.rsqrt(jnp.mean(x * x, axis=-1, keepdims=True) + epsilon)
+                normed_ref[...] = (x * root * gain_ref[...]).astype(bf16)
+
+        out_ref[0] = lax.dot_general(
+            normed_ref[...], weight_ref[...], (((1,), (1,)), ((), ())), preferred_element_type=f32
+        )
+
+    whole = lambda *shape: pl.BlockSpec(shape, lambda j, p: (0,) * len(shape))
+    return pl.pallas_call(
+        kernel,
+        grid_spec=pltpu.PrefetchScalarGridSpec(
+            num_scalar_prefetch=1,
+            grid=(count,),
+            in_specs=[whole(length, model)] * count + [whole(1, model), whole(width, model)],
+            out_specs=[
+                pl.BlockSpec((length, model), lambda j, p: (j, 0)),
+                pl.BlockSpec((1, length, width), lambda j, p: (j, 0, 0)),
+            ],
+        ),
+        out_shape=[
+            jax.ShapeDtypeStruct((count * length, model), bf16),
+            jax.ShapeDtypeStruct((count, length, width), f32),
+        ],
+        compiler_params=pltpu.CompilerParams(vmem_limit_bytes=VMEM_LIMIT),
+        name="norm_project",
+    )(place, *blocks, gain, weight_t)
+
+
+def recur_forward(inner, masks, rim, taps, vecs, rate_dense, input_dense):
     blocks, length, width = inner.shape
-    whole = lambda *shape: pl.BlockSpec(shape, lambda j, p: (0,) * len(shape))
-    block = pl.BlockSpec((1, length, width), lambda j, p: (j ^ p[0], 0, 0))
+    whole = lambda *shape: pl.BlockSpec(shape, lambda j: (0,) * len(shape))
+    block = pl.BlockSpec((1, length, width), lambda j: (j, 0, 0))
     full = jax.ShapeDtypeStruct((blocks, length, width), f32)
     return pl.pallas_call(
         forward_kernel,
         grid_spec=pltpu.PrefetchScalarGridSpec(
-            num_scalar_prefetch=1,
+            num_scalar_prefetch=0,
             grid=(blocks,),
             in_specs=[
                 block,
-                pl.BlockSpec((length, masks.shape[1]), lambda j, p: (j, 0)),
+                pl.BlockSpec((length, masks.shape[1]), lambda j: (j, 0)),
                 whole(*rim.shape),
                 whole(*taps.shape),
                 whole(*vecs.shape),
@@ -420,18 +764,18 @@
         ],
         compiler_params=pltpu.CompilerParams(vmem_limit_bytes=VMEM_LIMIT),
         name="recur_forward",
-    )(place, inner, masks, rim, taps, vecs, rate_dense, input_dense)
+    )(inner, masks, rim, taps, vecs, rate_dense, input_dense)
 
 
 def recur_backward(
-    place, direct, state, conv, sig_rate, sig_input, inner, masks, rim, state_in, after, taps, vecs, rate_dense, input_dense
+    direct, state, conv, sig_rate, sig_input, inner, masks, rim, state_in, after, taps, vecs, rate_dense, input_dense
 ):
     blocks, length, width = inner.shape
     last = length // TILE - 1
-    whole = lambda *shape: pl.BlockSpec(shape, lambda j, p: (0,) * len(shape))
-    block = pl.BlockSpec((1, length, width), lambda j, p: ((blocks - 1 - j) ^ p[0], 0, 0))
+    whole = lambda *shape: pl.BlockSpec(shape, lambda j: (0,) * len(shape))
+    block = pl.BlockSpec((1, length, width), lambda j: (blocks - 1 - j, 0, 0))
     edge = pl.BlockSpec(
-        (1, TILE, width), lambda j, p: (jnp.maximum(blocks - 2 - j, 0) ^ p[0], last, 0)
+        (1, TILE, width), lambda j: (jnp.maximum(blocks - 2 - j, 0), last, 0)
     )
     low = jax.ShapeDtypeStruct((blocks, length, width), bf16)
     tile = jax.ShapeDtypeStruct((TILE, width), f32)
@@ -439,7 +783,7 @@
     return pl.pallas_call(
         backward_kernel,
         grid_spec=pltpu.PrefetchScalarGridSpec(
-            num_scalar_prefetch=1,
+            num_scalar_prefetch=0,
             grid=(blocks,),
             in_specs=[
                 block,
@@ -450,7 +794,7 @@
                 block,
                 block,
                 edge,
-                pl.BlockSpec((length, masks.shape[1]), lambda j, p: (blocks - 1 - j, 0)),
+                pl.BlockSpec((length, masks.shape[1]), lambda j: (blocks - 1 - j, 0)),
                 whole(*rim.shape),
                 whole(*state_in.shape),
                 whole(*after.shape),
@@ -478,9 +822,9 @@
         ),
         out_shape=[low, low, low, tile, tile, jax.ShapeDtypeStruct((count, width), f32)],
         compiler_params=pltpu.CompilerParams(vmem_limit_bytes=VMEM_LIMIT),
+        cost_estimate=pl.CostEstimate(flops=1000, bytes_accessed=1000, transcendentals=0),
         name="recur_backward",
     )(
-        place,
         direct,
         state,
         state,
@@ -545,86 +889,85 @@
 ):
     tp_place = lax.axis_index("tp")
     seq_place = lax.axis_index("seq")
+    seq_size = lax.axis_size("seq")
     core = seq_place % 2
     tp_size = lax.axis_size("tp")
-    seq_size = lax.axis_size("seq")
-    place = tp_place.astype(jnp.int32)[None]
     gain_share = mixer_gain.shape[0]
     taps_n, width = conv_taps.shape
     rim_width = taps_n - 1
     length, model = tokens.shape
     group = length * tp_size
     blocks_n = rate_blocks.shape[0]
-    hidden_n = gate_proj.shape[1]
-    onward = [(i, i + 1) for i in range(seq_size - 1)]
-    backward_pairs = [(i + 1, i) for i in range(seq_size - 1)]
-
-    rows_rel = gather_rel(tokens)
-    gains = gather_rel(jnp.stack([mixer_gain, dense_gain]))
-    order = tp_place ^ jnp.arange(tp_size)
-    gains = jnp.take(gains, order, axis=0).transpose(1, 0, 2).reshape(2, -1).astype(f32)
+
+    in_t, branch_t = in_proj.T, branch_proj.T
+    place = tp_place.astype(jnp.int32)[None]
+
+    blocks = [tokens] + [swap(tokens, "tp", r) for r in range(1, tp_size)]
+    blocks[1], gains, ids, rate_in, input_in, vec_in = tied(
+        blocks[1],
+        jnp.stack([mixer_gain, dense_gain]),
+        segment_ids,
+        rate_blocks,
+        input_blocks,
+        (conv_bias, rate_bias, input_bias, decay_param),
+    )
+    gains = gather_rows(gains)
+    gains = gains.transpose(1, 0, 2).reshape(2, -1).astype(f32)
     mixer_scale, dense_scale = gains[0], gains[1]
-    rim_ids = lax.ppermute(segment_ids[-rim_width:], "seq", onward)
-    ext_ids = jnp.concatenate([rim_ids, segment_ids])
-    same = [ext_ids[rim_width - k : rim_width - k + group] == segment_ids for k in range(1, taps_n)]
+    rim_ids = from_neighbour(ids[-rim_width:], -1)
+    ext_ids = jnp.concatenate([rim_ids, ids])
+    same = [ext_ids[rim_width - k : rim_width - k + group] == ids for k in range(1, taps_n)]
     masks = jnp.stack([same[0]] + same, axis=1).astype(f32)
-
-    rate_dense = dense_blocks(rate_blocks)
-    input_dense = dense_blocks(input_blocks)
-    decay_rate = jax.nn.softplus(-decay_param)
-    vecs = jnp.stack([conv_bias, rate_bias, input_bias, -8.0 * decay_rate])
-
-    rows_f = rows_rel.reshape(group, model).astype(f32)
-    normed = (rows_f * rms(rows_f) * mixer_scale).astype(bf16)
-    inner = product(normed, in_proj).reshape(tp_size, length, width)
-    last_block = lax.dynamic_index_in_dim(inner, (tp_size - 1) ^ tp_place, 0, False)
-    rim = lax.ppermute(last_block[-TILE:], "seq", onward)
-    branch_pre = product(normed, branch_proj)
+    rate_dense = dense_blocks(rate_in)
+    input_dense = dense_blocks(input_in)
+    vecs = jnp.stack([*vec_in[:3], -8.0 * jax.nn.softplus(-vec_in[3])])
+    *blocks, masks, rate_dense, input_dense, vecs = tied(*blocks, masks, rate_dense, input_dense, vecs)
+    cot_all = lax.all_gather(cotangent, ("seq", "tp"), axis=0, tiled=True)
+
+    normed, inner = norm_project(blocks, place, mixer_scale[None], in_t)
+    rim = from_neighbour(inner[-1, -TILE:], -1)
     conv, conv_low, sig_rate, sig_input, keep_prefix, value_prefix, ends = recur_forward(
-        place, inner, masks, rim, conv_taps, vecs, rate_dense, input_dense
-    )
+        inner, masks, rim, conv_taps, vecs, rate_dense, input_dense
+    )
+    ends, normed_b = tied(ends, normed)
     state_in = carry_in(ends[0, 0], ends[1, 0], False)
-    state = value_prefix + keep_prefix * state_in
-    branch = gelu_tanh(branch_pre).reshape(state.shape)
-    mixed = (state * branch).astype(bf16).reshape(group, width)
-    mixer_out = scatter_rel(product(mixed, out_proj).astype(bf16).reshape(tp_size, length, model))
+    branch_pre = project_t(normed_b, branch_t).reshape(inner.shape)
+    state, mixed, mixer_part = mix_out(value_prefix, keep_prefix, branch_pre, state_in[None], out_proj)
+    mixed = mixed.reshape(group, width)
+    mixer_out = scatter_rows(mixer_part)
     mid = tokens.astype(f32) + mixer_out
     mid_root = rms(mid)
     xhat_dense = mid * mid_root
     normed_two = (xhat_dense * dense_scale).astype(bf16)
 
-    rows_two = gather_rel(normed_two).reshape(group, model)
-    cot_rows = gather_rel(cotangent).reshape(group, model)
-    gate_pre = product(rows_two, gate_proj)
-    up_pre = product(rows_two, up_proj)
-    hidden_float, act_pull = jax.vjp(dense_act, gate_pre, up_pre)
-    hidden = hidden_float.astype(bf16)
-    hidden_grad = product_right_t(cot_rows, down_proj)
-    gate_float, up_float = act_pull(hidden_grad)
-    gate_grad = gate_float.astype(bf16)
-    up_grad = up_float.astype(bf16)
-    down_sum = summed_grad(hidden, cot_rows, core)
-    gate_sum = summed_grad(rows_two, gate_grad, core)
-    up_sum = summed_grad(rows_two, up_grad, core)
-    normed_two_part = product_right_t(gate_grad, gate_proj) + product_right_t(up_grad, up_proj)
-    normed_two_grad = scatter_rel(normed_two_part.astype(bf16).reshape(tp_size, length, model))
-    dense_out = scatter_rel(product(hidden, down_proj).astype(bf16).reshape(tp_size, length, model))
-    output = (mid + dense_out).astype(bf16)
+    chips = seq_size // 2
+    same_core = [[core_no + 2 * i for i in range(chips)] for core_no in range(2)]
+    rows_z = lax.all_gather(normed_two, "seq", axis=0, tiled=True, axis_index_groups=same_core)
+    rows_two, cot_all = tied(gather_rows(normed_two).reshape(group, model), cot_all)
+    hidden, normed_two_part = dense_rows(
+        rows_two, cot_all, seq_place.astype(jnp.int32)[None], gate_proj, up_proj, down_proj
+    )
+    normed_two_grad = scatter_rows(normed_two_part.reshape(tp_size, length, model))
+    dense_part = product(hidden, down_proj).astype(bf16)
+    normed_two_grad, dense_part, rows_z = tied(normed_two_grad, dense_part, rows_z)
+    rows_mine = lax.all_gather(rows_z, "tp", axis=0, tiled=True)
     mid_from_norm, dense_gain_part = norm_back(normed_two_grad, xhat_dense, dense_scale, mid_root)
     mid_grad = cotangent.astype(f32) + mid_from_norm
-
-    mid_rows = gather_rel(mid_grad.astype(bf16)).reshape(group, model)
-    mixed_grad = product_right_t(mid_rows, out_proj).reshape(state.shape)
-    work_branch, branch_pull = jax.vjp(gelu_tanh, branch_pre.reshape(state.shape))
-    direct = mixed_grad * work_branch
-    reach = jnp.sum(direct * keep_prefix, axis=(0, 1))
-    out_sum = summed_grad(mixed, mid_rows, core)
-    branch_pre_grad = branch_pull(mixed_grad * state)[0].astype(bf16).reshape(group, width)
-    branch_sum = summed_grad(normed, branch_pre_grad, core)
+    mid_blocks = gather_rows(mid_grad.astype(bf16))
+    mid_blocks, dense_part = tied(mid_blocks, dense_part)
+
+    dense_out = scatter_rows(dense_part.reshape(tp_size, length, model))
+    direct, branch_pre_grad, reach = mix_back(mid_blocks, out_proj, branch_pre, state, keep_prefix)
+    branch_pre_grad = branch_pre_grad.reshape(group, width)
+    mid_rows = mid_blocks.reshape(group, model)
+    reach, direct, branch_pre_grad, mid_rows = tied(reach[0], direct, branch_pre_grad, mid_rows)
     after = carry_in(ends[0, 0], reach, True)
+    out_full = product_left_t(mixed, mid_rows).astype(bf16)
+    branch_full = product_left_t(branch_pre_grad, normed).astype(bf16)
+    after, out_full, branch_full = tied(after, out_full, branch_full)
+    out_sum, branch_sum = lax.psum((out_full, branch_full), "seq")
     tile = lambda v: jnp.broadcast_to(v, (TILE, width))
     rate_low, input_low, inner_grad, tail, rim_grad, sums = recur_backward(
-        place,
         direct,
         state,
         conv,
@@ -640,44 +983,62 @@
         rate_dense,
         input_dense,
     )
-    fixed = tail + lax.ppermute(rim_grad, "seq", backward_pairs)
-    inner_grad = lax.dynamic_update_slice(
-        inner_grad, fixed.astype(bf16)[None], ((tp_size - 1) ^ tp_place, length - TILE, 0)
-    ).reshape(group, width)
-    in_sum = summed_grad(normed, inner_grad, core)
+    rim_grad, rows_mine = tied(rim_grad, rows_mine)
+    fixed = tail + from_neighbour(rim_grad, 1)
     low_rows = conv_low.reshape(group, width)
     rate_w = diagonal_blocks(product_left_t(low_rows, rate_low.reshape(group, width)), blocks_n)
     input_w = diagonal_blocks(product_left_t(low_rows, input_low.reshape(group, width)), blocks_n)
-    rate_w, input_w = rate_w.astype(bf16), input_w.astype(bf16)
-    ours, theirs = both_halves(rate_w, input_w, core)
-    block_total = line_sum((ours.astype(f32) + swap(theirs, "seq", 1).astype(f32)).astype(bf16))
-    rate_sum, input_sum = both_halves(block_total, swap(block_total, "seq", 1), core)
-    normed_part = product_right_t(inner_grad, in_proj) + product_right_t(branch_pre_grad, branch_proj)
-    normed_grad = scatter_rel(normed_part.astype(bf16).reshape(tp_size, length, model))
+    inner_grad = lax.dynamic_update_slice(
+        inner_grad, fixed.astype(bf16)[None], (tp_size - 1, length - TILE, 0)
+    ).reshape(group, width)
+    in_full = product_left_t(inner_grad, normed).astype(bf16)
+    block_full = jnp.concatenate([rate_w, input_w]).astype(bf16)
+    normed_part = (product(inner_grad, in_t) + product(branch_pre_grad, branch_t)).astype(bf16)
+    rows_theirs = swap(rows_mine, "seq", 1)
+    normed_part, in_full, block_full, rows_theirs, dense_out = tied(
+        normed_part, in_full, block_full, rows_theirs, dense_out
+    )
+    in_sum, block_sum = lax.psum((in_full, block_full), "seq", axis_index_groups=[list(range(seq_size))[::-1]])
+    normed_grad = scatter_rows(normed_part.reshape(tp_size, length, model))
+
+    core_no = core.astype(jnp.int32)[None]
+    blocked = lambda rows: rows.reshape(tp_size, chips, length, model)
+    gate_w, up_w, down_w = dense_weight_grads(
+        blocked(rows_mine), blocked(rows_theirs), cot_all, gate_proj, up_proj, down_proj, core_no
+    )
+    gate_w, up_w, down_w, out_sum, branch_sum, normed_grad = tied(
+        gate_w, up_w, down_w, out_sum, branch_sum, normed_grad
+    )
+    gate_sum = joined(gate_w, swap(gate_w, "seq", 1), core_no, 1)
+    up_sum = joined(up_w, swap(up_w, "seq", 1), core_no, 1)
+    down_sum = joined(down_w, swap(down_w, "seq", 1), core_no, 0)
+    gate_sum, up_sum, down_sum, in_sum, block_sum = tied(gate_sum, up_sum, down_sum, in_sum, block_sum)
+
+    output = (mid + dense_out).astype(bf16)
     own = tokens.astype(f32)
     own_root = rms(own)
     rows_grad, mixer_gain_part = norm_back(normed_grad, own * own_root, mixer_scale, own_root)
     tokens_grad = mid_grad + rows_grad
-
     gain_parts = sum_bits(jnp.stack([mixer_gain_part, dense_gain_part]), "tp")
     gain_own = lax.dynamic_slice_in_dim(gain_parts, tp_place * gain_share, gain_share, 1)
     gain_sum = sum_bits(gain_own, "seq")
     sums = sum_bits(sums, "seq")
     decay_sum = 8.0 * jax.nn.sigmoid(-decay_param) * sums[2]
+    rate_sum, input_sum = block_sum[:blocks_n].astype(f32), block_sum[blocks_n:].astype(f32)
     return (
         output,
         tokens_grad,
         gain_sum[0],
-        in_sum,
-        branch_sum,
+        in_sum.astype(f32).T,
+        branch_sum.astype(f32).T,
         sums[4 : 4 + taps_n],
         sums[3],
-        rate_sum.astype(f32),
+        rate_sum,
         sums[0],
-        input_sum.astype(f32),
+        input_sum,
         sums[1],
         decay_sum,
-        out_sum,
+        out_sum.astype(f32),
         gain_sum[1],
         gate_sum,
         up_sum,

time: 1060 us -> 589 us (0.56)
  waiting for transfers between devices: 668 us -> 202 us
  Pallas kernels: 35.3 us -> 201 us
  other arithmetic: 116 us -> 36 us
  matrix products: 103 us -> 23.6 us
  starting transfers between devices: 108 us -> 67.8 us
  local copies, waits for them, and re-layouts: 18.5 us -> 36.9 us
  between operations: 2.56 us -> 15 us
    ppermute x24 -> x6, waiting for transfers between devices: 458 us -> 0.86 us  [the longest x3 0.85 us: from_neighbour(): inside = lax.ppermute(value, 'seq', [(i, i ^ 1) for i in range(count)])]
    pallas_call x0 -> x9, Pallas kernels: none -> 167 us  [the longest x1 94.1 us: dense_weight_grads(): pl.pallas_call(kernel, grid_spec=pltpu.PrefetchScalarGridSpec(num_scalar_...]
    ppermute x55 -> x42, waiting for transfers between devices: 210 us -> 147 us  [swap(): return lax.ppermute(value, axis, [(i, i ^ bit) for i in range(count)])]
    psum x0 -> x2, waiting for transfers between devices: none -> 44.2 us  [the longest x1 44.2 us: shards(): lax.psum((in_full, block_full), 'seq', axis_index_groups=[list(range(seq_...]
    convert_element_type x14 -> x3, other arithmetic: 41.3 us -> 5.63 us  [the longest x1 3.31 us: shards(): out_sum.astype(f32)]
    dot_general x6 -> x0, matrix products: 33.7 us -> none  [product_right_t(): lax.dot_general(left, right, (((1,), (1,)), ((), ())), preferred_element_...]
    add x14 -> x3, other arithmetic: 33.2 us -> 5.63 us  [scatter_rows(): total = total + swap(block(r), 'tp', r).astype(f32)]
    ppermute x24 -> x6, starting transfers between devices: 50 us -> 22.9 us  [the longest x3 13.6 us: from_neighbour(): across = lax.ppermute(value, 'seq', pairs)]
  transfers between devices with their start and end apart: 79 -> 53, of which waited for: 36 -> 27; matrix products, arithmetic and copies ran while one was open for 16% -> 13% of each run, Pallas kernels for 2% -> 35%
where the time goes in v2:
time: 589 us; the launch traced here: 583 us
  waiting for transfers between devices  202 us (34%)
  Pallas kernels  201 us (34%)
  starting transfers between devices  67.8 us (12%)
  local copies, waits for them, and re-layouts  36.9 us (6%)
  other arithmetic  36 us (6%)
  matrix products  23.6 us (4%)
  between operations  15 us (3%)
    ppermute x42, waiting for transfers between devices, swap(): return lax.ppermute(value, axis, [(i, i ^ bit) for i in range(count)])  147 us
    pallas_call x1, Pallas kernels, dense_weight_grads(): pl.pallas_call(kernel, grid_spec=pltpu.PrefetchScalarGridSpec(num_scalar_...  94.1 us
    ppermute x42, starting transfers between devices, swap(): return lax.ppermute(value, axis, [(i, i ^ bit) for i in range(count)])  44.5 us
    psum x1, waiting for transfers between devices, shards(): lax.psum((in_full, block_full), 'seq', axis_index_groups=[list(range(seq_...  44.2 us
    pallas_call x1, Pallas kernels, dense_rows(): pl.pallas_call(kernel, grid_spec=pltpu.PrefetchScalarGridSpec(num_scalar_...  25 us
    pallas_call x3, Pallas kernels, joined(): pl.pallas_call(kernel, grid_spec=pltpu.PrefetchScalarGridSpec(num_scalar_...  22.2 us
    pallas_call x1, Pallas kernels, recur_backward(): pl.pallas_call(backward_kernel, grid_spec=pltpu.PrefetchScalarGridSpec(nu...  19.3 us
    pallas_call x1, Pallas kernels, recur_forward(): pl.pallas_call(forward_kernel, grid_spec=pltpu.PrefetchScalarGridSpec(num...  15.2 us
  transfers between devices with their start and end apart: 53, of which 27 were waited for; matrix products, arithmetic and copies ran while one was open for 13% of the time, Pallas kernels for 35%

profile of v2, /device:TPU:0, one launch (start us, length us, event | category | flops | bytes accessed | tf_op | source)
XLA Modules:
  0.0 582.6 jit_solution(13212892214910128051)
XLA Ops:
  13.9 10.3 %collective-permute-done.refs_1_ = bf16[128,2048]{1,0:T(8,128)(2,1)S(1)} collective-permute-done((bf16[128,2048]{1,0:T(8,128)(2,1)}, bf16[128,2048]{1,0:T(8,128)(2,1)S(1)}, u32[]{:S(2)}, u32[]{:S(2)}) %collective-permute-start) | collective-permute-done | bytes 524320 | tf_op jit(solution)/shard_map/ppermute | solution.py:39
  44.0 7.0 %norm_project.1 = (bf16[512,2048]{1,0:T(8,128)(2,1)}, f32[4,128,704]{2,1,0:T(8,128)S(1)}) custom-call(s32[1]{0:T(128)} %bitcast.place_ref, bf16[128,2048]{1,0:T(8,128)(2,1)S(1)} %copy-done.7, bf16[128,2048]{1,0:T(8,128)(2,1)S(1)} %collective-permute-done.refs_1_, bf16[128,2048]{1,0:T(8,128)(2,1)S(1)} %collective-permute-done.1.refs_2_, ...), custom_call_target="tpu_custom_call" | custom-call | tf_op jit(solution)/shard_map/norm_project/pallas_call | solution.py:709
  55.9 15.2 %recur_forward.1 = (f32[4,128,704]{2,1,0:T(8,128)}, bf16[4,128,704]{2,1,0:T(8,128)(2,1)S(1)}, f32[4,128,704]{2,1,0:T(8,128)}, f32[4,128,704]{2,1,0:T(8,128)}, f3...) custom-call(f32[4,128,704]{2,1,0:T(8,128)} %copy-done, ...), custom_call_target="tpu_custom_call" | custom-call | tf_op jit(solution)/shard_map/recur_forward/pallas_call | solution.py:734
  87.3 6.4 %mix_out.1 = (f32[4,128,704]{2,1,0:T(8,128)S(1)}, bf16[4,128,704]{2,1,0:T(8,128)(2,1)S(1)}, bf16[4,128,2048]{2,1,0:T(8,128)(2,1)}) custom-call(f32[4,128,704]{2,1,0:T(8,128)S(1)} %copy-done.14, f32[4,128,704]{2,1,0:T(8,128)} %get-tuple-element.113.keep_ref, f32[4,128,704]{2,1,0:T(8,128)} %bitcast.158, f32[1,704]{1,0:T(1,128)S(1)} %get-tuple-element.184.in_ref, ...), custom_call_target="tpu_custom_call" | custom-call | tf_op jit(solution)/shard_map/mix_out/pallas_call | solution.py:360
  99.3 22.5 %collective-permute-done.13 = bf16[128,2048]{1,0:T(8,128)(2,1)S(1)} collective-permute-done((bf16[128,2048]{1,0:T(8,128)(2,1)S(1)}, bf16[128,2048]{1,0:T(8,128)(2,1)S(1)}, u32[]{:S(2)}, u32[]{:S(2)}) %collective-permute-start.13) | collective-permute-done | bytes 524320 | tf_op jit(solution)/shard_map/ppermute | solution.py:39
  121.8 19.1 %collective-permute-done.15 = bf16[128,2048]{1,0:T(8,128)(2,1)S(1)} collective-permute-done((bf16[128,2048]{1,0:T(8,128)(2,1)S(1)}, bf16[128,2048]{1,0:T(8,128)(2,1)S(1)}, u32[]{:S(2)}, u32[]{:S(2)}) %collective-permute-start.15) | collective-permute-done | bytes 524320 | tf_op jit(solution)/shard_map/ppermute | solution.py:39
  149.0 11.0 %collective-permute-done.16 = bf16[128,2048]{1,0:T(8,128)(2,1)} collective-permute-done((bf16[128,2048]{1,0:T(8,128)(2,1)S(1)}, bf16[128,2048]{1,0:T(8,128)(2,1)}, u32[]{:S(2)}, u32[]{:S(2)}) %collective-permute-start.16) | collective-permute-done | bytes 524320 | tf_op jit(solution)/shard_map/ppermute | solution.py:39
  161.9 9.5 %collective-permute-done.17 = bf16[128,2048]{1,0:T(8,128)(2,1)S(1)} collective-permute-done((bf16[128,2048]{1,0:T(8,128)(2,1)}, bf16[128,2048]{1,0:T(8,128)(2,1)S(1)}, u32[]{:S(2)}, u32[]{:S(2)}) %collective-permute-start.17) | collective-permute-done | bytes 524320 | tf_op jit(solution)/shard_map/ppermute | solution.py:39
  173.0 25.0 %dense_rows.1 = (bf16[512,1536]{1,0:T(8,128)(2,1)S(1)}, bf16[512,2048]{1,0:T(8,128)(2,1)S(1)}) custom-call(s32[1]{0:T(128)} %bitcast.18.place_ref, bf16[512,2048]{1,0:T(8,128)(2,1)} %bitcast.23.x_ref, bf16[4096,2048]{1,0:T(8,128)(2,1)} %all-gather.4.cloned.1.call-done.c_ref, bf16[2048,1536]{1,0:T(8,128)(2,1)} %gate_ref.3, bf16[2048,1536]{1,0:T(8,128)(2,1)} %up_ref.3, ...), custom_call_target="tpu_custom_call" | custom-call | tf_op jit(solution)/shard_map/dense_rows/pallas_call | solution.py:291
  206.4 6.7 %collective-permute-done.19 = bf16[128,2048]{1,0:T(8,128)(2,1)S(1)} collective-permute-done((bf16[128,2048]{1,0:T(8,128)(2,1)S(1)}, bf16[128,2048]{1,0:T(8,128)(2,1)S(1)}, u32[]{:S(2)}, u32[]{:S(2)}) %collective-permute-start.19) | collective-permute-done | bytes 524320 | tf_op jit(solution)/shard_map/ppermute | solution.py:39
  213.0 7.9 %collective-permute-done.21 = bf16[128,2048]{1,0:T(8,128)(2,1)S(1)} collective-permute-done((bf16[128,2048]{1,0:T(8,128)(2,1)S(1)}, bf16[128,2048]{1,0:T(8,128)(2,1)S(1)}, u32[]{:S(2)}, u32[]{:S(2)}) %collective-permute-start.21) | collective-permute-done | bytes 524320 | tf_op jit(solution)/shard_map/ppermute | solution.py:39
  232.8 18.8 %collective-permute-done.22 = bf16[128,2048]{1,0:T(8,128)(2,1)} collective-permute-done((bf16[128,2048]{1,0:T(8,128)(2,1)}, bf16[128,2048]{1,0:T(8,128)(2,1)}, u32[]{:S(2)}, u32[]{:S(2)}) %collective-permute-start.22) | collective-permute-done | bytes 524320 | tf_op jit(solution)/shard_map/ppermute | solution.py:39
  258.8 12.9 %collective-permute-done.24 = bf16[128,2048]{1,0:T(8,128)(2,1)S(1)} collective-permute-done((bf16[128,2048]{1,0:T(8,128)(2,1)}, bf16[128,2048]{1,0:T(8,128)(2,1)S(1)}, u32[]{:S(2)}, u32[]{:S(2)}) %collective-permute-start.24) | collective-permute-done | bytes 524320 | tf_op jit(solution)/shard_map/ppermute | solution.py:39
  272.6 8.0 %mix_back.1 = (f32[4,128,704]{2,1,0:T(8,128)S(1)}, bf16[4,128,704]{2,1,0:T(8,128)(2,1)S(1)}, f32[1,704]{1,0:T(1,128)S(1)}) custom-call(bf16[4,128,2048]{2,1,0:T(8,128)(2,1)} %bitcast_dynamic-update-slice_fusion.mid_ref, bf16[704,2048]{1,0:T(8,128)(2,1)} %out_ref.3, f32[4,128,704]{2,1,0:T(8,128)S(1)} %bitcast.159, f32[4,128,704]{2,1,0:T(8,128)} %copy-done.1, ...), custom_call_target="tpu_custom_call" | custom-call | tf_op jit(solution)/shard_map/mix_back/pallas_call | solution.py:412
  282.8 5.2 convolution_convert_fusion.1
  296.5 19.3 %recur_backward.1 = (bf16[4,128,704]{2,1,0:T(8,128)(2,1)S(1)}, bf16[4,128,704]{2,1,0:T(8,128)(2,1)S(1)}, bf16[4,128,704]{2,1,0:T(8,128)(2,1)S(1)}, f32[8,704]{1,...) custom-call(f32[4,128,704]{2,1,0:T(8,128)} %copy-done.13, f32[4,128,704]{2,1,0:T(8,128)} %copy-done.1, ...), custom_call_target="tpu_custom_call" | custom-call | flops 1000 | bytes 1000 | tf_op jit(solution)/shard_map/recur_backward/pallas_call | solution.py:783
  318.4 8.9 %all-gather.8.cloned.1.call-done = bf16[2048,2048]{1,0:T(8,128)(2,1)} async-done(((bf16[512,2048]{1,0:T(8,128)(2,1)}), bf16[2048,2048]{1,0:T(8,128)(2,1)}) %all-gather.8.cloned.1.call-update) | async-done | bytes 8388624 | tf_op jit(solution)/shard_map/all_gather | solution.py:953
  340.8 12.2 %collective-permute-start.29 = (f32[8,704]{1,0:T(8,128)S(1)}, f32[8,704]{1,0:T(8,128)S(1)}, u32[]{:S(2)}, u32[]{:S(2)}) collective-permute-start(f32[8,704]{1,0:T(8,128)S(1)} %get-tuple-element.143), channel_id=1, source_target_pairs={{4,8},{12,16},{20,24},{8,4},{16,12},{24,20},{5,9},{13,17},{21,25},... | collective-permute-start | bytes 67592 | tf_op jit(solution)/shard_map/ppermute | solution.py:84
  381.7 94.1 %dense_weight_grads.1 = (bf16[2048,768]{1,0:T(8,128)(2,1)}, bf16[2048,768]{1,0:T(8,128)(2,1)}, bf16[768,2048]{1,0:T(8,128)(2,1)}) custom-call(s32[1]{0:T(128)} %bitcast.53.core_ref, bf16[4,4,128,2048]{3,2,1,0:T(8,128)(2,1)} %bitcast.173, bf16[4,4,128,2048]{3,2,1,0:T(8,128)(2,1)} %bitcast.55.theirs_ref, bf16[4,2,4,128,2048]{4,3,2,1,0:T(8,128)(2,1)} %bitcast.168, ...), custom_call_target="tpu_custom_call" | custom-call | flops 1000 | bytes 1000 | tf_op jit(solution)/shard_map/dense_weight_grads/pallas_call | solution.py:181
  486.2 5.5 convert_bitcast_fusion
  502.0 6.3 %joined.5 = f32[2,768,2048]{2,1,0:T(8,128)} custom-call(s32[1]{0:T(128)} %bitcast.53.core_ref, bf16[768,2048]{1,0:T(8,128)(2,1)S(1)} %copy-done.10, bf16[768,2048]{1,0:T(8,128)(2,1)} %collective-permute-done.44.theirs_ref), custom_call_target="tpu_custom_call" | custom-call | flops 1000 | bytes 1000 | tf_op jit(solution)/shard_map/joined/pallas_call | solution.py:245
  508.3 8.0 %joined.4 = f32[2048,1536]{1,0:T(8,128)} custom-call(s32[1]{0:T(128)} %bitcast.53.core_ref, bf16[2048,768]{1,0:T(8,128)(2,1)S(1)} %copy-done.9, bf16[2048,768]{1,0:T(8,128)(2,1)} %collective-permute-done.43.theirs_ref), custom_call_target="tpu_custom_call" | custom-call | flops 1000 | bytes 1000 | tf_op jit(solution)/shard_map/joined/pallas_call | solution.py:245
  516.4 7.9 %joined.3 = f32[2048,1536]{1,0:T(8,128)} custom-call(s32[1]{0:T(128)} %bitcast.53.core_ref, bf16[2048,768]{1,0:T(8,128)(2,1)S(1)} %copy-done.8, bf16[2048,768]{1,0:T(8,128)(2,1)} %collective-permute-done.42.theirs_ref), custom_call_target="tpu_custom_call" | custom-call | flops 1000 | bytes 1000 | tf_op jit(solution)/shard_map/joined/pallas_call | solution.py:245
  524.2 44.2 %all-reduce.7.cloned.1.call-done = (bf16[704,2048]{1,0:T(8,128)(2,1)}, bf16[8,176,176]{2,1,0:T(8,128)(2,1)}) async-done(((bf16[704,2048]{1,0:T(8,128)(2,1)}, bf16[8,176,176]{2,1,0:T(8,128)(2,1)}), (bf16[704,2048]{1,0:T(8,128)(2,1)}, bf16[8,176,176]{2,1,0:T(8,128)(2,1)})) %all-reduce.7.cloned.1.call-update) | async-done | bytes 3379216 | tf_op jit(solution)/shard_map/psum | solution.py:1001
  (315 shorter events, 175.7 us)
Async XLA Ops:
  7.2 165.8 %all-gather.4.cloned.1.call-start = ((), (), s32[]{:S(2)}) async-start(), calls=%async_computation | async-start | bytes 17301504 | tf_op jit(solution)/shard_map/all_gather | solution.py:925
  7.9 216.8 %all-gather.6.cloned.1.call-start = ((), (), s32[]{:S(2)}) async-start(), calls=%async_computation.1 | async-start | bytes 2621440 | tf_op jit(solution)/shard_map/all_gather | solution.py:945
  11.0 29.8 %collective-permute-start.1 = (bf16[128,2048]{1,0:T(8,128)(2,1)}, bf16[128,2048]{1,0:T(8,128)(2,1)S(1)}, u32[]{:S(2)}, u32[]{:S(2)}) collective-permute-start(bf16[128,2048]{1,0:T(8,128)(2,1)} %refs_0_), channel_id=1, source_target_pairs={{0,2},{1,3},{2,0},{3,1},{4,6},{5,7},{6,4},{7,5},{8,10},{9,11},{10,... | collective-permute-start | bytes 1572872 | tf_op jit(solution)/shard_map/ppermute | solution.py:39
  12.5 28.3 %collective-permute-start.2 = (bf16[128,2048]{1,0:T(8,128)(2,1)}, bf16[128,2048]{1,0:T(8,128)(2,1)S(1)}, u32[]{:S(2)}, u32[]{:S(2)}) collective-permute-start(bf16[128,2048]{1,0:T(8,128)(2,1)} %refs_0_), channel_id=1, source_target_pairs={{0,3},{1,2},{2,1},{3,0},{4,7},{5,6},{6,5},{7,4},{8,11},{9,10},{10,... | collective-permute-start | bytes 1572872 | tf_op jit(solution)/shard_map/ppermute | solution.py:39
  95.7 26.1 %collective-permute-start.13 = (bf16[128,2048]{1,0:T(8,128)(2,1)S(1)}, bf16[128,2048]{1,0:T(8,128)(2,1)S(1)}, u32[]{:S(2)}, u32[]{:S(2)}) collective-permute-start(bf16[128,2048]{1,0:T(8,128)(2,1)S(1)} %get-tuple-element.200), channel_id=1, source_target_pairs={{0,1},{1,0},{2,3},{3,2},{4,5},{5,4},{6,7},{7,6},{8,9},{9,8},{10,11... | collective-permute-start | bytes 1572872 | tf_op jit(solution)/shard_map/ppermute | solution.py:39
  96.4 44.4 %collective-permute-start.15 = (bf16[128,2048]{1,0:T(8,128)(2,1)S(1)}, bf16[128,2048]{1,0:T(8,128)(2,1)S(1)}, u32[]{:S(2)}, u32[]{:S(2)}) collective-permute-start(bf16[128,2048]{1,0:T(8,128)(2,1)S(1)} %get-tuple-element.201), channel_id=1, source_target_pairs={{0,3},{1,2},{2,1},{3,0},{4,7},{5,6},{6,5},{7,4},{8,11},{9,10},{10,... | collective-permute-start | bytes 1572872 | tf_op jit(solution)/shard_map/ppermute | solution.py:39
  98.7 42.2 %collective-permute-start.14 = (bf16[128,2048]{1,0:T(8,128)(2,1)S(1)}, bf16[128,2048]{1,0:T(8,128)(2,1)S(1)}, u32[]{:S(2)}, u32[]{:S(2)}) collective-permute-start(bf16[128,2048]{1,0:T(8,128)(2,1)S(1)} %get-tuple-element.202), channel_id=1, source_target_pairs={{0,2},{1,3},{2,0},{3,1},{4,6},{5,7},{6,4},{7,5},{8,10},{9,11},{10,... | collective-permute-start | bytes 1572872 | tf_op jit(solution)/shard_map/ppermute | solution.py:39
  145.9 181.5 %all-gather.8.cloned.1.call-start = ((), (), s32[]{:S(2)}) async-start(), calls=%async_computation.2 | async-start | bytes 10485760 | tf_op jit(solution)/shard_map/all_gather | solution.py:953
  146.2 25.1 %collective-permute-start.17 = (bf16[128,2048]{1,0:T(8,128)(2,1)}, bf16[128,2048]{1,0:T(8,128)(2,1)S(1)}, u32[]{:S(2)}, u32[]{:S(2)}) collective-permute-start(bf16[128,2048]{1,0:T(8,128)(2,1)} %copy-done.38), channel_id=1, source_target_pairs={{0,2},{1,3},{2,0},{3,1},{4,6},{5,7},{6,4},{7,5},{8,10},{9,11},{10,... | collective-permute-start | bytes 1572872 | tf_op jit(solution)/shard_map/ppermute | solution.py:39
  146.8 25.4 %collective-permute-start.18 = (bf16[128,2048]{1,0:T(8,128)(2,1)}, bf16[128,2048]{1,0:T(8,128)(2,1)S(1)}, u32[]{:S(2)}, u32[]{:S(2)}) collective-permute-start(bf16[128,2048]{1,0:T(8,128)(2,1)} %copy-done.38), channel_id=1, source_target_pairs={{0,3},{1,2},{2,1},{3,0},{4,7},{5,6},{6,5},{7,4},{8,11},{9,10},{10,... | collective-permute-start | bytes 1572872 | tf_op jit(solution)/shard_map/ppermute | solution.py:39
  224.8 252.6 %all-reduce.5.cloned.1.call-start = ((), (), s32[]{:S(2)}) async-start(), calls=%async_computation.3 | async-start | bytes 11534336 | tf_op jit(solution)/shard_map/psum | solution.py:968
  229.9 27.1 %collective-permute-start.23 = (bf16[128,2048]{1,0:T(8,128)(2,1)}, bf16[128,2048]{1,0:T(8,128)(2,1)}, u32[]{:S(2)}, u32[]{:S(2)}) collective-permute-start(bf16[128,2048]{1,0:T(8,128)(2,1)} %get-tuple-element.186), channel_id=1, source_target_pairs={{0,2},{1,3},{2,0},{3,1},{4,6},{5,7},{6,4},{7,5},{8,10},{9,11},{10,... | collective-permute-start | bytes 1572872 | tf_op jit(solution)/shard_map/ppermute | solution.py:39
  231.5 40.2 %collective-permute-start.24 = (bf16[128,2048]{1,0:T(8,128)(2,1)}, bf16[128,2048]{1,0:T(8,128)(2,1)S(1)}, u32[]{:S(2)}, u32[]{:S(2)}) collective-permute-start(bf16[128,2048]{1,0:T(8,128)(2,1)} %get-tuple-element.186), channel_id=1, source_target_pairs={{0,3},{1,2},{2,1},{3,0},{4,7},{5,6},{6,5},{7,4},{8,11},{9,10},{10,... | collective-permute-start | bytes 1572872 | tf_op jit(solution)/shard_map/ppermute | solution.py:39
  327.4 42.6 %collective-permute-start.30 = (bf16[2048,2048]{1,0:T(8,128)(2,1)}, bf16[2048,2048]{1,0:T(8,128)(2,1)}, u32[]{:S(2)}, u32[]{:S(2)}) collective-permute-start(bf16[2048,2048]{1,0:T(8,128)(2,1)} %all-gather.8.cloned.1.call-done), channel_id=1, source_target_pairs={{0,4},{4,0},{8,12},{12,8},{16,20},{20,16},{24,28},{28,24},{1,5},{5... | collective-permute-start | bytes 25165832 | tf_op jit(solution)/shard_map/ppermute | solution.py:39
  331.5 25.4 %collective-permute-start.33 = (bf16[128,2048]{1,0:T(8,128)(2,1)}, bf16[128,2048]{1,0:T(8,128)(2,1)}, u32[]{:S(2)}, u32[]{:S(2)}) collective-permute-start(bf16[128,2048]{1,0:T(8,128)(2,1)} %get-tuple-element.195), channel_id=1, source_target_pairs={{0,3},{1,2},{2,1},{3,0},{4,7},{5,6},{6,5},{7,4},{8,11},{9,10},{10,... | collective-permute-start | bytes 1572872 | tf_op jit(solution)/shard_map/ppermute | solution.py:39
  332.9 25.3 %collective-permute-start.32 = (bf16[128,2048]{1,0:T(8,128)(2,1)}, bf16[128,2048]{1,0:T(8,128)(2,1)}, u32[]{:S(2)}, u32[]{:S(2)}) collective-permute-start(bf16[128,2048]{1,0:T(8,128)(2,1)} %get-tuple-element.196), channel_id=1, source_target_pairs={{0,2},{1,3},{2,0},{3,1},{4,6},{5,7},{6,4},{7,5},{8,10},{9,11},{10,... | collective-permute-start | bytes 1572872 | tf_op jit(solution)/shard_map/ppermute | solution.py:39
  337.4 231.0 %all-reduce.7.cloned.1.call-start = ((), (), s32[]{:S(2)}) async-start(), calls=%async_computation.4 | async-start | bytes 7208960 | tf_op jit(solution)/shard_map/psum | solution.py:1001
  370.1 105.7 %collective-permute-start.34 = (bf16[128,2048]{1,0:T(8,128)(2,1)S(1)}, bf16[128,2048]{1,0:T(8,128)(2,1)S(1)}, u32[]{:S(2)}, u32[]{:S(2)}) collective-permute-start(bf16[128,2048]{1,0:T(8,128)(2,1)S(1)} %get-tuple-element.191), channel_id=1, source_target_pairs={{0,1},{1,0},{2,3},{3,2},{4,5},{5,4},{6,7},{7,6},{8,9},{9,8},{10,11... | collective-permute-start | bytes 1572872 | tf_op jit(solution)/shard_map/ppermute | solution.py:39
  370.8 105.0 %collective-permute-start.36 = (bf16[128,2048]{1,0:T(8,128)(2,1)S(1)}, bf16[128,2048]{1,0:T(8,128)(2,1)S(1)}, u32[]{:S(2)}, u32[]{:S(2)}) collective-permute-start(bf16[128,2048]{1,0:T(8,128)(2,1)S(1)} %get-tuple-element.192), channel_id=1, source_target_pairs={{0,3},{1,2},{2,1},{3,0},{4,7},{5,6},{6,5},{7,4},{8,11},{9,10},{10,... | collective-permute-start | bytes 1572872 | tf_op jit(solution)/shard_map/ppermute | solution.py:39
  372.2 103.6 %collective-permute-start.35 = (bf16[128,2048]{1,0:T(8,128)(2,1)S(1)}, bf16[128,2048]{1,0:T(8,128)(2,1)}, u32[]{:S(2)}, u32[]{:S(2)}) collective-permute-start(bf16[128,2048]{1,0:T(8,128)(2,1)S(1)} %get-tuple-element.193), channel_id=1, source_target_pairs={{0,2},{1,3},{2,0},{3,1},{4,6},{5,7},{6,4},{7,5},{8,10},{9,11},{10,... | collective-permute-start | bytes 1572872 | tf_op jit(solution)/shard_map/ppermute | solution.py:39
  379.3 98.7 %collective-permute-start.47 = (f32[8,704]{1,0:T(8,128)S(1)}, f32[8,704]{1,0:T(8,128)S(1)}, u32[]{:S(2)}, u32[]{:S(2)}) collective-permute-start(f32[8,704]{1,0:T(8,128)S(1)} %add.235), channel_id=1, source_target_pairs={{0,16},{4,20},{8,24},{12,28},{16,0},{20,4},{24,8},{28,12},{1,17},{... | collective-permute-start | bytes 67592 | tf_op jit(solution)/shard_map/ppermute | solution.py:39
  477.4 39.0 %collective-permute-start.42 = (bf16[2048,768]{1,0:T(8,128)(2,1)}, bf16[2048,768]{1,0:T(8,128)(2,1)}, u32[]{:S(2)}, u32[]{:S(2)}) collective-permute-start(bf16[2048,768]{1,0:T(8,128)(2,1)} %get-tuple-element.158.mine_ref), channel_id=1, source_target_pairs={{0,4},{4,0},{8,12},{12,8},{16,20},{20,16},{24,28},{28,24},{1,5},{5... | collective-permute-start | bytes 9437192 | tf_op jit(solution)/shard_map/ppermute | solution.py:39
  477.5 30.9 %collective-permute-start.43 = (bf16[2048,768]{1,0:T(8,128)(2,1)}, bf16[2048,768]{1,0:T(8,128)(2,1)}, u32[]{:S(2)}, u32[]{:S(2)}) collective-permute-start(bf16[2048,768]{1,0:T(8,128)(2,1)} %get-tuple-element.159.mine_ref), channel_id=1, source_target_pairs={{0,4},{4,0},{8,12},{12,8},{16,20},{20,16},{24,28},{28,24},{1,5},{5... | collective-permute-start | bytes 9437192 | tf_op jit(solution)/shard_map/ppermute | solution.py:39
  478.0 24.0 %collective-permute-start.44 = (bf16[768,2048]{1,0:T(8,128)(2,1)}, bf16[768,2048]{1,0:T(8,128)(2,1)}, u32[]{:S(2)}, u32[]{:S(2)}) collective-permute-start(bf16[768,2048]{1,0:T(8,128)(2,1)} %get-tuple-element.160.mine_ref), channel_id=1, source_target_pairs={{0,4},{4,0},{8,12},{12,8},{16,20},{20,16},{24,28},{28,24},{1,5},{5... | collective-permute-start | bytes 9437192 | tf_op jit(solution)/shard_map/ppermute | solution.py:39
  (75 other events, 849.5 us)
Sparse Core Ops, SparseCore 0:
  10.9 147.7 all-gather.3
  160.8 44.0 all-gather.5
  224.9 102.4 all-gather.7
  337.5 127.8 all-reduce.4
  484.3 84.0 all-reduce.6

commit v3 on v2

--- a/solution.py
+++ b/solution.py
@@ -47,6 +47,22 @@
         block = rows if r == 0 else swap(rows, "tp", r)
         whole = lax.dynamic_update_index_in_dim(whole, block, place ^ r, 0)
     return whole
+
+
+def spread(rows):
+    count = lax.axis_size("tp")
+    if count != 4:
+        whole = jnp.stack([rows] + [swap(rows, "tp", r) for r in range(1, count)])
+        return lambda *after: tied(whole, *after)
+    half = rows.shape[0] // 2
+    sides = swap(rows, "tp", 1), swap(rows, "tp", 2)
+
+    def finish(*after):
+        one, two, *after = tied(*sides, *after)
+        far = jnp.concatenate([swap(two[:half], "tp", 1), swap(one[half:], "tp", 2)])
+        return (jnp.stack([rows, one, two, far]), *after)
+
+    return finish
 
 
 def scatter_rows(blocks):
@@ -108,9 +124,8 @@
     return act * up_pre, hidden_grad * up_pre * slope, hidden_grad * act
 
 
-def dense_weight_grads(mine, theirs, cot_all, gate_proj, up_proj, down_proj, places):
+def dense_weight_grads(mine, theirs, cot_all, gate_proj, up_proj, down_proj, places, half, base):
     tp_size, chips, block, model = mine.shape
-    half = gate_proj.shape[1] // 2
     cot_all = cot_all.reshape(chips, 2, tp_size, block, model)
     part = math.gcd(chips, 4)
     length = part * block
@@ -169,7 +184,7 @@
     def cot_index(i, c):
         i = jnp.minimum(i, steps - 1)
         n = i % per_core
-        return n % groups, c[0] ^ (i // per_core), n // groups, 0, 0
+        return n % groups, c[0] ^ (i // per_core), c[1] ^ (n // groups), 0, 0
 
     def rows_index(first):
         def index(i, c):
@@ -187,9 +202,9 @@
                 rows_index(0),
                 rows_index(per_core),
                 pl.BlockSpec((part, 1, 1, block, model), cot_index),
-                pl.BlockSpec((model, half), lambda i, c: (0, c[0]), pipeline_mode=once),
-                pl.BlockSpec((model, half), lambda i, c: (0, c[0]), pipeline_mode=once),
-                pl.BlockSpec((half, model), lambda i, c: (c[0], 0), pipeline_mode=once),
+                pl.BlockSpec((model, half), lambda i, c: (0, base + c[0]), pipeline_mode=once),
+                pl.BlockSpec((model, half), lambda i, c: (0, base + c[0]), pipeline_mode=once),
+                pl.BlockSpec((half, model), lambda i, c: (base + c[0], 0), pipeline_mode=once),
             ],
             out_specs=[
                 pl.BlockSpec((model // outs, half), out_index),
@@ -217,42 +232,48 @@
     )(places, mine, theirs, cot_all, gate_proj, up_proj, down_proj)
 
 
-def joined(mine, theirs, core, axis):
-    rows, cols = mine.shape
-    block = math.gcd(rows, 256)
-    steps = rows // block
-
-    def kernel(core_ref, mine_ref, theirs_ref, out_ref):
+def joined(big, small, core, axis):
+    sizes = [pair[0].shape[axis] for pair in (big, small)]
+    total = 2 * sum(sizes)
+    other = big[0].shape[1 - axis]
+    block = math.gcd(other, 256)
+
+    def kernel(core_ref, *refs):
+        out_ref = refs[-1]
         for low in range(2):
 
             @pl.when(core_ref[0] == low)
             def _(low=low):
-                pair = (mine_ref, theirs_ref) if low == 0 else (theirs_ref, mine_ref)
-                if axis == 1:
-                    out_ref[:, :cols] = pair[0][...].astype(f32)
-                    out_ref[:, cols:] = pair[1][...].astype(f32)
-                else:
-                    out_ref[0] = pair[0][...].astype(f32)
-                    out_ref[1] = pair[1][...].astype(f32)
-
-    half = pl.BlockSpec((block, cols), lambda i, c: (i, 0))
+                first = 0
+                for n, size in enumerate(sizes):
+                    for half in range(2):
+                        source = refs[2 * n + (half ^ low)]
+                        at = slice(first, first + size)
+                        if axis == 1:
+                            out_ref[:, at] = source[...].astype(f32)
+                        else:
+                            out_ref[at, :] = source[...].astype(f32)
+                        first += size
+
     if axis == 1:
-        out_spec = pl.BlockSpec((block, 2 * cols), lambda i, c: (i, 0))
-        out_shape = jax.ShapeDtypeStruct((rows, 2 * cols), f32)
+        spec = lambda size: pl.BlockSpec((block, size), lambda i, c: (i, 0))
+        out_shape = (other, total)
     else:
-        out_spec = pl.BlockSpec((2, block, cols), lambda i, c: (0, i, 0))
-        out_shape = jax.ShapeDtypeStruct((2, rows, cols), f32)
-    out = pl.pallas_call(
+        spec = lambda size: pl.BlockSpec((size, block), lambda i, c: (0, i))
+        out_shape = (total, other)
+    return pl.pallas_call(
         kernel,
         grid_spec=pltpu.PrefetchScalarGridSpec(
-            num_scalar_prefetch=1, grid=(steps,), in_specs=[half, half], out_specs=out_spec
+            num_scalar_prefetch=1,
+            grid=(other // block,),
+            in_specs=[spec(sizes[0])] * 2 + [spec(sizes[1])] * 2,
+            out_specs=spec(total),
         ),
-        out_shape=out_shape,
+        out_shape=jax.ShapeDtypeStruct(out_shape, f32),
         compiler_params=pltpu.CompilerParams(vmem_limit_bytes=VMEM_LIMIT),
         cost_estimate=pl.CostEstimate(flops=1000, bytes_accessed=1000, transcendentals=0),
         name="joined",
-    )(core, mine, theirs)
-    return out if axis == 1 else out.reshape(2 * rows, cols)
+    )(core, *big, *small)
 
 
 def dense_rows(rows, cot_all, group_place, gate_proj, up_proj, down_proj):
@@ -949,14 +970,13 @@
     )
     normed_two_grad = scatter_rows(normed_two_part.reshape(tp_size, length, model))
     dense_part = product(hidden, down_proj).astype(bf16)
-    normed_two_grad, dense_part, rows_z = tied(normed_two_grad, dense_part, rows_z)
-    rows_mine = lax.all_gather(rows_z, "tp", axis=0, tiled=True)
+    normed_two_grad, dense_part = tied(normed_two_grad, dense_part)
     mid_from_norm, dense_gain_part = norm_back(normed_two_grad, xhat_dense, dense_scale, mid_root)
     mid_grad = cotangent.astype(f32) + mid_from_norm
     mid_blocks = gather_rows(mid_grad.astype(bf16))
-    mid_blocks, dense_part = tied(mid_blocks, dense_part)
-
-    dense_out = scatter_rows(dense_part.reshape(tp_size, length, model))
+    mid_blocks, dense_part, rows_z = tied(mid_blocks, dense_part, rows_z)
+    rows_spread = spread(rows_z)
+
     direct, branch_pre_grad, reach = mix_back(mid_blocks, out_proj, branch_pre, state, keep_prefix)
     branch_pre_grad = branch_pre_grad.reshape(group, width)
     mid_rows = mid_blocks.reshape(group, model)
@@ -983,7 +1003,7 @@
         rate_dense,
         input_dense,
     )
-    rim_grad, rows_mine = tied(rim_grad, rows_mine)
+    rows_mine, rim_grad = rows_spread(rim_grad)
     fixed = tail + from_neighbour(rim_grad, 1)
     low_rows = conv_low.reshape(group, width)
     rate_w = diagonal_blocks(product_left_t(low_rows, rate_low.reshape(group, width)), blocks_n)
@@ -995,26 +1015,10 @@
     block_full = jnp.concatenate([rate_w, input_w]).astype(bf16)
     normed_part = (product(inner_grad, in_t) + product(branch_pre_grad, branch_t)).astype(bf16)
     rows_theirs = swap(rows_mine, "seq", 1)
-    normed_part, in_full, block_full, rows_theirs, dense_out = tied(
-        normed_part, in_full, block_full, rows_theirs, dense_out
-    )
+    normed_part, in_full, block_full, sums = tied(normed_part, in_full, block_full, sums)
     in_sum, block_sum = lax.psum((in_full, block_full), "seq", axis_index_groups=[list(range(seq_size))[::-1]])
     normed_grad = scatter_rows(normed_part.reshape(tp_size, length, model))
-
-    core_no = core.astype(jnp.int32)[None]
-    blocked = lambda rows: rows.reshape(tp_size, chips, length, model)
-    gate_w, up_w, down_w = dense_weight_grads(
-        blocked(rows_mine), blocked(rows_theirs), cot_all, gate_proj, up_proj, down_proj, core_no
-    )
-    gate_w, up_w, down_w, out_sum, branch_sum, normed_grad = tied(
-        gate_w, up_w, down_w, out_sum, branch_sum, normed_grad
-    )
-    gate_sum = joined(gate_w, swap(gate_w, "seq", 1), core_no, 1)
-    up_sum = joined(up_w, swap(up_w, "seq", 1), core_no, 1)
-    down_sum = joined(down_w, swap(down_w, "seq", 1), core_no, 0)
-    gate_sum, up_sum, down_sum, in_sum, block_sum = tied(gate_sum, up_sum, down_sum, in_sum, block_sum)
-
-    output = (mid + dense_out).astype(bf16)
+    sums = sum_bits(sums, "seq")
     own = tokens.astype(f32)
     own_root = rms(own)
     rows_grad, mixer_gain_part = norm_back(normed_grad, own * own_root, mixer_scale, own_root)
@@ -1022,8 +1026,26 @@
     gain_parts = sum_bits(jnp.stack([mixer_gain_part, dense_gain_part]), "tp")
     gain_own = lax.dynamic_slice_in_dim(gain_parts, tp_place * gain_share, gain_share, 1)
     gain_sum = sum_bits(gain_own, "seq")
-    sums = sum_bits(sums, "seq")
     decay_sum = 8.0 * jax.nn.sigmoid(-decay_param) * sums[2]
+    rows_mine, rows_theirs, tokens_grad, gain_sum, sums, dense_part = tied(
+        rows_mine, rows_theirs, tokens_grad, gain_sum, sums, dense_part
+    )
+    dense_out = scatter_rows(dense_part.reshape(tp_size, length, model))
+
+    places = jnp.stack([core, tp_place]).astype(jnp.int32)
+    blocked = lambda rows: rows.reshape(tp_size, chips, length, model)
+    hidden_n = gate_proj.shape[1]
+    weights = (cot_all, gate_proj, up_proj, down_proj, places)
+    big = dense_weight_grads(blocked(rows_mine), blocked(rows_theirs), *weights, hidden_n // 3, 0)
+    *big, out_sum, branch_sum, rows_mine, rows_theirs = tied(*big, out_sum, branch_sum, rows_mine, rows_theirs)
+    big = [(part, swap(part, "seq", 1)) for part in big]
+    small = dense_weight_grads(blocked(rows_mine), blocked(rows_theirs), *weights, hidden_n // 6, 4)
+    *small, in_sum, block_sum = tied(*small, in_sum, block_sum)
+    small = [(part, swap(part, "seq", 1)) for part in small]
+    gate_sum = joined(big[0], small[0], places, 1)
+    up_sum = joined(big[1], small[1], places, 1)
+    down_sum = joined(big[2], small[2], places, 0)
+    output = (mid + dense_out).astype(bf16)
     rate_sum, input_sum = block_sum[:blocks_n].astype(f32), block_sum[blocks_n:].astype(f32)
     return (
         output,

time: 589 us -> 636 us (1.080)
  Pallas kernels: 201 us -> 224 us
  waiting for transfers between devices: 202 us -> 224 us
    ppermute x42 -> x49, waiting for transfers between devices: 147 us -> 177 us  [swap(): return lax.ppermute(value, axis, [(i, i ^ bit) for i in range(count)])]
    pallas_call x1 -> x2, Pallas kernels: 94.1 us -> 114 us  [dense_weight_grads(): pl.pallas_call(kernel, grid_spec=pltpu.PrefetchScalarGridSpec(num_scalar_...]
    ppermute x42 -> x49, starting transfers between devices: 44.5 us -> 59.9 us  [swap(): return lax.ppermute(value, axis, [(i, i ^ bit) for i in range(count)])]
    ppermute x3, starting transfers between devices: 13.6 us -> 2.55 us  [from_neighbour(): across = lax.ppermute(value, 'seq', pairs)]
    all_gather x1 -> x0, waiting for transfers between devices: 8.91 us -> none  [shards(): rows_mine = lax.all_gather(rows_z, 'tp', axis=0, tiled=True)]
    ppermute x3, starting transfers between devices: 9.3 us -> 1.88 us  [from_neighbour(): inside = lax.ppermute(value, 'seq', [(i, i ^ 1) for i in range(count)])]
    another operation x0 -> x3, other arithmetic: none -> 7.24 us  [the longest x2 6.58 us: finish(): return (jnp.stack([rows, one, two, far]), *after)]
    unnamed x103 -> x91, local copies, waits for them, and re-layouts: 13.8 us -> 9.87 us
  transfers between devices with their start and end apart: 53 -> 59, of which waited for: 27 -> 29; matrix products, arithmetic and copies ran while one was open for 13% -> 14% of each run, Pallas kernels for 35% -> 34%
where the time goes in v3:
time: 636 us; the launch traced here: 628 us
  waiting for transfers between devices  224 us (35%)
  Pallas kernels  224 us (35%)
  starting transfers between devices  65 us (10%)
  other arithmetic  39.4 us (6%)
  local copies, waits for them, and re-layouts  35.8 us (6%)
  matrix products  25.2 us (4%)
  between operations  14.9 us (2%)
    ppermute x49, waiting for transfers between devices, swap(): return lax.ppermute(value, axis, [(i, i ^ bit) for i in range(count)])  177 us
    pallas_call x2, Pallas kernels, dense_weight_grads(): pl.pallas_call(kernel, grid_spec=pltpu.PrefetchScalarGridSpec(num_scalar_...  114 us
    ppermute x49, starting transfers between devices, swap(): return lax.ppermute(value, axis, [(i, i ^ bit) for i in range(count)])  59.9 us
    psum x1, waiting for transfers between devices, shards(): lax.psum((in_full, block_full), 'seq', axis_index_groups=[list(range(seq_...  41.6 us
    pallas_call x3, Pallas kernels, joined(): pl.pallas_call(kernel, grid_spec=pltpu.PrefetchScalarGridSpec(num_scalar_...  25.9 us
    pallas_call x1, Pallas kernels, dense_rows(): pl.pallas_call(kernel, grid_spec=pltpu.PrefetchScalarGridSpec(num_scalar_...  24.9 us
    pallas_call x1, Pallas kernels, recur_backward(): pl.pallas_call(backward_kernel, grid_spec=pltpu.PrefetchScalarGridSpec(nu...  19.3 us
    pallas_call x1, Pallas kernels, recur_forward(): pl.pallas_call(forward_kernel, grid_spec=pltpu.PrefetchScalarGridSpec(num...  15.2 us
  transfers between devices with their start and end apart: 59, of which 29 were waited for; matrix products, arithmetic and copies ran while one was open for 14% of the time, Pallas kernels for 34%

profile of v3, /device:TPU:0, one launch (start us, length us, event | category | flops | bytes accessed | tf_op | source)
XLA Modules:
  0.0 628.4 jit_solution(1179220835878400603)
XLA Ops:
  13.9 10.3 %collective-permute-done.refs_1_ = bf16[128,2048]{1,0:T(8,128)(2,1)S(1)} collective-permute-done((bf16[128,2048]{1,0:T(8,128)(2,1)}, bf16[128,2048]{1,0:T(8,128)(2,1)S(1)}, u32[]{:S(2)}, u32[]{:S(2)}) %collective-permute-start) | collective-permute-done | bytes 524320 | tf_op jit(solution)/shard_map/ppermute | solution.py:39
  41.9 7.0 %norm_project.1 = (bf16[512,2048]{1,0:T(8,128)(2,1)}, f32[4,128,704]{2,1,0:T(8,128)S(1)}) custom-call(s32[1]{0:T(128)} %bitcast.place_ref, bf16[128,2048]{1,0:T(8,128)(2,1)S(1)} %copy-done.7, bf16[128,2048]{1,0:T(8,128)(2,1)S(1)} %collective-permute-done.refs_1_, bf16[128,2048]{1,0:T(8,128)(2,1)S(1)} %collective-permute-done.1.refs_2_, ...), custom_call_target="tpu_custom_call" | custom-call | tf_op jit(solution)/shard_map/norm_project/pallas_call | solution.py:730
  51.2 15.2 %recur_forward.1 = (f32[4,128,704]{2,1,0:T(8,128)}, bf16[4,128,704]{2,1,0:T(8,128)(2,1)S(1)}, f32[4,128,704]{2,1,0:T(8,128)}, f32[4,128,704]{2,1,0:T(8,128)}, f3...) custom-call(f32[4,128,704]{2,1,0:T(8,128)} %copy-done, ...), custom_call_target="tpu_custom_call" | custom-call | tf_op jit(solution)/shard_map/recur_forward/pallas_call | solution.py:755
  66.4 6.4 %collective-permute-start.10 = (f32[2,704]{1,0:T(2,128)S(1)}, f32[2,704]{1,0:T(2,128)S(1)}, u32[]{:S(2)}, u32[]{:S(2)}) collective-permute-start(f32[2,704]{1,0:T(2,128)S(1)} %pad_maximum_fusion.4), channel_id=1, source_target_pairs={{0,4},{4,0},{8,12},{12,8},{16,20},{20,16},{24,28},{28,24},{1,5},{5... | collective-permute-start | bytes 16904 | tf_op jit(solution)/shard_map/ppermute | solution.py:39
  87.1 6.4 %mix_out.1 = (f32[4,128,704]{2,1,0:T(8,128)S(1)}, bf16[4,128,704]{2,1,0:T(8,128)(2,1)S(1)}, bf16[4,128,2048]{2,1,0:T(8,128)(2,1)}) custom-call(f32[4,128,704]{2,1,0:T(8,128)S(1)} %copy-done.11, f32[4,128,704]{2,1,0:T(8,128)} %get-tuple-element.123.keep_ref, f32[4,128,704]{2,1,0:T(8,128)} %bitcast.165, f32[1,704]{1,0:T(1,128)S(1)} %get-tuple-element.204.in_ref, ...), custom_call_target="tpu_custom_call" | custom-call | tf_op jit(solution)/shard_map/mix_out/pallas_call | solution.py:381
  99.1 22.5 %collective-permute-done.13 = bf16[128,2048]{1,0:T(8,128)(2,1)S(1)} collective-permute-done((bf16[128,2048]{1,0:T(8,128)(2,1)S(1)}, bf16[128,2048]{1,0:T(8,128)(2,1)S(1)}, u32[]{:S(2)}, u32[]{:S(2)}) %collective-permute-start.13) | collective-permute-done | bytes 524320 | tf_op jit(solution)/shard_map/ppermute | solution.py:39
  123.1 17.8 %collective-permute-done.15 = bf16[128,2048]{1,0:T(8,128)(2,1)S(1)} collective-permute-done((bf16[128,2048]{1,0:T(8,128)(2,1)S(1)}, bf16[128,2048]{1,0:T(8,128)(2,1)S(1)}, u32[]{:S(2)}, u32[]{:S(2)}) %collective-permute-start.15) | collective-permute-done | bytes 524320 | tf_op jit(solution)/shard_map/ppermute | solution.py:39
  149.1 10.9 %collective-permute-done.16 = bf16[128,2048]{1,0:T(8,128)(2,1)} collective-permute-done((bf16[128,2048]{1,0:T(8,128)(2,1)S(1)}, bf16[128,2048]{1,0:T(8,128)(2,1)}, u32[]{:S(2)}, u32[]{:S(2)}) %collective-permute-start.16) | collective-permute-done | bytes 524320 | tf_op jit(solution)/shard_map/ppermute | solution.py:39
  171.9 24.9 %dense_rows.1 = (bf16[512,1536]{1,0:T(8,128)(2,1)S(1)}, bf16[512,2048]{1,0:T(8,128)(2,1)S(1)}) custom-call(s32[1]{0:T(128)} %bitcast.18.place_ref, bf16[512,2048]{1,0:T(8,128)(2,1)} %bitcast.23.x_ref, bf16[4096,2048]{1,0:T(8,128)(2,1)} %all-gather.3.cloned.1.call-done.c_ref, bf16[2048,1536]{1,0:T(8,128)(2,1)} %gate_ref.5, bf16[2048,1536]{1,0:T(8,128)(2,1)} %up_ref.5, ...), custom_call_target="tpu_custom_call" | custom-call | tf_op jit(solution)/shard_map/dense_rows/pallas_call | solution.py:312
  206.5 6.6 %collective-permute-done.19 = bf16[128,2048]{1,0:T(8,128)(2,1)S(1)} collective-permute-done((bf16[128,2048]{1,0:T(8,128)(2,1)S(1)}, bf16[128,2048]{1,0:T(8,128)(2,1)S(1)}, u32[]{:S(2)}, u32[]{:S(2)}) %collective-permute-start.19) | collective-permute-done | bytes 524320 | tf_op jit(solution)/shard_map/ppermute | solution.py:39
  213.1 8.0 %collective-permute-done.20 = bf16[128,2048]{1,0:T(8,128)(2,1)S(1)} collective-permute-done((bf16[128,2048]{1,0:T(8,128)(2,1)S(1)}, bf16[128,2048]{1,0:T(8,128)(2,1)S(1)}, u32[]{:S(2)}, u32[]{:S(2)}) %collective-permute-start.20) | collective-permute-done | bytes 524320 | tf_op jit(solution)/shard_map/ppermute | solution.py:39
  228.2 11.7 %collective-permute-done.22 = bf16[128,2048]{1,0:T(8,128)(2,1)} collective-permute-done((bf16[128,2048]{1,0:T(8,128)(2,1)}, bf16[128,2048]{1,0:T(8,128)(2,1)}, u32[]{:S(2)}, u32[]{:S(2)}) %collective-permute-start.22) | collective-permute-done | bytes 524320 | tf_op jit(solution)/shard_map/ppermute | solution.py:39
  253.4 8.0 %mix_back.1 = (f32[4,128,704]{2,1,0:T(8,128)S(1)}, bf16[4,128,704]{2,1,0:T(8,128)(2,1)S(1)}, f32[1,704]{1,0:T(1,128)S(1)}) custom-call(bf16[4,128,2048]{2,1,0:T(8,128)(2,1)} %bitcast_dynamic-update-slice_fusion.mid_ref, bf16[704,2048]{1,0:T(8,128)(2,1)} %out_ref.3, f32[4,128,704]{2,1,0:T(8,128)S(1)} %bitcast.166, f32[4,128,704]{2,1,0:T(8,128)} %copy-done.1, ...), custom_call_target="tpu_custom_call" | custom-call | tf_op jit(solution)/shard_map/mix_back/pallas_call | solution.py:433
  278.5 19.3 %recur_backward.1 = (bf16[4,128,704]{2,1,0:T(8,128)(2,1)S(1)}, bf16[4,128,704]{2,1,0:T(8,128)(2,1)S(1)}, bf16[4,128,704]{2,1,0:T(8,128)(2,1)S(1)}, f32[8,704]{1,...) custom-call(f32[4,128,704]{2,1,0:T(8,128)} %copy-done.10, f32[4,128,704]{2,1,0:T(8,128)} %copy-done.1, ...), custom_call_target="tpu_custom_call" | custom-call | flops 1000 | bytes 1000 | tf_op jit(solution)/shard_map/recur_backward/pallas_call | solution.py:804
  302.1 21.8 %collective-permute-done.30 = bf16[256,2048]{1,0:T(8,128)(2,1)S(1)} collective-permute-done((bf16[256,2048]{1,0:T(8,128)(2,1)S(1)}, bf16[256,2048]{1,0:T(8,128)(2,1)S(1)}, u32[]{:S(2)}, u32[]{:S(2)}) %collective-permute-start.30) | collective-permute-done | bytes 1048608 | tf_op jit(solution)/shard_map/ppermute | solution.py:39
  357.9 11.3 %collective-permute-done.35 = bf16[128,2048]{1,0:T(8,128)(2,1)S(1)} collective-permute-done((bf16[128,2048]{1,0:T(8,128)(2,1)S(1)}, bf16[128,2048]{1,0:T(8,128)(2,1)S(1)}, u32[]{:S(2)}, u32[]{:S(2)}) %collective-permute-start.35) | collective-permute-done | bytes 524320 | tf_op jit(solution)/shard_map/ppermute | solution.py:39
  369.2 12.5 %collective-permute-done.36 = bf16[128,2048]{1,0:T(8,128)(2,1)S(1)} collective-permute-done((bf16[128,2048]{1,0:T(8,128)(2,1)S(1)}, bf16[128,2048]{1,0:T(8,128)(2,1)S(1)}, u32[]{:S(2)}, u32[]{:S(2)}) %collective-permute-start.36) | collective-permute-done | bytes 524320 | tf_op jit(solution)/shard_map/ppermute | solution.py:39
  405.1 66.7 %dense_weight_grads.2 = (bf16[2048,512]{1,0:T(8,128)(2,1)}, bf16[2048,512]{1,0:T(8,128)(2,1)}, bf16[512,2048]{1,0:T(8,128)(2,1)}) custom-call(s32[2]{0:T(128)} %pad_add_fusion.2.core_ref, bf16[4,4,128,2048]{3,2,1,0:T(8,128)(2,1)} %bitcast.66.mine_ref, bf16[4,4,128,2048]{3,2,1,0:T(8,128)(2,1)} %bitcast.67.theirs_ref, bf16[4,2,4,128,2048]{4,3,2,1,0:T(8,128)(2,1)} %bitcast.175, ...), custom_call_target="tpu_custom_call" | custom-call | flops 1000 | bytes 1000 | tf_op jit(solution)/shard_map/dense_weight_grads/pallas_call | solution.py:196
  471.8 46.8 %dense_weight_grads.3 = (bf16[2048,256]{1,0:T(8,128)(2,1)}, bf16[2048,256]{1,0:T(8,128)(2,1)}, bf16[256,2048]{1,0:T(8,128)(2,1)}) custom-call(s32[2]{0:T(128)} %pad_add_fusion.2.core_ref, bf16[4,4,128,2048]{3,2,1,0:T(8,128)(2,1)} %bitcast.69.mine_ref, bf16[4,4,128,2048]{3,2,1,0:T(8,128)(2,1)} %bitcast.70.theirs_ref, bf16[4,2,4,128,2048]{4,3,2,1,0:T(8,128)(2,1)} %bitcast.176, ...), custom_call_target="tpu_custom_call" | custom-call | flops 1000 | bytes 1000 | tf_op jit(solution)/shard_map/dense_weight_grads/pallas_call | solution.py:196
  518.7 41.6 %all-reduce.7.cloned.1.call-done = (bf16[704,2048]{1,0:T(8,128)(2,1)}, bf16[8,176,176]{2,1,0:T(8,128)(2,1)}) async-done(((bf16[704,2048]{1,0:T(8,128)(2,1)}, bf16[8,176,176]{2,1,0:T(8,128)(2,1)}), (bf16[704,2048]{1,0:T(8,128)(2,1)}, bf16[8,176,176]{2,1,0:T(8,128)(2,1)})) %all-reduce.7.cloned.1.call-update) | async-done | bytes 3379216 | tf_op jit(solution)/shard_map/psum | solution.py:1019
  580.8 8.8 %collective-permute-done.48 = bf16[128,2048]{1,0:T(8,128)(2,1)S(1)} collective-permute-done((bf16[128,2048]{1,0:T(8,128)(2,1)S(1)}, bf16[128,2048]{1,0:T(8,128)(2,1)S(1)}, u32[]{:S(2)}, u32[]{:S(2)}) %collective-permute-start.48) | collective-permute-done | bytes 524320 | tf_op jit(solution)/shard_map/ppermute | solution.py:39
  595.7 8.7 %joined.5 = f32[1536,2048]{1,0:T(8,128)} custom-call(s32[2]{0:T(128)S(1)} %copy-done.16, bf16[512,2048]{1,0:T(8,128)(2,1)} %get-tuple-element.189.refs_0_, bf16[512,2048]{1,0:T(8,128)(2,1)} %collective-permute-done.53.refs_1_, bf16[256,2048]{1,0:T(8,128)(2,1)S(1)} %copy-done.14, bf16[256,2048]{1,0:T(8,128)(2,1)S(1)} %collective-permute-done.54.refs_3_), custom_call_target="tpu_custom_call" | custom-call | flops 1000 | bytes 1000 | tf_op jit(solution)/shard_map/joined/pallas_call | solution.py:264
  604.4 8.6 %joined.4 = f32[2048,1536]{1,0:T(8,128)} custom-call(s32[2]{0:T(128)S(1)} %copy-done.16, bf16[2048,512]{1,0:T(8,128)(2,1)} %get-tuple-element.187.refs_0_, bf16[2048,512]{1,0:T(8,128)(2,1)} %collective-permute-done.51.refs_1_, bf16[2048,256]{1,0:T(8,128)(2,1)S(1)} %copy-done.13, bf16[2048,256]{1,0:T(8,128)(2,1)S(1)} %collective-permute-done.52.refs_3_), custom_call_target="tpu_custom_call" | custom-call | flops 1000 | bytes 1000 | tf_op jit(solution)/shard_map/joined/pallas_call | solution.py:264
  613.0 8.6 %joined.3 = f32[2048,1536]{1,0:T(8,128)} custom-call(s32[2]{0:T(128)S(1)} %copy-done.16, bf16[2048,512]{1,0:T(8,128)(2,1)} %get-tuple-element.185.refs_0_, bf16[2048,512]{1,0:T(8,128)(2,1)} %collective-permute-done.49.refs_1_, bf16[2048,256]{1,0:T(8,128)(2,1)S(1)} %copy-done.12, bf16[2048,256]{1,0:T(8,128)(2,1)S(1)} %collective-permute-done.50.refs_3_), custom_call_target="tpu_custom_call" | custom-call | flops 1000 | bytes 1000 | tf_op jit(solution)/shard_map/joined/pallas_call | solution.py:264
  (320 shorter events, 202.9 us)
Async XLA Ops:
  7.2 164.7 %all-gather.3.cloned.1.call-start = ((), (), s32[]{:S(2)}) async-start(), calls=%async_computation | async-start | bytes 17301504 | tf_op jit(solution)/shard_map/all_gather | solution.py:946
  7.9 242.4 %all-gather.5.cloned.1.call-start = ((), (), s32[]{:S(2)}) async-start(), calls=%async_computation.1 | async-start | bytes 2621440 | tf_op jit(solution)/shard_map/all_gather | solution.py:966
  11.0 26.8 %collective-permute-start.1 = (bf16[128,2048]{1,0:T(8,128)(2,1)}, bf16[128,2048]{1,0:T(8,128)(2,1)S(1)}, u32[]{:S(2)}, u32[]{:S(2)}) collective-permute-start(bf16[128,2048]{1,0:T(8,128)(2,1)} %refs_0_), channel_id=1, source_target_pairs={{0,2},{1,3},{2,0},{3,1},{4,6},{5,7},{6,4},{7,5},{8,10},{9,11},{10,... | collective-permute-start | bytes 1572872 | tf_op jit(solution)/shard_map/ppermute | solution.py:39
  12.5 26.9 %collective-permute-start.2 = (bf16[128,2048]{1,0:T(8,128)(2,1)}, bf16[128,2048]{1,0:T(8,128)(2,1)S(1)}, u32[]{:S(2)}, u32[]{:S(2)}) collective-permute-start(bf16[128,2048]{1,0:T(8,128)(2,1)} %refs_0_), channel_id=1, source_target_pairs={{0,3},{1,2},{2,1},{3,0},{4,7},{5,6},{6,5},{7,4},{8,11},{9,10},{10,... | collective-permute-start | bytes 1572872 | tf_op jit(solution)/shard_map/ppermute | solution.py:39
  95.5 26.1 %collective-permute-start.13 = (bf16[128,2048]{1,0:T(8,128)(2,1)S(1)}, bf16[128,2048]{1,0:T(8,128)(2,1)S(1)}, u32[]{:S(2)}, u32[]{:S(2)}) collective-permute-start(bf16[128,2048]{1,0:T(8,128)(2,1)S(1)} %get-tuple-element.220), channel_id=1, source_target_pairs={{0,1},{1,0},{2,3},{3,2},{4,5},{5,4},{6,7},{7,6},{8,9},{9,8},{10,11... | collective-permute-start | bytes 1572872 | tf_op jit(solution)/shard_map/ppermute | solution.py:39
  96.3 26.8 %collective-permute-start.14 = (bf16[128,2048]{1,0:T(8,128)(2,1)S(1)}, bf16[128,2048]{1,0:T(8,128)(2,1)S(1)}, u32[]{:S(2)}, u32[]{:S(2)}) collective-permute-start(bf16[128,2048]{1,0:T(8,128)(2,1)S(1)} %get-tuple-element.222), channel_id=1, source_target_pairs={{0,2},{1,3},{2,0},{3,1},{4,6},{5,7},{6,4},{7,5},{8,10},{9,11},{10,... | collective-permute-start | bytes 1572872 | tf_op jit(solution)/shard_map/ppermute | solution.py:39
  96.7 44.2 %collective-permute-start.15 = (bf16[128,2048]{1,0:T(8,128)(2,1)S(1)}, bf16[128,2048]{1,0:T(8,128)(2,1)S(1)}, u32[]{:S(2)}, u32[]{:S(2)}) collective-permute-start(bf16[128,2048]{1,0:T(8,128)(2,1)S(1)} %get-tuple-element.221), channel_id=1, source_target_pairs={{0,3},{1,2},{2,1},{3,0},{4,7},{5,6},{6,5},{7,4},{8,11},{9,10},{10,... | collective-permute-start | bytes 1572872 | tf_op jit(solution)/shard_map/ppermute | solution.py:39
  146.0 24.0 %collective-permute-start.18 = (bf16[128,2048]{1,0:T(8,128)(2,1)S(1)}, bf16[128,2048]{1,0:T(8,128)(2,1)}, u32[]{:S(2)}, u32[]{:S(2)}) collective-permute-start(bf16[128,2048]{1,0:T(8,128)(2,1)S(1)} %get-tuple-element.208), channel_id=1, source_target_pairs={{0,3},{1,2},{2,1},{3,0},{4,7},{5,6},{6,5},{7,4},{8,11},{9,10},{10,... | collective-permute-start | bytes 1572872 | tf_op jit(solution)/shard_map/ppermute | solution.py:39
  148.6 323.2 %all-reduce.5.cloned.1.call-start = ((), (), s32[]{:S(2)}) async-start(), calls=%async_computation.2 | async-start | bytes 11534336 | tf_op jit(solution)/shard_map/psum | solution.py:988
  250.3 47.5 %collective-permute-start.25 = (bf16[512,2048]{1,0:T(8,128)(2,1)}, bf16[512,2048]{1,0:T(8,128)(2,1)}, u32[]{:S(2)}, u32[]{:S(2)}) collective-permute-start(bf16[512,2048]{1,0:T(8,128)(2,1)} %all-gather.5.cloned.1.call-done), channel_id=1, source_target_pairs={{0,1},{1,0},{2,3},{3,2},{4,5},{5,4},{6,7},{7,6},{8,9},{9,8},{10,11... | collective-permute-start | bytes 6291464 | tf_op jit(solution)/shard_map/ppermute | solution.py:39
  250.9 46.9 %collective-permute-start.26 = (bf16[512,2048]{1,0:T(8,128)(2,1)}, bf16[512,2048]{1,0:T(8,128)(2,1)}, u32[]{:S(2)}, u32[]{:S(2)}) collective-permute-start(bf16[512,2048]{1,0:T(8,128)(2,1)} %all-gather.5.cloned.1.call-done), channel_id=1, source_target_pairs={{0,2},{1,3},{2,0},{3,1},{4,6},{5,7},{6,4},{7,5},{8,10},{9,11},{10,... | collective-permute-start | bytes 6291464 | tf_op jit(solution)/shard_map/ppermute | solution.py:39
  299.5 24.5 %collective-permute-start.30 = (bf16[256,2048]{1,0:T(8,128)(2,1)S(1)}, bf16[256,2048]{1,0:T(8,128)(2,1)S(1)}, u32[]{:S(2)}, u32[]{:S(2)}) collective-permute-start(bf16[256,2048]{1,0:T(8,128)(2,1)S(1)} %slice.257), channel_id=1, source_target_pairs={{0,1},{1,0},{2,3},{3,2},{4,5},{5,4},{6,7},{7,6},{8,9},{9,8},{10,11... | collective-permute-start | bytes 3145736 | tf_op jit(solution)/shard_map/ppermute | solution.py:39
  301.1 24.3 %collective-permute-start.31 = (bf16[256,2048]{1,0:T(8,128)(2,1)S(1)}, bf16[256,2048]{1,0:T(8,128)(2,1)S(1)}, u32[]{:S(2)}, u32[]{:S(2)}) collective-permute-start(bf16[256,2048]{1,0:T(8,128)(2,1)S(1)} %slice.258), channel_id=1, source_target_pairs={{0,2},{1,3},{2,0},{3,1},{4,6},{5,7},{6,4},{7,5},{8,10},{9,11},{10,... | collective-permute-start | bytes 3145736 | tf_op jit(solution)/shard_map/ppermute | solution.py:39
  332.0 71.8 %collective-permute-start.32 = (bf16[4,512,2048]{2,1,0:T(8,128)(2,1)}, bf16[4,512,2048]{2,1,0:T(8,128)(2,1)}, u32[]{:S(2)}, u32[]{:S(2)}) collective-permute-start(bf16[4,512,2048]{2,1,0:T(8,128)(2,1)} %pad_maximum_fusion), channel_id=1, source_target_pairs={{0,4},{4,0},{8,12},{12,8},{16,20},{20,16},{24,28},{28,24},{1,5},{5... | collective-permute-start | bytes 25165832 | tf_op jit(solution)/shard_map/ppermute | solution.py:39
  341.1 219.2 %all-reduce.7.cloned.1.call-start = ((), (), s32[]{:S(2)}) async-start(), calls=%async_computation.3 | async-start | bytes 7208960 | tf_op jit(solution)/shard_map/psum | solution.py:1019
  356.1 25.6 %collective-permute-start.36 = (bf16[128,2048]{1,0:T(8,128)(2,1)S(1)}, bf16[128,2048]{1,0:T(8,128)(2,1)S(1)}, u32[]{:S(2)}, u32[]{:S(2)}) collective-permute-start(bf16[128,2048]{1,0:T(8,128)(2,1)S(1)} %get-tuple-element.216), channel_id=1, source_target_pairs={{0,2},{1,3},{2,0},{3,1},{4,6},{5,7},{6,4},{7,5},{8,10},{9,11},{10,... | collective-permute-start | bytes 1572872 | tf_op jit(solution)/shard_map/ppermute | solution.py:39
  357.4 24.3 %collective-permute-start.37 = (bf16[128,2048]{1,0:T(8,128)(2,1)S(1)}, bf16[128,2048]{1,0:T(8,128)(2,1)S(1)}, u32[]{:S(2)}, u32[]{:S(2)}) collective-permute-start(bf16[128,2048]{1,0:T(8,128)(2,1)S(1)} %get-tuple-element.215), channel_id=1, source_target_pairs={{0,3},{1,2},{2,1},{3,0},{4,7},{5,6},{6,5},{7,4},{8,11},{9,10},{10,... | collective-permute-start | bytes 1572872 | tf_op jit(solution)/shard_map/ppermute | solution.py:39
  357.9 26.2 %collective-permute-start.43 = (f32[8,704]{1,0:T(8,128)S(1)}, f32[8,704]{1,0:T(8,128)S(1)}, u32[]{:S(2)}, u32[]{:S(2)}) collective-permute-start(f32[8,704]{1,0:T(8,128)S(1)} %get-tuple-element.161), channel_id=1, source_target_pairs={{0,4},{4,0},{8,12},{12,8},{16,20},{20,16},{24,28},{28,24},{1,5},{5... | collective-permute-start | bytes 67592 | tf_op jit(solution)/shard_map/ppermute | solution.py:39
  403.9 160.7 %collective-permute-start.46 = (bf16[128,2048]{1,0:T(8,128)(2,1)S(1)}, bf16[128,2048]{1,0:T(8,128)(2,1)S(1)}, u32[]{:S(2)}, u32[]{:S(2)}) collective-permute-start(bf16[128,2048]{1,0:T(8,128)(2,1)S(1)} %get-tuple-element.211), channel_id=1, source_target_pairs={{0,1},{1,0},{2,3},{3,2},{4,5},{5,4},{6,7},{7,6},{8,9},{9,8},{10,11... | collective-permute-start | bytes 1572872 | tf_op jit(solution)/shard_map/ppermute | solution.py:39
  560.2 29.3 %collective-permute-start.54 = (bf16[256,2048]{1,0:T(8,128)(2,1)}, bf16[256,2048]{1,0:T(8,128)(2,1)S(1)}, u32[]{:S(2)}, u32[]{:S(2)}) collective-permute-start(bf16[256,2048]{1,0:T(8,128)(2,1)} %get-tuple-element.190.refs_2_), channel_id=1, source_target_pairs={{0,4},{4,0},{8,12},{12,8},{16,20},{20,16},{24,28},{28,24},{1,5},{5... | collective-permute-start | bytes 3145736 | tf_op jit(solution)/shard_map/ppermute | solution.py:39
  560.2 35.4 %collective-permute-start.53 = (bf16[512,2048]{1,0:T(8,128)(2,1)}, bf16[512,2048]{1,0:T(8,128)(2,1)}, u32[]{:S(2)}, u32[]{:S(2)}) collective-permute-start(bf16[512,2048]{1,0:T(8,128)(2,1)} %get-tuple-element.189.refs_0_), channel_id=1, source_target_pairs={{0,4},{4,0},{8,12},{12,8},{16,20},{20,16},{24,28},{28,24},{1,5},{5... | collective-permute-start | bytes 6291464 | tf_op jit(solution)/shard_map/ppermute | solution.py:39
  560.8 43.6 %collective-permute-start.51 = (bf16[2048,512]{1,0:T(8,128)(2,1)}, bf16[2048,512]{1,0:T(8,128)(2,1)}, u32[]{:S(2)}, u32[]{:S(2)}) collective-permute-start(bf16[2048,512]{1,0:T(8,128)(2,1)} %get-tuple-element.187.refs_0_), channel_id=1, source_target_pairs={{0,4},{4,0},{8,12},{12,8},{16,20},{20,16},{24,28},{28,24},{1,5},{5... | collective-permute-start | bytes 6291464 | tf_op jit(solution)/shard_map/ppermute | solution.py:39
  564.6 48.5 %collective-permute-start.49 = (bf16[2048,512]{1,0:T(8,128)(2,1)}, bf16[2048,512]{1,0:T(8,128)(2,1)}, u32[]{:S(2)}, u32[]{:S(2)}) collective-permute-start(bf16[2048,512]{1,0:T(8,128)(2,1)} %get-tuple-element.185.refs_0_), channel_id=1, source_target_pairs={{0,4},{4,0},{8,12},{12,8},{16,20},{20,16},{24,28},{28,24},{1,5},{5... | collective-permute-start | bytes 6291464 | tf_op jit(solution)/shard_map/ppermute | solution.py:39
  589.6 23.4 %collective-permute-start.50 = (bf16[2048,256]{1,0:T(8,128)(2,1)S(1)}, bf16[2048,256]{1,0:T(8,128)(2,1)S(1)}, u32[]{:S(2)}, u32[]{:S(2)}) collective-permute-start(bf16[2048,256]{1,0:T(8,128)(2,1)S(1)} %copy-done.12), channel_id=1, source_target_pairs={{0,4},{4,0},{8,12},{12,8},{16,20},{20,16},{24,28},{28,24},{1,5},{5... | collective-permute-start | bytes 3145736 | tf_op jit(solution)/shard_map/ppermute | solution.py:39
  (75 other events, 902.1 us)
Sparse Core Ops, SparseCore 0:
  10.9 147.2 all-gather.2
  160.3 46.5 all-gather.4
  341.2 129.6 all-reduce.4
  474.4 85.8 all-reduce.6

commit v4 on v2

--- a/solution.py
+++ b/solution.py
@@ -47,6 +47,22 @@
         block = rows if r == 0 else swap(rows, "tp", r)
         whole = lax.dynamic_update_index_in_dim(whole, block, place ^ r, 0)
     return whole
+
+
+def spread(rows):
+    count = lax.axis_size("tp")
+    if count != 4:
+        whole = jnp.stack([rows] + [swap(rows, "tp", r) for r in range(1, count)])
+        return lambda *after: tied(whole, *after)
+    half = rows.shape[0] // 2
+    sides = swap(rows, "tp", 1), swap(rows, "tp", 2)
+
+    def finish(*after):
+        one, two, *after = tied(*sides, *after)
+        far = jnp.concatenate([swap(two[:half], "tp", 1), swap(one[half:], "tp", 2)])
+        return (jnp.stack([rows, one, two, far]), *after)
+
+    return finish
 
 
 def scatter_rows(blocks):
@@ -169,7 +185,7 @@
     def cot_index(i, c):
         i = jnp.minimum(i, steps - 1)
         n = i % per_core
-        return n % groups, c[0] ^ (i // per_core), n // groups, 0, 0
+        return n % groups, c[0] ^ (i // per_core), c[1] ^ (n // groups), 0, 0
 
     def rows_index(first):
         def index(i, c):
@@ -949,14 +965,13 @@
     )
     normed_two_grad = scatter_rows(normed_two_part.reshape(tp_size, length, model))
     dense_part = product(hidden, down_proj).astype(bf16)
-    normed_two_grad, dense_part, rows_z = tied(normed_two_grad, dense_part, rows_z)
-    rows_mine = lax.all_gather(rows_z, "tp", axis=0, tiled=True)
+    normed_two_grad, dense_part = tied(normed_two_grad, dense_part)
     mid_from_norm, dense_gain_part = norm_back(normed_two_grad, xhat_dense, dense_scale, mid_root)
     mid_grad = cotangent.astype(f32) + mid_from_norm
     mid_blocks = gather_rows(mid_grad.astype(bf16))
-    mid_blocks, dense_part = tied(mid_blocks, dense_part)
-
-    dense_out = scatter_rows(dense_part.reshape(tp_size, length, model))
+    mid_blocks, dense_part, rows_z = tied(mid_blocks, dense_part, rows_z)
+    rows_spread = spread(rows_z)
+
     direct, branch_pre_grad, reach = mix_back(mid_blocks, out_proj, branch_pre, state, keep_prefix)
     branch_pre_grad = branch_pre_grad.reshape(group, width)
     mid_rows = mid_blocks.reshape(group, model)
@@ -964,8 +979,8 @@
     after = carry_in(ends[0, 0], reach, True)
     out_full = product_left_t(mixed, mid_rows).astype(bf16)
     branch_full = product_left_t(branch_pre_grad, normed).astype(bf16)
-    after, out_full, branch_full = tied(after, out_full, branch_full)
-    out_sum, branch_sum = lax.psum((out_full, branch_full), "seq")
+    after, pair_full = tied(after, jnp.concatenate([out_full, branch_full]))
+    pair_part = lax.psum_scatter(pair_full, "seq", scatter_dimension=0, tiled=True)
     tile = lambda v: jnp.broadcast_to(v, (TILE, width))
     rate_low, input_low, inner_grad, tail, rim_grad, sums = recur_backward(
         direct,
@@ -983,7 +998,7 @@
         rate_dense,
         input_dense,
     )
-    rim_grad, rows_mine = tied(rim_grad, rows_mine)
+    rows_mine, rim_grad = rows_spread(rim_grad)
     fixed = tail + from_neighbour(rim_grad, 1)
     low_rows = conv_low.reshape(group, width)
     rate_w = diagonal_blocks(product_left_t(low_rows, rate_low.reshape(group, width)), blocks_n)
@@ -992,29 +1007,30 @@
         inner_grad, fixed.astype(bf16)[None], (tp_size - 1, length - TILE, 0)
     ).reshape(group, width)
     in_full = product_left_t(inner_grad, normed).astype(bf16)
-    block_full = jnp.concatenate([rate_w, input_w]).astype(bf16)
+    flat = lambda blocks: blocks.astype(bf16).reshape(width, -1)
+    in_full = jnp.concatenate([in_full, flat(rate_w), flat(input_w)], axis=1)
     normed_part = (product(inner_grad, in_t) + product(branch_pre_grad, branch_t)).astype(bf16)
     rows_theirs = swap(rows_mine, "seq", 1)
-    normed_part, in_full, block_full, rows_theirs, dense_out = tied(
-        normed_part, in_full, block_full, rows_theirs, dense_out
-    )
-    in_sum, block_sum = lax.psum((in_full, block_full), "seq", axis_index_groups=[list(range(seq_size))[::-1]])
+    normed_part, in_full, pair_part, rows_mine, rows_theirs = tied(
+        normed_part, in_full, pair_part, rows_mine, rows_theirs
+    )
+    pair_sum = lax.all_gather(pair_part, "seq", axis=0, tiled=True)
+    in_part = lax.psum_scatter(in_full, "seq", scatter_dimension=0, tiled=True)
     normed_grad = scatter_rows(normed_part.reshape(tp_size, length, model))
 
-    core_no = core.astype(jnp.int32)[None]
+    places = jnp.stack([core, tp_place]).astype(jnp.int32)
     blocked = lambda rows: rows.reshape(tp_size, chips, length, model)
     gate_w, up_w, down_w = dense_weight_grads(
-        blocked(rows_mine), blocked(rows_theirs), cot_all, gate_proj, up_proj, down_proj, core_no
-    )
-    gate_w, up_w, down_w, out_sum, branch_sum, normed_grad = tied(
-        gate_w, up_w, down_w, out_sum, branch_sum, normed_grad
-    )
-    gate_sum = joined(gate_w, swap(gate_w, "seq", 1), core_no, 1)
-    up_sum = joined(up_w, swap(up_w, "seq", 1), core_no, 1)
-    down_sum = joined(down_w, swap(down_w, "seq", 1), core_no, 0)
-    gate_sum, up_sum, down_sum, in_sum, block_sum = tied(gate_sum, up_sum, down_sum, in_sum, block_sum)
-
-    output = (mid + dense_out).astype(bf16)
+        blocked(rows_mine), blocked(rows_theirs), cot_all, gate_proj, up_proj, down_proj, places
+    )
+    gate_w, up_w, down_w, in_part, normed_grad, sums, dense_part = tied(
+        gate_w, up_w, down_w, in_part, normed_grad, sums, dense_part
+    )
+    in_sum = lax.all_gather(in_part, "seq", axis=0, tiled=True)
+    gate_sum = joined(gate_w, swap(gate_w, "seq", 1), places, 1)
+    up_sum = joined(up_w, swap(up_w, "seq", 1), places, 1)
+    down_sum = joined(down_w, swap(down_w, "seq", 1), places, 0)
+
     own = tokens.astype(f32)
     own_root = rms(own)
     rows_grad, mixer_gain_part = norm_back(normed_grad, own * own_root, mixer_scale, own_root)
@@ -1024,7 +1040,15 @@
     gain_sum = sum_bits(gain_own, "seq")
     sums = sum_bits(sums, "seq")
     decay_sum = 8.0 * jax.nn.sigmoid(-decay_param) * sums[2]
-    rate_sum, input_sum = block_sum[:blocks_n].astype(f32), block_sum[blocks_n:].astype(f32)
+    dense_out = scatter_rows(dense_part.reshape(tp_size, length, model))
+    output = (mid + dense_out).astype(bf16)
+    gate_sum, up_sum, down_sum, in_sum = tied(gate_sum, up_sum, down_sum, in_sum)
+    out_sum, branch_sum = pair_sum[:width], pair_sum[width:]
+    block_sum = in_sum[:, model:]
+    in_sum = in_sum[:, :model]
+    block_w = block_sum.shape[1] // 2
+    rate_sum = block_sum[:, :block_w].astype(f32).reshape(rate_blocks.shape)
+    input_sum = block_sum[:, block_w:].astype(f32).reshape(input_blocks.shape)
     return (
         output,
         tokens_grad,

time: 589 us -> 584 us (level)
  waiting for transfers between devices: 202 us -> 184 us
  other arithmetic: 36 us -> 41.9 us
    psum x2 -> x0, waiting for transfers between devices: 44.2 us -> none  [the longest x1 44.2 us: shards(): lax.psum((in_full, block_full), 'seq', axis_index_groups=[list(range(seq_...]
    ppermute x42 -> x46, waiting for transfers between devices: 147 us -> 174 us  [swap(): return lax.ppermute(value, axis, [(i, i ^ bit) for i in range(count)])]
    ppermute x3, starting transfers between devices: 13.6 us -> 2.11 us  [from_neighbour(): across = lax.ppermute(value, 'seq', pairs)]
    ppermute x42 -> x46, starting transfers between devices: 44.5 us -> 55.1 us  [swap(): return lax.ppermute(value, axis, [(i, i ^ bit) for i in range(count)])]
    all_gather x1 -> x2, waiting for transfers between devices: 8.91 us -> 0.01 us  [the longest x1 0.01 us: shards(): pair_sum = lax.all_gather(pair_part, 'seq', axis=0, tiled=True)]
    ppermute x3, waiting for transfers between devices: 0.85 us -> 8.68 us  [from_neighbour(): inside = lax.ppermute(value, 'seq', [(i, i ^ 1) for i in range(count)])]
    another operation x0 -> x5, other arithmetic: none -> 7.22 us  [the longest x2 6.4 us: finish(): return (jnp.stack([rows, one, two, far]), *after)]
    unnamed x103 -> x88, local copies, waits for them, and re-layouts: 13.8 us -> 9.92 us
  transfers between devices with their start and end apart: 53 -> 58, of which waited for: 27 -> 28; matrix products, arithmetic and copies ran while one was open for 13% -> 15% of each run, Pallas kernels for 35% -> 35%
where the time goes in v4:
time: 584 us; the launch traced here: 576 us
  Pallas kernels  204 us (35%)
  waiting for transfers between devices  184 us (32%)
  starting transfers between devices  67.4 us (12%)
  other arithmetic  41.9 us (7%)
  local copies, waits for them, and re-layouts  41.7 us (7%)
  matrix products  21.8 us (4%)
  between operations  15.3 us (3%)
    ppermute x46, waiting for transfers between devices, swap(): return lax.ppermute(value, axis, [(i, i ^ bit) for i in range(count)])  174 us
    pallas_call x1, Pallas kernels, dense_weight_grads(): pl.pallas_call(kernel, grid_spec=pltpu.PrefetchScalarGridSpec(num_scalar_...  94.6 us
    ppermute x46, starting transfers between devices, swap(): return lax.ppermute(value, axis, [(i, i ^ bit) for i in range(count)])  55.1 us
    pallas_call x1, Pallas kernels, dense_rows(): pl.pallas_call(kernel, grid_spec=pltpu.PrefetchScalarGridSpec(num_scalar_...  25 us
    pallas_call x3, Pallas kernels, joined(): pl.pallas_call(kernel, grid_spec=pltpu.PrefetchScalarGridSpec(num_scalar_...  24.1 us
    pallas_call x1, Pallas kernels, recur_backward(): pl.pallas_call(backward_kernel, grid_spec=pltpu.PrefetchScalarGridSpec(nu...  19.3 us
    pallas_call x1, Pallas kernels, recur_forward(): pl.pallas_call(forward_kernel, grid_spec=pltpu.PrefetchScalarGridSpec(num...  15.2 us
  transfers between devices with their start and end apart: 58, of which 28 were waited for; matrix products, arithmetic and copies ran while one was open for 15% of the time, Pallas kernels for 35%

profile of v4, /device:TPU:0, one launch (start us, length us, event | category | flops | bytes accessed | tf_op | source)
XLA Modules:
  0.0 576.0 jit_solution(6187822763485789710)
XLA Ops:
  13.9 10.3 %collective-permute-done.refs_1_ = bf16[128,2048]{1,0:T(8,128)(2,1)S(1)} collective-permute-done((bf16[128,2048]{1,0:T(8,128)(2,1)}, bf16[128,2048]{1,0:T(8,128)(2,1)S(1)}, u32[]{:S(2)}, u32[]{:S(2)}) %collective-permute-start) | collective-permute-done | bytes 524320 | tf_op jit(solution)/shard_map/ppermute | solution.py:39
  44.1 7.0 %norm_project.1 = (bf16[512,2048]{1,0:T(8,128)(2,1)}, f32[4,128,704]{2,1,0:T(8,128)S(1)}) custom-call(s32[1]{0:T(128)} %bitcast.place_ref, bf16[128,2048]{1,0:T(8,128)(2,1)S(1)} %copy-done.7, bf16[128,2048]{1,0:T(8,128)(2,1)S(1)} %collective-permute-done.refs_1_, bf16[128,2048]{1,0:T(8,128)(2,1)S(1)} %collective-permute-done.1.refs_2_, ...), custom_call_target="tpu_custom_call" | custom-call | tf_op jit(solution)/shard_map/norm_project/pallas_call | solution.py:725
  56.0 15.2 %recur_forward.1 = (f32[4,128,704]{2,1,0:T(8,128)}, bf16[4,128,704]{2,1,0:T(8,128)(2,1)S(1)}, f32[4,128,704]{2,1,0:T(8,128)}, f32[4,128,704]{2,1,0:T(8,128)}, f3...) custom-call(f32[4,128,704]{2,1,0:T(8,128)} %copy-done, ...), custom_call_target="tpu_custom_call" | custom-call | tf_op jit(solution)/shard_map/recur_forward/pallas_call | solution.py:750
  87.3 6.4 %mix_out.1 = (f32[4,128,704]{2,1,0:T(8,128)S(1)}, bf16[4,128,704]{2,1,0:T(8,128)(2,1)S(1)}, bf16[4,128,2048]{2,1,0:T(8,128)(2,1)}) custom-call(f32[4,128,704]{2,1,0:T(8,128)S(1)} %copy-done.14, f32[4,128,704]{2,1,0:T(8,128)} %get-tuple-element.113.keep_ref, f32[4,128,704]{2,1,0:T(8,128)} %bitcast.154, f32[1,704]{1,0:T(1,128)S(1)} %get-tuple-element.180.in_ref, ...), custom_call_target="tpu_custom_call" | custom-call | tf_op jit(solution)/shard_map/mix_out/pallas_call | solution.py:376
  99.6 22.5 %collective-permute-done.13 = bf16[128,2048]{1,0:T(8,128)(2,1)S(1)} collective-permute-done((bf16[128,2048]{1,0:T(8,128)(2,1)S(1)}, bf16[128,2048]{1,0:T(8,128)(2,1)S(1)}, u32[]{:S(2)}, u32[]{:S(2)}) %collective-permute-start.13) | collective-permute-done | bytes 524320 | tf_op jit(solution)/shard_map/ppermute | solution.py:39
  122.1 18.7 %collective-permute-done.15 = bf16[128,2048]{1,0:T(8,128)(2,1)S(1)} collective-permute-done((bf16[128,2048]{1,0:T(8,128)(2,1)S(1)}, bf16[128,2048]{1,0:T(8,128)(2,1)S(1)}, u32[]{:S(2)}, u32[]{:S(2)}) %collective-permute-start.15) | collective-permute-done | bytes 524320 | tf_op jit(solution)/shard_map/ppermute | solution.py:39
  148.8 11.1 %collective-permute-done.16 = bf16[128,2048]{1,0:T(8,128)(2,1)} collective-permute-done((bf16[128,2048]{1,0:T(8,128)(2,1)S(1)}, bf16[128,2048]{1,0:T(8,128)(2,1)}, u32[]{:S(2)}, u32[]{:S(2)}) %collective-permute-start.16) | collective-permute-done | bytes 524320 | tf_op jit(solution)/shard_map/ppermute | solution.py:39
  161.7 8.2 %collective-permute-done.17 = bf16[128,2048]{1,0:T(8,128)(2,1)S(1)} collective-permute-done((bf16[128,2048]{1,0:T(8,128)(2,1)S(1)}, bf16[128,2048]{1,0:T(8,128)(2,1)S(1)}, u32[]{:S(2)}, u32[]{:S(2)}) %collective-permute-start.17) | collective-permute-done | bytes 524320 | tf_op jit(solution)/shard_map/ppermute | solution.py:39
  171.6 25.0 %dense_rows.1 = (bf16[512,1536]{1,0:T(8,128)(2,1)S(1)}, bf16[512,2048]{1,0:T(8,128)(2,1)S(1)}) custom-call(s32[1]{0:T(128)} %bitcast.19.place_ref, bf16[512,2048]{1,0:T(8,128)(2,1)} %bitcast.169, bf16[4096,2048]{1,0:T(8,128)(2,1)} %all-gather.5.cloned.1.call-done.c_ref, bf16[2048,1536]{1,0:T(8,128)(2,1)} %gate_ref.3, bf16[2048,1536]{1,0:T(8,128)(2,1)} %up_ref.3, ...), custom_call_target="tpu_custom_call" | custom-call | tf_op jit(solution)/shard_map/dense_rows/pallas_call | solution.py:307
  204.9 6.7 %collective-permute-done.19 = bf16[128,2048]{1,0:T(8,128)(2,1)S(1)} collective-permute-done((bf16[128,2048]{1,0:T(8,128)(2,1)S(1)}, bf16[128,2048]{1,0:T(8,128)(2,1)S(1)}, u32[]{:S(2)}, u32[]{:S(2)}) %collective-permute-start.19) | collective-permute-done | bytes 524320 | tf_op jit(solution)/shard_map/ppermute | solution.py:39
  211.6 9.1 %collective-permute-done.21 = bf16[128,2048]{1,0:T(8,128)(2,1)S(1)} collective-permute-done((bf16[128,2048]{1,0:T(8,128)(2,1)S(1)}, bf16[128,2048]{1,0:T(8,128)(2,1)S(1)}, u32[]{:S(2)}, u32[]{:S(2)}) %collective-permute-start.21) | collective-permute-done | bytes 524320 | tf_op jit(solution)/shard_map/ppermute | solution.py:39
  229.8 11.7 %collective-permute-done.22 = bf16[128,2048]{1,0:T(8,128)(2,1)} collective-permute-done((bf16[128,2048]{1,0:T(8,128)(2,1)}, bf16[128,2048]{1,0:T(8,128)(2,1)}, u32[]{:S(2)}, u32[]{:S(2)}) %collective-permute-start.22) | collective-permute-done | bytes 524320 | tf_op jit(solution)/shard_map/ppermute | solution.py:39
  254.7 8.0 %mix_back.1 = (f32[4,128,704]{2,1,0:T(8,128)S(1)}, bf16[4,128,704]{2,1,0:T(8,128)(2,1)S(1)}, f32[1,704]{1,0:T(1,128)S(1)}) custom-call(bf16[4,128,2048]{2,1,0:T(8,128)(2,1)} %bitcast_dynamic-update-slice_fusion.mid_ref, bf16[704,2048]{1,0:T(8,128)(2,1)} %out_ref.3, f32[4,128,704]{2,1,0:T(8,128)S(1)} %bitcast.155, f32[4,128,704]{2,1,0:T(8,128)} %copy-done.1, ...), custom_call_target="tpu_custom_call" | custom-call | tf_op jit(solution)/shard_map/mix_back/pallas_call | solution.py:428
  280.1 19.3 %recur_backward.1 = (bf16[4,128,704]{2,1,0:T(8,128)(2,1)S(1)}, bf16[4,128,704]{2,1,0:T(8,128)(2,1)S(1)}, bf16[4,128,704]{2,1,0:T(8,128)(2,1)S(1)}, f32[8,704]{1,...) custom-call(f32[4,128,704]{2,1,0:T(8,128)} %copy-done.13, f32[4,128,704]{2,1,0:T(8,128)} %copy-done.1, ...), custom_call_target="tpu_custom_call" | custom-call | flops 1000 | bytes 1000 | tf_op jit(solution)/shard_map/recur_backward/pallas_call | solution.py:799
  304.6 21.6 %collective-permute-done.32 = bf16[256,2048]{1,0:T(8,128)(2,1)S(1)} collective-permute-done((bf16[256,2048]{1,0:T(8,128)(2,1)S(1)}, bf16[256,2048]{1,0:T(8,128)(2,1)S(1)}, u32[]{:S(2)}, u32[]{:S(2)}) %collective-permute-start.32) | collective-permute-done | bytes 1048608 | tf_op jit(solution)/shard_map/ppermute | solution.py:39
  327.0 6.2 %pad_maximum_fusion = bf16[4,512,2048]{2,1,0:T(8,128)(2,1)} fusion(bf16[1,512,2048]{2,1,0:T(8,128)(2,1)S(1)} %maximum_bitcast_fusion, bf16[1,512,2048]{2,1,0:T(8,128)(2,1)} %bitcast.53, bf16[1,512,2048]{2,1,0:T(8,128)(2,1)} %bitcast.52, bf16[1,512,2048]{2,1,0:T(8,128)(2,1)S(1)} %bitcast.176), kind=kLoop, calls=%fused_computation | loop fusion | flops 12582912 | bytes 16777216 | tf_op jit(solution)/shard_map/stack | solution.py:63
  338.6 7.8 %collective-permute-done.30 = f32[8,704]{1,0:T(8,128)S(1)} collective-permute-done((f32[8,704]{1,0:T(8,128)S(1)}, f32[8,704]{1,0:T(8,128)S(1)}, u32[]{:S(2)}, u32[]{:S(2)}) %collective-permute-start.30) | collective-permute-done | bytes 22560 | tf_op jit(solution)/shard_map/ppermute | solution.py:98
  349.7 6.0 %concatenate.22 = bf16[704,2400]{1,0:T(8,128)(2,1)} concatenate(bf16[704,2048]{1,0:T(8,128)(2,1)} %convolution_convert_fusion, bf16[704,176]{1,0:T(8,128)(2,1)S(1)} %bitcast.180, bf16[704,176]{1,0:T(8,128)(2,1)S(1)} %bitcast.179), dimensions={1} | concatenate | bytes 6758400 | tf_op jit(solution)/shard_map/concatenate | solution.py:1011
  369.2 94.6 %dense_weight_grads.1 = (bf16[2048,768]{1,0:T(8,128)(2,1)}, bf16[2048,768]{1,0:T(8,128)(2,1)}, bf16[768,2048]{1,0:T(8,128)(2,1)}) custom-call(s32[2]{0:T(128)} %pad_add_fusion.2.core_ref, bf16[4,4,128,2048]{3,2,1,0:T(8,128)(2,1)} %bitcast.55.mine_ref, bf16[4,4,128,2048]{3,2,1,0:T(8,128)(2,1)} %bitcast.56.theirs_ref, bf16[4,2,4,128,2048]{4,3,2,1,0:T(8,128)(2,1)} %bitcast.164, ...), custom_call_target="tpu_custom_call" | custom-call | flops 1000 | bytes 1000 | tf_op jit(solution)/shard_map/dense_weight_grads/pallas_call | solution.py:197
  513.1 11.1 %collective-permute-done.39 = bf16[128,2048]{1,0:T(8,128)(2,1)S(1)} collective-permute-done((bf16[128,2048]{1,0:T(8,128)(2,1)}, bf16[128,2048]{1,0:T(8,128)(2,1)S(1)}, u32[]{:S(2)}, u32[]{:S(2)}) %collective-permute-start.39) | collective-permute-done | bytes 524320 | tf_op jit(solution)/shard_map/ppermute | solution.py:39
  527.9 7.0 %joined.5 = f32[2,768,2048]{2,1,0:T(8,128)} custom-call(s32[2]{0:T(128)S(1)} %copy-done.16, bf16[768,2048]{1,0:T(8,128)(2,1)S(1)} %copy-done.10, bf16[768,2048]{1,0:T(8,128)(2,1)} %collective-permute-done.48.theirs_ref), custom_call_target="tpu_custom_call" | custom-call | flops 1000 | bytes 1000 | tf_op jit(solution)/shard_map/joined/pallas_call | solution.py:261
  534.9 8.7 %joined.4 = f32[2048,1536]{1,0:T(8,128)} custom-call(s32[2]{0:T(128)S(1)} %copy-done.16, bf16[2048,768]{1,0:T(8,128)(2,1)S(1)} %copy-done.9, bf16[2048,768]{1,0:T(8,128)(2,1)} %collective-permute-done.47.theirs_ref), custom_call_target="tpu_custom_call" | custom-call | flops 1000 | bytes 1000 | tf_op jit(solution)/shard_map/joined/pallas_call | solution.py:261
  543.6 8.4 %joined.3 = f32[2048,1536]{1,0:T(8,128)} custom-call(s32[2]{0:T(128)S(1)} %copy-done.16, bf16[2048,768]{1,0:T(8,128)(2,1)S(1)} %copy-done.8, bf16[2048,768]{1,0:T(8,128)(2,1)} %collective-permute-done.46.theirs_ref), custom_call_target="tpu_custom_call" | custom-call | flops 1000 | bytes 1000 | tf_op jit(solution)/shard_map/joined/pallas_call | solution.py:261
  552.0 8.7 %slice_convert_fusion = (f32[704,2048]{1,0:T(8,128)}, f32[2048,704]{0,1:T(8,128)}) fusion(bf16[1408,2048]{1,0:T(8,128)(2,1)} %all-gather.11.cloned.1.call-done), kind=kLoop, calls=%fused_computation.9 | loop fusion | flops 2883584 | bytes 17301504 | tf_op jit(solution)/shard_map/convert_element_type | solution.py:1065
  (321 shorter events, 201.5 us)
Async XLA Ops:
  7.2 164.3 %all-gather.5.cloned.1.call-start = ((), (), s32[]{:S(2)}) async-start(), calls=%async_computation.2 | async-start | bytes 17301504 | tf_op jit(solution)/shard_map/all_gather | solution.py:941
  7.9 243.8 %all-gather.7.cloned.1.call-start = ((), (), s32[]{:S(2)}) async-start(), calls=%async_computation.3 | async-start | bytes 2621440 | tf_op jit(solution)/shard_map/all_gather | solution.py:961
  11.0 29.9 %collective-permute-start.1 = (bf16[128,2048]{1,0:T(8,128)(2,1)}, bf16[128,2048]{1,0:T(8,128)(2,1)S(1)}, u32[]{:S(2)}, u32[]{:S(2)}) collective-permute-start(bf16[128,2048]{1,0:T(8,128)(2,1)} %refs_0_), channel_id=1, source_target_pairs={{0,2},{1,3},{2,0},{3,1},{4,6},{5,7},{6,4},{7,5},{8,10},{9,11},{10,... | collective-permute-start | bytes 1572872 | tf_op jit(solution)/shard_map/ppermute | solution.py:39
  12.5 28.4 %collective-permute-start.2 = (bf16[128,2048]{1,0:T(8,128)(2,1)}, bf16[128,2048]{1,0:T(8,128)(2,1)S(1)}, u32[]{:S(2)}, u32[]{:S(2)}) collective-permute-start(bf16[128,2048]{1,0:T(8,128)(2,1)} %refs_0_), channel_id=1, source_target_pairs={{0,3},{1,2},{2,1},{3,0},{4,7},{5,6},{6,5},{7,4},{8,11},{9,10},{10,... | collective-permute-start | bytes 1572872 | tf_op jit(solution)/shard_map/ppermute | solution.py:39
  96.1 26.1 %collective-permute-start.13 = (bf16[128,2048]{1,0:T(8,128)(2,1)S(1)}, bf16[128,2048]{1,0:T(8,128)(2,1)S(1)}, u32[]{:S(2)}, u32[]{:S(2)}) collective-permute-start(bf16[128,2048]{1,0:T(8,128)(2,1)S(1)} %get-tuple-element.200), channel_id=1, source_target_pairs={{0,1},{1,0},{2,3},{3,2},{4,5},{5,4},{6,7},{7,6},{8,9},{9,8},{10,11... | collective-permute-start | bytes 1572872 | tf_op jit(solution)/shard_map/ppermute | solution.py:39
  96.8 44.1 %collective-permute-start.15 = (bf16[128,2048]{1,0:T(8,128)(2,1)S(1)}, bf16[128,2048]{1,0:T(8,128)(2,1)S(1)}, u32[]{:S(2)}, u32[]{:S(2)}) collective-permute-start(bf16[128,2048]{1,0:T(8,128)(2,1)S(1)} %get-tuple-element.201), channel_id=1, source_target_pairs={{0,3},{1,2},{2,1},{3,0},{4,7},{5,6},{6,5},{7,4},{8,11},{9,10},{10,... | collective-permute-start | bytes 1572872 | tf_op jit(solution)/shard_map/ppermute | solution.py:39
  99.0 41.8 %collective-permute-start.14 = (bf16[128,2048]{1,0:T(8,128)(2,1)S(1)}, bf16[128,2048]{1,0:T(8,128)(2,1)S(1)}, u32[]{:S(2)}, u32[]{:S(2)}) collective-permute-start(bf16[128,2048]{1,0:T(8,128)(2,1)S(1)} %get-tuple-element.202), channel_id=1, source_target_pairs={{0,2},{1,3},{2,0},{3,1},{4,6},{5,7},{6,4},{7,5},{8,10},{9,11},{10,... | collective-permute-start | bytes 1572872 | tf_op jit(solution)/shard_map/ppermute | solution.py:39
  145.5 24.4 %collective-permute-start.17 = (bf16[128,2048]{1,0:T(8,128)(2,1)S(1)}, bf16[128,2048]{1,0:T(8,128)(2,1)S(1)}, u32[]{:S(2)}, u32[]{:S(2)}) collective-permute-start(bf16[128,2048]{1,0:T(8,128)(2,1)S(1)} %get-tuple-element.184), channel_id=1, source_target_pairs={{0,2},{1,3},{2,0},{3,1},{4,6},{5,7},{6,4},{7,5},{8,10},{9,11},{10,... | collective-permute-start | bytes 1572872 | tf_op jit(solution)/shard_map/ppermute | solution.py:39
  145.8 24.9 %collective-permute-start.18 = (bf16[128,2048]{1,0:T(8,128)(2,1)S(1)}, bf16[128,2048]{1,0:T(8,128)(2,1)S(1)}, u32[]{:S(2)}, u32[]{:S(2)}) collective-permute-start(bf16[128,2048]{1,0:T(8,128)(2,1)S(1)} %get-tuple-element.184), channel_id=1, source_target_pairs={{0,3},{1,2},{2,1},{3,0},{4,7},{5,6},{6,5},{7,4},{8,11},{9,10},{10,... | collective-permute-start | bytes 1572872 | tf_op jit(solution)/shard_map/ppermute | solution.py:39
  148.4 214.2 %reduce-scatter.5.cloned.1.call-start = ((), (), s32[]{:S(2)}) async-start(), calls=%async_computation.4 | async-start | bytes 6488064 | tf_op jit(solution)/shard_map/reduce_scatter | solution.py:983
  251.8 47.6 %collective-permute-start.29 = (bf16[512,2048]{1,0:T(8,128)(2,1)}, bf16[512,2048]{1,0:T(8,128)(2,1)}, u32[]{:S(2)}, u32[]{:S(2)}) collective-permute-start(bf16[512,2048]{1,0:T(8,128)(2,1)} %all-gather.7.cloned.1.call-done), channel_id=1, source_target_pairs={{0,2},{1,3},{2,0},{3,1},{4,6},{5,7},{6,4},{7,5},{8,10},{9,11},{10,... | collective-permute-start | bytes 6291464 | tf_op jit(solution)/shard_map/ppermute | solution.py:39
  251.8 47.6 %collective-permute-start.28 = (bf16[512,2048]{1,0:T(8,128)(2,1)}, bf16[512,2048]{1,0:T(8,128)(2,1)}, u32[]{:S(2)}, u32[]{:S(2)}) collective-permute-start(bf16[512,2048]{1,0:T(8,128)(2,1)} %all-gather.7.cloned.1.call-done), channel_id=1, source_target_pairs={{0,1},{1,0},{2,3},{3,2},{4,5},{5,4},{6,7},{7,6},{8,9},{9,8},{10,11... | collective-permute-start | bytes 6291464 | tf_op jit(solution)/shard_map/ppermute | solution.py:39
  278.9 186.4 %reduce-scatter.7.cloned.1.call-start = ((), (), s32[]{:S(2)}) async-start(), calls=%async_computation.7 | async-start | bytes 3852288
  302.5 24.3 %collective-permute-start.33 = (bf16[256,2048]{1,0:T(8,128)(2,1)S(1)}, bf16[256,2048]{1,0:T(8,128)(2,1)S(1)}, u32[]{:S(2)}, u32[]{:S(2)}) collective-permute-start(bf16[256,2048]{1,0:T(8,128)(2,1)S(1)} %slice.278), channel_id=1, source_target_pairs={{0,2},{1,3},{2,0},{3,1},{4,6},{5,7},{6,4},{7,5},{8,10},{9,11},{10,... | collective-permute-start | bytes 3145736 | tf_op jit(solution)/shard_map/ppermute | solution.py:39
  333.2 29.4 %collective-permute-start.34 = (bf16[4,512,2048]{2,1,0:T(8,128)(2,1)}, bf16[4,512,2048]{2,1,0:T(8,128)(2,1)}, u32[]{:S(2)}, u32[]{:S(2)}) collective-permute-start(bf16[4,512,2048]{2,1,0:T(8,128)(2,1)} %pad_maximum_fusion), channel_id=1, source_target_pairs={{0,4},{4,0},{8,12},{12,8},{16,20},{20,16},{24,28},{28,24},{1,5},{5... | collective-permute-start | bytes 25165832 | tf_op jit(solution)/shard_map/ppermute | solution.py:39
  362.7 189.3 %all-gather.11.cloned.1.call-start = ((), (), s32[]{:S(2)}) async-start(), calls=%async_computation.6 | async-start | bytes 6488064 | tf_op jit(solution)/shard_map/all_gather | solution.py:1017
  363.2 197.4 %all-gather.9.cloned.1.call-start = ((), (), s32[]{:S(2)}) async-start(), calls=%async_computation.5 | async-start | bytes 3852288 | tf_op jit(solution)/shard_map/all_gather | solution.py:1029
  365.0 98.8 %collective-permute-start.35 = (bf16[128,2048]{1,0:T(8,128)(2,1)S(1)}, bf16[128,2048]{1,0:T(8,128)(2,1)S(1)}, u32[]{:S(2)}, u32[]{:S(2)}) collective-permute-start(bf16[128,2048]{1,0:T(8,128)(2,1)S(1)} %get-tuple-element.194), channel_id=1, source_target_pairs={{0,1},{1,0},{2,3},{3,2},{4,5},{5,4},{6,7},{7,6},{8,9},{9,8},{10,11... | collective-permute-start | bytes 1572872 | tf_op jit(solution)/shard_map/ppermute | solution.py:39
  366.5 97.4 %collective-permute-start.37 = (bf16[128,2048]{1,0:T(8,128)(2,1)S(1)}, bf16[128,2048]{1,0:T(8,128)(2,1)S(1)}, u32[]{:S(2)}, u32[]{:S(2)}) collective-permute-start(bf16[128,2048]{1,0:T(8,128)(2,1)S(1)} %get-tuple-element.195), channel_id=1, source_target_pairs={{0,3},{1,2},{2,1},{3,0},{4,7},{5,6},{6,5},{7,4},{8,11},{9,10},{10,... | collective-permute-start | bytes 1572872 | tf_op jit(solution)/shard_map/ppermute | solution.py:39
  368.3 95.6 %collective-permute-start.36 = (bf16[128,2048]{1,0:T(8,128)(2,1)S(1)}, bf16[128,2048]{1,0:T(8,128)(2,1)S(1)}, u32[]{:S(2)}, u32[]{:S(2)}) collective-permute-start(bf16[128,2048]{1,0:T(8,128)(2,1)S(1)} %get-tuple-element.196), channel_id=1, source_target_pairs={{0,2},{1,3},{2,0},{3,1},{4,6},{5,7},{6,4},{7,5},{8,10},{9,11},{10,... | collective-permute-start | bytes 1572872 | tf_op jit(solution)/shard_map/ppermute | solution.py:39
  465.3 62.6 %collective-permute-start.48 = (bf16[768,2048]{1,0:T(8,128)(2,1)}, bf16[768,2048]{1,0:T(8,128)(2,1)}, u32[]{:S(2)}, u32[]{:S(2)}) collective-permute-start(bf16[768,2048]{1,0:T(8,128)(2,1)} %get-tuple-element.163.mine_ref), channel_id=1, source_target_pairs={{0,4},{4,0},{8,12},{12,8},{16,20},{20,16},{24,28},{28,24},{1,5},{5... | collective-permute-start | bytes 9437192 | tf_op jit(solution)/shard_map/ppermute | solution.py:39
  465.4 69.5 %collective-permute-start.47 = (bf16[2048,768]{1,0:T(8,128)(2,1)}, bf16[2048,768]{1,0:T(8,128)(2,1)}, u32[]{:S(2)}, u32[]{:S(2)}) collective-permute-start(bf16[2048,768]{1,0:T(8,128)(2,1)} %get-tuple-element.162.mine_ref), channel_id=1, source_target_pairs={{0,4},{4,0},{8,12},{12,8},{16,20},{20,16},{24,28},{28,24},{1,5},{5... | collective-permute-start | bytes 9437192 | tf_op jit(solution)/shard_map/ppermute | solution.py:39
  465.9 77.7 %collective-permute-start.46 = (bf16[2048,768]{1,0:T(8,128)(2,1)}, bf16[2048,768]{1,0:T(8,128)(2,1)}, u32[]{:S(2)}, u32[]{:S(2)}) collective-permute-start(bf16[2048,768]{1,0:T(8,128)(2,1)} %get-tuple-element.161.mine_ref), channel_id=1, source_target_pairs={{0,4},{4,0},{8,12},{12,8},{16,20},{20,16},{24,28},{28,24},{1,5},{5... | collective-permute-start | bytes 9437192 | tf_op jit(solution)/shard_map/ppermute | solution.py:39
  470.7 34.4 %collective-permute-start.38 = (bf16[128,2048]{1,0:T(8,128)(2,1)}, bf16[128,2048]{1,0:T(8,128)(2,1)}, u32[]{:S(2)}, u32[]{:S(2)}) collective-permute-start(bf16[128,2048]{1,0:T(8,128)(2,1)} %get-tuple-element.191), channel_id=1, source_target_pairs={{0,1},{1,0},{2,3},{3,2},{4,5},{5,4},{6,7},{7,6},{8,9},{9,8},{10,11... | collective-permute-start | bytes 1572872 | tf_op jit(solution)/shard_map/ppermute | solution.py:39
  (76 other events, 1039.3 us)
Sparse Core Ops, SparseCore 0:
  10.9 147.3 all-gather.4
  160.4 44.0 all-gather.6
  279.0 68.5 reduce-scatter.4
  362.8 46.4 reduce-scatter.6
  410.8 60.5 all-gather.10
  472.9 42.2 all-gather.8

commit v5 on v4

--- a/solution.py
+++ b/solution.py
@@ -265,7 +265,7 @@
         ),
         out_shape=out_shape,
         compiler_params=pltpu.CompilerParams(vmem_limit_bytes=VMEM_LIMIT),
-        cost_estimate=pl.CostEstimate(flops=1000, bytes_accessed=1000, transcendentals=0),
+        cost_estimate=pl.CostEstimate(flops=0, bytes_accessed=12 * rows * cols, transcendentals=0),
         name="joined",
     )(core, mine, theirs)
     return out if axis == 1 else out.reshape(2 * rows, cols)
@@ -1007,48 +1007,63 @@
         inner_grad, fixed.astype(bf16)[None], (tp_size - 1, length - TILE, 0)
     ).reshape(group, width)
     in_full = product_left_t(inner_grad, normed).astype(bf16)
-    flat = lambda blocks: blocks.astype(bf16).reshape(width, -1)
-    in_full = jnp.concatenate([in_full, flat(rate_w), flat(input_w)], axis=1)
+    block_full = jnp.concatenate([rate_w, input_w]).astype(bf16)
+    block_sum = block_full + swap(block_full, "seq", 1)
     normed_part = (product(inner_grad, in_t) + product(branch_pre_grad, branch_t)).astype(bf16)
     rows_theirs = swap(rows_mine, "seq", 1)
-    normed_part, in_full, pair_part, rows_mine, rows_theirs = tied(
-        normed_part, in_full, pair_part, rows_mine, rows_theirs
+    normed_part, in_full, pair_part, rows_mine, rows_theirs, block_sum, dense_part = tied(
+        normed_part, in_full, pair_part, rows_mine, rows_theirs, block_sum, dense_part
     )
     pair_sum = lax.all_gather(pair_part, "seq", axis=0, tiled=True)
     in_part = lax.psum_scatter(in_full, "seq", scatter_dimension=0, tiled=True)
-    normed_grad = scatter_rows(normed_part.reshape(tp_size, length, model))
+    split = lambda rows: rows.reshape(tp_size, length, model)
+    grad_and_out = scatter_rows(jnp.concatenate([split(normed_part), split(dense_part)], axis=1))
+    block_other = swap(block_sum, "seq", 2)
 
     places = jnp.stack([core, tp_place]).astype(jnp.int32)
     blocked = lambda rows: rows.reshape(tp_size, chips, length, model)
     gate_w, up_w, down_w = dense_weight_grads(
         blocked(rows_mine), blocked(rows_theirs), cot_all, gate_proj, up_proj, down_proj, places
     )
-    gate_w, up_w, down_w, in_part, normed_grad, sums, dense_part = tied(
-        gate_w, up_w, down_w, in_part, normed_grad, sums, dense_part
-    )
+    gate_w, up_w, down_w, in_part, grad_and_out, block_other = tied(
+        gate_w, up_w, down_w, in_part, grad_and_out, block_other
+    )
+    normed_grad, dense_out = grad_and_out[:length], grad_and_out[length:]
+    block_sum = block_sum + block_other
+    bit = 4
+    while bit < seq_size:
+        block_sum = block_sum + swap(block_sum, "seq", bit)
+        bit *= 2
     in_sum = lax.all_gather(in_part, "seq", axis=0, tiled=True)
-    gate_sum = joined(gate_w, swap(gate_w, "seq", 1), places, 1)
-    up_sum = joined(up_w, swap(up_w, "seq", 1), places, 1)
-    down_sum = joined(down_w, swap(down_w, "seq", 1), places, 0)
-
+    halves = [(gate_w, swap(gate_w, "seq", 1), 1), (up_w, swap(up_w, "seq", 1), 1), (down_w, swap(down_w, "seq", 1), 0)]
+    output = (mid + dense_out).astype(bf16)
     own = tokens.astype(f32)
     own_root = rms(own)
     rows_grad, mixer_gain_part = norm_back(normed_grad, own * own_root, mixer_scale, own_root)
     tokens_grad = mid_grad + rows_grad
-    gain_parts = sum_bits(jnp.stack([mixer_gain_part, dense_gain_part]), "tp")
-    gain_own = lax.dynamic_slice_in_dim(gain_parts, tp_place * gain_share, gain_share, 1)
-    gain_sum = sum_bits(gain_own, "seq")
-    sums = sum_bits(sums, "seq")
+    out_sum, branch_sum = pair_sum[:width].astype(f32), pair_sum[width:].astype(f32)
+
+    small = jnp.stack([mixer_gain_part, dense_gain_part])
+    whole = []
+    for axis, size in (("tp", tp_size), ("seq", seq_size)):
+        if axis == "seq":
+            gain_own = lax.dynamic_slice_in_dim(small, tp_place * gain_share, gain_share, 1)
+            wide = max(width, gain_share)
+            fit = lambda v: jnp.pad(v, ((0, 0), (0, wide - v.shape[1])))
+            small = jnp.concatenate([fit(sums), fit(gain_own)])
+        bit = 1
+        while bit < size:
+            other = swap(small, axis, bit)
+            if halves:
+                mine, theirs, along = halves.pop(0)
+                made, other = tied(joined(mine, theirs, places, along), other)
+                whole.append(made)
+            small = small + other
+            bit *= 2
+    gate_sum, up_sum, down_sum = whole
+    sums, gain_sum = small[:-2, :width], small[-2:, :gain_share]
     decay_sum = 8.0 * jax.nn.sigmoid(-decay_param) * sums[2]
-    dense_out = scatter_rows(dense_part.reshape(tp_size, length, model))
-    output = (mid + dense_out).astype(bf16)
-    gate_sum, up_sum, down_sum, in_sum = tied(gate_sum, up_sum, down_sum, in_sum)
-    out_sum, branch_sum = pair_sum[:width], pair_sum[width:]
-    block_sum = in_sum[:, model:]
-    in_sum = in_sum[:, :model]
-    block_w = block_sum.shape[1] // 2
-    rate_sum = block_sum[:, :block_w].astype(f32).reshape(rate_blocks.shape)
-    input_sum = block_sum[:, block_w:].astype(f32).reshape(input_blocks.shape)
+    rate_sum, input_sum = block_sum[:blocks_n].astype(f32), block_sum[blocks_n:].astype(f32)
     return (
         output,
         tokens_grad,

time: 584 us -> 577 us (0.988)
  starting transfers between devices: 67.4 us -> 58.5 us
  local copies, waits for them, and re-layouts: 41.7 us -> 34.5 us
    ppermute x46 -> x43, waiting for transfers between devices: 174 us -> 186 us  [swap(): return lax.ppermute(value, axis, [(i, i ^ bit) for i in range(count)])]
    ppermute x3, waiting for transfers between devices: 8.68 us -> 0.2 us  [from_neighbour(): inside = lax.ppermute(value, 'seq', [(i, i ^ 1) for i in range(count)])]
    ppermute x3, starting transfers between devices: 9.02 us -> 1.47 us  [from_neighbour(): inside = lax.ppermute(value, 'seq', [(i, i ^ 1) for i in range(count)])]
    concatenate x1, local copies, waits for them, and re-layouts: 5.98 us -> 0.09 us  [shards(): block_full = jnp.concatenate([rate_w, input_w]).astype(bf16)]
    unnamed x88 -> x91, local copies, waits for them, and re-layouts: 9.92 us -> 12.8 us
    ppermute x46 -> x43, starting transfers between devices: 55.1 us -> 53.8 us  [swap(): return lax.ppermute(value, axis, [(i, i ^ bit) for i in range(count)])]
  transfers between devices with their start and end apart: 58 -> 55, of which waited for: 28 -> 25; matrix products, arithmetic and copies ran while one was open for 15% -> 15% of each run, Pallas kernels for 35% -> 36%
where the time goes in v5:
time: 577 us; the launch traced here: 569 us
  Pallas kernels  204 us (35%)
  waiting for transfers between devices  187 us (32%)
  starting transfers between devices  58.5 us (10%)
  other arithmetic  47.7 us (8%)
  local copies, waits for them, and re-layouts  34.5 us (6%)
  matrix products  22 us (4%)
  between operations  15.4 us (3%)
    ppermute x43, waiting for transfers between devices, swap(): return lax.ppermute(value, axis, [(i, i ^ bit) for i in range(count)])  186 us
    pallas_call x1, Pallas kernels, dense_weight_grads(): pl.pallas_call(kernel, grid_spec=pltpu.PrefetchScalarGridSpec(num_scalar_...  94.8 us
    ppermute x43, starting transfers between devices, swap(): return lax.ppermute(value, axis, [(i, i ^ bit) for i in range(count)])  53.8 us
    pallas_call x1, Pallas kernels, dense_rows(): pl.pallas_call(kernel, grid_spec=pltpu.PrefetchScalarGridSpec(num_scalar_...  24.9 us
    pallas_call x3, Pallas kernels, joined(): pl.pallas_call(kernel, grid_spec=pltpu.PrefetchScalarGridSpec(num_scalar_...  24.1 us
    pallas_call x1, Pallas kernels, recur_backward(): pl.pallas_call(backward_kernel, grid_spec=pltpu.PrefetchScalarGridSpec(nu...  19.3 us
    pallas_call x1, Pallas kernels, recur_forward(): pl.pallas_call(forward_kernel, grid_spec=pltpu.PrefetchScalarGridSpec(num...  15.2 us
    unnamed x91, local copies, waits for them, and re-layouts  12.8 us
  transfers between devices with their start and end apart: 55, of which 25 were waited for; matrix products, arithmetic and copies ran while one was open for 15% of the time, Pallas kernels for 36%

profile of v5, /device:TPU:0, one launch (start us, length us, event | category | flops | bytes accessed | tf_op | source)
XLA Modules:
  0.0 569.0 jit_solution(1917729024201839045)
XLA Ops:
  13.9 10.3 %collective-permute-done.refs_1_ = bf16[128,2048]{1,0:T(8,128)(2,1)S(1)} collective-permute-done((bf16[128,2048]{1,0:T(8,128)(2,1)}, bf16[128,2048]{1,0:T(8,128)(2,1)S(1)}, u32[]{:S(2)}, u32[]{:S(2)}) %collective-permute-start) | collective-permute-done | bytes 524320 | tf_op jit(solution)/shard_map/ppermute | solution.py:39
  42.0 7.0 %norm_project.1 = (bf16[512,2048]{1,0:T(8,128)(2,1)}, f32[4,128,704]{2,1,0:T(8,128)S(1)}) custom-call(s32[1]{0:T(128)} %bitcast.place_ref, bf16[128,2048]{1,0:T(8,128)(2,1)S(1)} %copy-done.7, bf16[128,2048]{1,0:T(8,128)(2,1)S(1)} %collective-permute-done.refs_1_, bf16[128,2048]{1,0:T(8,128)(2,1)S(1)} %collective-permute-done.1.refs_2_, ...), custom_call_target="tpu_custom_call" | custom-call | tf_op jit(solution)/shard_map/norm_project/pallas_call | solution.py:725
  51.3 15.2 %recur_forward.1 = (f32[4,128,704]{2,1,0:T(8,128)}, bf16[4,128,704]{2,1,0:T(8,128)(2,1)S(1)}, f32[4,128,704]{2,1,0:T(8,128)}, f32[4,128,704]{2,1,0:T(8,128)}, f3...) custom-call(f32[4,128,704]{2,1,0:T(8,128)} %copy-done, ...), custom_call_target="tpu_custom_call" | custom-call | tf_op jit(solution)/shard_map/recur_forward/pallas_call | solution.py:750
  66.5 6.4 %collective-permute-start.10 = (f32[2,704]{1,0:T(2,128)S(1)}, f32[2,704]{1,0:T(2,128)S(1)}, u32[]{:S(2)}, u32[]{:S(2)}) collective-permute-start(f32[2,704]{1,0:T(2,128)S(1)} %pad_maximum_fusion.5), channel_id=1, source_target_pairs={{0,4},{4,0},{8,12},{12,8},{16,20},{20,16},{24,28},{28,24},{1,5},{5... | collective-permute-start | bytes 16904 | tf_op jit(solution)/shard_map/ppermute | solution.py:39
  87.1 6.4 %mix_out.1 = (f32[4,128,704]{2,1,0:T(8,128)S(1)}, bf16[4,128,704]{2,1,0:T(8,128)(2,1)S(1)}, bf16[4,128,2048]{2,1,0:T(8,128)(2,1)}) custom-call(f32[4,128,704]{2,1,0:T(8,128)S(1)} %copy-done.14, f32[4,128,704]{2,1,0:T(8,128)} %get-tuple-element.116.keep_ref, f32[4,128,704]{2,1,0:T(8,128)} %bitcast.156, f32[1,704]{1,0:T(1,128)S(1)} %get-tuple-element.186.in_ref, ...), custom_call_target="tpu_custom_call" | custom-call | tf_op jit(solution)/shard_map/mix_out/pallas_call | solution.py:376
  99.5 22.5 %collective-permute-done.13 = bf16[128,2048]{1,0:T(8,128)(2,1)S(1)} collective-permute-done((bf16[128,2048]{1,0:T(8,128)(2,1)S(1)}, bf16[128,2048]{1,0:T(8,128)(2,1)S(1)}, u32[]{:S(2)}, u32[]{:S(2)}) %collective-permute-start.13) | collective-permute-done | bytes 524320 | tf_op jit(solution)/shard_map/ppermute | solution.py:39
  123.4 17.5 %collective-permute-done.15 = bf16[128,2048]{1,0:T(8,128)(2,1)S(1)} collective-permute-done((bf16[128,2048]{1,0:T(8,128)(2,1)S(1)}, bf16[128,2048]{1,0:T(8,128)(2,1)S(1)}, u32[]{:S(2)}, u32[]{:S(2)}) %collective-permute-start.15) | collective-permute-done | bytes 524320 | tf_op jit(solution)/shard_map/ppermute | solution.py:39
  149.0 11.1 %collective-permute-done.16 = bf16[128,2048]{1,0:T(8,128)(2,1)} collective-permute-done((bf16[128,2048]{1,0:T(8,128)(2,1)S(1)}, bf16[128,2048]{1,0:T(8,128)(2,1)}, u32[]{:S(2)}, u32[]{:S(2)}) %collective-permute-start.16) | collective-permute-done | bytes 524320 | tf_op jit(solution)/shard_map/ppermute | solution.py:39
  162.8 7.2 %collective-permute-done.18 = bf16[128,2048]{1,0:T(8,128)(2,1)S(1)} collective-permute-done((bf16[128,2048]{1,0:T(8,128)(2,1)S(1)}, bf16[128,2048]{1,0:T(8,128)(2,1)S(1)}, u32[]{:S(2)}, u32[]{:S(2)}) %collective-permute-start.18) | collective-permute-done | bytes 524320 | tf_op jit(solution)/shard_map/ppermute | solution.py:39
  170.8 24.9 %dense_rows.1 = (bf16[512,1536]{1,0:T(8,128)(2,1)S(1)}, bf16[512,2048]{1,0:T(8,128)(2,1)S(1)}) custom-call(s32[1]{0:T(128)} %bitcast.19.place_ref, bf16[512,2048]{1,0:T(8,128)(2,1)} %bitcast.24.x_ref, bf16[4096,2048]{1,0:T(8,128)(2,1)} %all-gather.5.cloned.1.call-done.c_ref, bf16[2048,1536]{1,0:T(8,128)(2,1)} %gate_ref.3, bf16[2048,1536]{1,0:T(8,128)(2,1)} %up_ref.3, ...), custom_call_target="tpu_custom_call" | custom-call | tf_op jit(solution)/shard_map/dense_rows/pallas_call | solution.py:307
  204.3 6.6 %collective-permute-done.19 = bf16[128,2048]{1,0:T(8,128)(2,1)S(1)} collective-permute-done((bf16[128,2048]{1,0:T(8,128)(2,1)S(1)}, bf16[128,2048]{1,0:T(8,128)(2,1)S(1)}, u32[]{:S(2)}, u32[]{:S(2)}) %collective-permute-start.19) | collective-permute-done | bytes 524320 | tf_op jit(solution)/shard_map/ppermute | solution.py:39
  211.3 8.7 %collective-permute-done.21 = bf16[128,2048]{1,0:T(8,128)(2,1)S(1)} collective-permute-done((bf16[128,2048]{1,0:T(8,128)(2,1)S(1)}, bf16[128,2048]{1,0:T(8,128)(2,1)S(1)}, u32[]{:S(2)}, u32[]{:S(2)}) %collective-permute-start.21) | collective-permute-done | bytes 524320 | tf_op jit(solution)/shard_map/ppermute | solution.py:39
  227.7 11.7 %collective-permute-done.22 = bf16[128,2048]{1,0:T(8,128)(2,1)} collective-permute-done((bf16[128,2048]{1,0:T(8,128)(2,1)}, bf16[128,2048]{1,0:T(8,128)(2,1)}, u32[]{:S(2)}, u32[]{:S(2)}) %collective-permute-start.22) | collective-permute-done | bytes 524320 | tf_op jit(solution)/shard_map/ppermute | solution.py:39
  253.3 8.0 %mix_back.1 = (f32[4,128,704]{2,1,0:T(8,128)S(1)}, bf16[4,128,704]{2,1,0:T(8,128)(2,1)S(1)}, f32[1,704]{1,0:T(1,128)S(1)}) custom-call(bf16[4,128,2048]{2,1,0:T(8,128)(2,1)} %bitcast_dynamic-update-slice_fusion.mid_ref, bf16[704,2048]{1,0:T(8,128)(2,1)} %out_ref.3, f32[4,128,704]{2,1,0:T(8,128)S(1)} %bitcast.157, f32[4,128,704]{2,1,0:T(8,128)} %copy-done.1, ...), custom_call_target="tpu_custom_call" | custom-call | tf_op jit(solution)/shard_map/mix_back/pallas_call | solution.py:428
  278.6 19.3 %recur_backward.1 = (bf16[4,128,704]{2,1,0:T(8,128)(2,1)S(1)}, bf16[4,128,704]{2,1,0:T(8,128)(2,1)S(1)}, bf16[4,128,704]{2,1,0:T(8,128)(2,1)S(1)}, f32[8,704]{1,...) custom-call(f32[4,128,704]{2,1,0:T(8,128)} %copy-done.13, f32[4,128,704]{2,1,0:T(8,128)} %copy-done.1, ...), custom_call_target="tpu_custom_call" | custom-call | flops 1000 | bytes 1000 | tf_op jit(solution)/shard_map/recur_backward/pallas_call | solution.py:799
  302.4 20.9 %collective-permute-done.32 = bf16[256,2048]{1,0:T(8,128)(2,1)S(1)} collective-permute-done((bf16[256,2048]{1,0:T(8,128)(2,1)S(1)}, bf16[256,2048]{1,0:T(8,128)(2,1)S(1)}, u32[]{:S(2)}, u32[]{:S(2)}) %collective-permute-start.32) | collective-permute-done | bytes 1048608 | tf_op jit(solution)/shard_map/ppermute | solution.py:39
  325.2 6.2 %pad_maximum_fusion = bf16[4,512,2048]{2,1,0:T(8,128)(2,1)} fusion(bf16[1,512,2048]{2,1,0:T(8,128)(2,1)S(1)} %maximum_bitcast_fusion, bf16[1,512,2048]{2,1,0:T(8,128)(2,1)} %bitcast.41, bf16[1,512,2048]{2,1,0:T(8,128)(2,1)} %bitcast.40, bf16[1,512,2048]{2,1,0:T(8,128)(2,1)S(1)} %bitcast.177), kind=kLoop, calls=%fused_computation | loop fusion | flops 12582912 | bytes 16777216 | tf_op jit(solution)/shard_map/stack | solution.py:63
  334.8 10.7 %collective-permute-done.35 = bf16[8,176,176]{2,1,0:T(8,128)(2,1)S(1)} collective-permute-done((bf16[8,176,176]{2,1,0:T(8,128)(2,1)S(1)}, bf16[8,176,176]{2,1,0:T(8,128)(2,1)S(1)}, u32[]{:S(2)}, u32[]{:S(2)}) %collective-permute-start.35) | collective-permute-done | bytes 495648 | tf_op jit(solution)/shard_map/ppermute | solution.py:39
  367.2 94.8 %dense_weight_grads.1 = (bf16[2048,768]{1,0:T(8,128)(2,1)}, bf16[2048,768]{1,0:T(8,128)(2,1)}, bf16[768,2048]{1,0:T(8,128)(2,1)}) custom-call(s32[2]{0:T(128)} %pad_add_fusion.2.core_ref, bf16[4,4,128,2048]{3,2,1,0:T(8,128)(2,1)} %bitcast.53.mine_ref, bf16[4,4,128,2048]{3,2,1,0:T(8,128)(2,1)} %bitcast.54.theirs_ref, bf16[4,2,4,128,2048]{4,3,2,1,0:T(8,128)(2,1)} %bitcast.166, ...), custom_call_target="tpu_custom_call" | custom-call | flops 1000 | bytes 1000 | tf_op jit(solution)/shard_map/dense_weight_grads/pallas_call | solution.py:197
  474.0 8.4 %joined.3 = f32[2048,1536]{1,0:T(8,128)} custom-call(s32[2]{0:T(128)S(1)} %copy-done.16, bf16[2048,768]{1,0:T(8,128)(2,1)S(1)} %copy-done.10, bf16[2048,768]{1,0:T(8,128)(2,1)} %collective-permute-done.40.theirs_ref), custom_call_target="tpu_custom_call" | custom-call | bytes 18874368 | tf_op jit(solution)/shard_map/joined/pallas_call | solution.py:261
  487.5 8.7 %joined.4 = f32[2048,1536]{1,0:T(8,128)} custom-call(s32[2]{0:T(128)S(1)} %copy-done.16, bf16[2048,768]{1,0:T(8,128)(2,1)S(1)} %copy-done.9, bf16[2048,768]{1,0:T(8,128)(2,1)} %collective-permute-done.42.theirs_ref), custom_call_target="tpu_custom_call" | custom-call | bytes 18874368 | tf_op jit(solution)/shard_map/joined/pallas_call | solution.py:261
  496.4 7.0 %joined.5 = f32[2,768,2048]{2,1,0:T(8,128)} custom-call(s32[2]{0:T(128)S(1)} %copy-done.16, bf16[768,2048]{1,0:T(8,128)(2,1)S(1)} %copy-done.8, bf16[768,2048]{1,0:T(8,128)(2,1)} %collective-permute-done.44.theirs_ref), custom_call_target="tpu_custom_call" | custom-call | bytes 18874368 | tf_op jit(solution)/shard_map/joined/pallas_call | solution.py:261
  506.1 34.3 %collective-permute-done.48 = bf16[8,176,176]{2,1,0:T(8,128)(2,1)S(1)} collective-permute-done((bf16[8,176,176]{2,1,0:T(8,128)(2,1)S(1)}, bf16[8,176,176]{2,1,0:T(8,128)(2,1)S(1)}, u32[]{:S(2)}, u32[]{:S(2)}) %collective-permute-start.48) | collective-permute-done | bytes 495648 | tf_op jit(solution)/shard_map/ppermute | solution.py:39
  548.1 8.7 %slice_convert_fusion = (f32[704,2048]{1,0:T(8,128)}, f32[2048,704]{0,1:T(8,128)}) fusion(bf16[1408,2048]{1,0:T(8,128)(2,1)} %all-gather.11.cloned.1.call-done), kind=kLoop, calls=%fused_computation.17 | loop fusion | flops 2883584 | bytes 17301504 | tf_op jit(solution)/shard_map/convert_element_type | solution.py:1044
  (312 shorter events, 171.2 us)
Async XLA Ops:
  7.2 163.6 %all-gather.5.cloned.1.call-start = ((), (), s32[]{:S(2)}) async-start(), calls=%async_computation.2 | async-start | bytes 17301504 | tf_op jit(solution)/shard_map/all_gather | solution.py:941
  7.9 241.0 %all-gather.7.cloned.1.call-start = ((), (), s32[]{:S(2)}) async-start(), calls=%async_computation.3 | async-start | bytes 2621440 | tf_op jit(solution)/shard_map/all_gather | solution.py:961
  11.0 26.9 %collective-permute-start.1 = (bf16[128,2048]{1,0:T(8,128)(2,1)}, bf16[128,2048]{1,0:T(8,128)(2,1)S(1)}, u32[]{:S(2)}, u32[]{:S(2)}) collective-permute-start(bf16[128,2048]{1,0:T(8,128)(2,1)} %refs_0_), channel_id=1, source_target_pairs={{0,2},{1,3},{2,0},{3,1},{4,6},{5,7},{6,4},{7,5},{8,10},{9,11},{10,... | collective-permute-start | bytes 1572872 | tf_op jit(solution)/shard_map/ppermute | solution.py:39
  12.5 26.9 %collective-permute-start.2 = (bf16[128,2048]{1,0:T(8,128)(2,1)}, bf16[128,2048]{1,0:T(8,128)(2,1)S(1)}, u32[]{:S(2)}, u32[]{:S(2)}) collective-permute-start(bf16[128,2048]{1,0:T(8,128)(2,1)} %refs_0_), channel_id=1, source_target_pairs={{0,3},{1,2},{2,1},{3,0},{4,7},{5,6},{6,5},{7,4},{8,11},{9,10},{10,... | collective-permute-start | bytes 1572872 | tf_op jit(solution)/shard_map/ppermute | solution.py:39
  95.9 26.1 %collective-permute-start.13 = (bf16[128,2048]{1,0:T(8,128)(2,1)S(1)}, bf16[128,2048]{1,0:T(8,128)(2,1)S(1)}, u32[]{:S(2)}, u32[]{:S(2)}) collective-permute-start(bf16[128,2048]{1,0:T(8,128)(2,1)S(1)} %get-tuple-element.203), channel_id=1, source_target_pairs={{0,1},{1,0},{2,3},{3,2},{4,5},{5,4},{6,7},{7,6},{8,9},{9,8},{10,11... | collective-permute-start | bytes 1572872 | tf_op jit(solution)/shard_map/ppermute | solution.py:39
  96.7 26.7 %collective-permute-start.14 = (bf16[128,2048]{1,0:T(8,128)(2,1)S(1)}, bf16[128,2048]{1,0:T(8,128)(2,1)S(1)}, u32[]{:S(2)}, u32[]{:S(2)}) collective-permute-start(bf16[128,2048]{1,0:T(8,128)(2,1)S(1)} %get-tuple-element.205), channel_id=1, source_target_pairs={{0,2},{1,3},{2,0},{3,1},{4,6},{5,7},{6,4},{7,5},{8,10},{9,11},{10,... | collective-permute-start | bytes 1572872 | tf_op jit(solution)/shard_map/ppermute | solution.py:39
  97.2 43.7 %collective-permute-start.15 = (bf16[128,2048]{1,0:T(8,128)(2,1)S(1)}, bf16[128,2048]{1,0:T(8,128)(2,1)S(1)}, u32[]{:S(2)}, u32[]{:S(2)}) collective-permute-start(bf16[128,2048]{1,0:T(8,128)(2,1)S(1)} %get-tuple-element.204), channel_id=1, source_target_pairs={{0,3},{1,2},{2,1},{3,0},{4,7},{5,6},{6,5},{7,4},{8,11},{9,10},{10,... | collective-permute-start | bytes 1572872 | tf_op jit(solution)/shard_map/ppermute | solution.py:39
  146.0 23.9 %collective-permute-start.18 = (bf16[128,2048]{1,0:T(8,128)(2,1)S(1)}, bf16[128,2048]{1,0:T(8,128)(2,1)S(1)}, u32[]{:S(2)}, u32[]{:S(2)}) collective-permute-start(bf16[128,2048]{1,0:T(8,128)(2,1)S(1)} %get-tuple-element.190), channel_id=1, source_target_pairs={{0,3},{1,2},{2,1},{3,0},{4,7},{5,6},{6,5},{7,4},{8,11},{9,10},{10,... | collective-permute-start | bytes 1572872 | tf_op jit(solution)/shard_map/ppermute | solution.py:39
  148.6 208.4 %reduce-scatter.3.cloned.1.call-start = ((), (), s32[]{:S(2)}) async-start(), calls=%async_computation.4 | async-start | bytes 6488064 | tf_op jit(solution)/shard_map/reduce_scatter | solution.py:983
  248.9 48.9 %collective-permute-start.28 = (bf16[512,2048]{1,0:T(8,128)(2,1)}, bf16[512,2048]{1,0:T(8,128)(2,1)}, u32[]{:S(2)}, u32[]{:S(2)}) collective-permute-start(bf16[512,2048]{1,0:T(8,128)(2,1)} %all-gather.7.cloned.1.call-done), channel_id=1, source_target_pairs={{0,1},{1,0},{2,3},{3,2},{4,5},{5,4},{6,7},{7,6},{8,9},{9,8},{10,11... | collective-permute-start | bytes 6291464 | tf_op jit(solution)/shard_map/ppermute | solution.py:39
  251.6 46.2 %collective-permute-start.29 = (bf16[512,2048]{1,0:T(8,128)(2,1)}, bf16[512,2048]{1,0:T(8,128)(2,1)}, u32[]{:S(2)}, u32[]{:S(2)}) collective-permute-start(bf16[512,2048]{1,0:T(8,128)(2,1)} %all-gather.7.cloned.1.call-done), channel_id=1, source_target_pairs={{0,2},{1,3},{2,0},{3,1},{4,6},{5,7},{6,4},{7,5},{8,10},{9,11},{10,... | collective-permute-start | bytes 6291464 | tf_op jit(solution)/shard_map/ppermute | solution.py:39
  277.4 188.5 %reduce-scatter.5.cloned.1.call-start = ((), (), s32[]{:S(2)}) async-start(), calls=%async_computation.5 | async-start | bytes 3244032 | tf_op jit(solution)/shard_map/reduce_scatter | solution.py:1018
  299.2 24.1 %collective-permute-start.32 = (bf16[256,2048]{1,0:T(8,128)(2,1)S(1)}, bf16[256,2048]{1,0:T(8,128)(2,1)S(1)}, u32[]{:S(2)}, u32[]{:S(2)}) collective-permute-start(bf16[256,2048]{1,0:T(8,128)(2,1)S(1)} %slice.278), channel_id=1, source_target_pairs={{0,1},{1,0},{2,3},{3,2},{4,5},{5,4},{6,7},{7,6},{8,9},{9,8},{10,11... | collective-permute-start | bytes 3145736 | tf_op jit(solution)/shard_map/ppermute | solution.py:39
  301.0 24.0 %collective-permute-start.33 = (bf16[256,2048]{1,0:T(8,128)(2,1)S(1)}, bf16[256,2048]{1,0:T(8,128)(2,1)S(1)}, u32[]{:S(2)}, u32[]{:S(2)}) collective-permute-start(bf16[256,2048]{1,0:T(8,128)(2,1)S(1)} %slice.279), channel_id=1, source_target_pairs={{0,2},{1,3},{2,0},{3,1},{4,6},{5,7},{6,4},{7,5},{8,10},{9,11},{10,... | collective-permute-start | bytes 3145736 | tf_op jit(solution)/shard_map/ppermute | solution.py:39
  331.3 25.7 %collective-permute-start.34 = (bf16[4,512,2048]{2,1,0:T(8,128)(2,1)}, bf16[4,512,2048]{2,1,0:T(8,128)(2,1)}, u32[]{:S(2)}, u32[]{:S(2)}) collective-permute-start(bf16[4,512,2048]{2,1,0:T(8,128)(2,1)} %pad_maximum_fusion), channel_id=1, source_target_pairs={{0,4},{4,0},{8,12},{12,8},{16,20},{20,16},{24,28},{28,24},{1,5},{5... | collective-permute-start | bytes 25165832 | tf_op jit(solution)/shard_map/ppermute | solution.py:39
  357.1 191.0 %all-gather.11.cloned.1.call-start = ((), (), s32[]{:S(2)}) async-start(), calls=%async_computation.7 | async-start | bytes 6488064 | tf_op jit(solution)/shard_map/all_gather | solution.py:1017
  357.7 199.1 %all-gather.9.cloned.1.call-start = ((), (), s32[]{:S(2)}) async-start(), calls=%async_computation.6 | async-start | bytes 3244032 | tf_op jit(solution)/shard_map/all_gather | solution.py:1037
  361.5 100.5 %collective-permute-start.36 = (bf16[256,2048]{1,0:T(8,128)(2,1)}, bf16[256,2048]{1,0:T(8,128)(2,1)S(1)}, u32[]{:S(2)}, u32[]{:S(2)}) collective-permute-start(bf16[256,2048]{1,0:T(8,128)(2,1)} %get-tuple-element.195), channel_id=1, source_target_pairs={{0,1},{1,0},{2,3},{3,2},{4,5},{5,4},{6,7},{7,6},{8,9},{9,8},{10,11... | collective-permute-start | bytes 3145736 | tf_op jit(solution)/shard_map/ppermute | solution.py:39
  363.0 99.0 %collective-permute-start.37 = (bf16[256,2048]{1,0:T(8,128)(2,1)}, bf16[256,2048]{1,0:T(8,128)(2,1)}, u32[]{:S(2)}, u32[]{:S(2)}) collective-permute-start(bf16[256,2048]{1,0:T(8,128)(2,1)} %get-tuple-element.196), channel_id=1, source_target_pairs={{0,2},{1,3},{2,0},{3,1},{4,6},{5,7},{6,4},{7,5},{8,10},{9,11},{10,... | collective-permute-start | bytes 3145736 | tf_op jit(solution)/shard_map/ppermute | solution.py:39
  364.6 97.4 %collective-permute-start.38 = (bf16[256,2048]{1,0:T(8,128)(2,1)}, bf16[256,2048]{1,0:T(8,128)(2,1)}, u32[]{:S(2)}, u32[]{:S(2)}) collective-permute-start(bf16[256,2048]{1,0:T(8,128)(2,1)} %get-tuple-element.197), channel_id=1, source_target_pairs={{0,3},{1,2},{2,1},{3,0},{4,7},{5,6},{6,5},{7,4},{8,11},{9,10},{10,... | collective-permute-start | bytes 3145736 | tf_op jit(solution)/shard_map/ppermute | solution.py:39
  365.6 100.2 %collective-permute-start.39 = (bf16[8,176,176]{2,1,0:T(8,128)(2,1)S(1)}, bf16[8,176,176]{2,1,0:T(8,128)(2,1)S(1)}, u32[]{:S(2)}, u32[]{:S(2)}) collective-permute-start(bf16[8,176,176]{2,1,0:T(8,128)(2,1)S(1)} %add.205), channel_id=1, source_target_pairs={{0,8},{4,12},{8,0},{12,4},{16,24},{20,28},{24,16},{28,20},{1,9},{5... | collective-permute-start | bytes 1486856 | tf_op jit(solution)/shard_map/ppermute | solution.py:39
  466.3 30.0 %collective-permute-start.44 = (bf16[768,2048]{1,0:T(8,128)(2,1)}, bf16[768,2048]{1,0:T(8,128)(2,1)}, u32[]{:S(2)}, u32[]{:S(2)}) collective-permute-start(bf16[768,2048]{1,0:T(8,128)(2,1)} %get-tuple-element.169.mine_ref), channel_id=1, source_target_pairs={{0,4},{4,0},{8,12},{12,8},{16,20},{20,16},{24,28},{28,24},{1,5},{5... | collective-permute-start | bytes 9437192 | tf_op jit(solution)/shard_map/ppermute | solution.py:39
  482.7 57.7 %collective-permute-start.48 = (bf16[8,176,176]{2,1,0:T(8,128)(2,1)S(1)}, bf16[8,176,176]{2,1,0:T(8,128)(2,1)S(1)}, u32[]{:S(2)}, u32[]{:S(2)}) collective-permute-start(bf16[8,176,176]{2,1,0:T(8,128)(2,1)S(1)} %add.218), channel_id=1, source_target_pairs={{0,16},{4,20},{8,24},{12,28},{16,0},{20,4},{24,8},{28,12},{1,17},{... | collective-permute-start | bytes 1486856 | tf_op jit(solution)/shard_map/ppermute | solution.py:39
  503.4 37.2 %collective-permute-start.46 = (f32[10,704]{1,0:T(8,128)S(1)}, f32[10,704]{1,0:T(8,128)S(1)}, u32[]{:S(2)}, u32[]{:S(2)}) collective-permute-start(f32[10,704]{1,0:T(8,128)S(1)} %fusion.43), channel_id=1, source_target_pairs={{0,8},{4,12},{8,0},{12,4},{16,24},{20,28},{24,16},{28,20},{1,9},{5... | collective-permute-start | bytes 84488 | tf_op jit(solution)/shard_map/ppermute | solution.py:39
  (71 other events, 828.9 us)
Sparse Core Ops, SparseCore 0:
  10.9 146.7 all-gather.4
  159.8 46.6 all-gather.6
  277.5 68.2 reduce-scatter.2
  357.2 53.7 reduce-scatter.4
  412.5 59.5 all-gather.10
  473.6 64.6 all-gather.8

commit v6 on v5

--- a/solution.py
+++ b/solution.py
@@ -998,7 +998,6 @@
         rate_dense,
         input_dense,
     )
-    rows_mine, rim_grad = rows_spread(rim_grad)
     fixed = tail + from_neighbour(rim_grad, 1)
     low_rows = conv_low.reshape(group, width)
     rate_w = diagonal_blocks(product_left_t(low_rows, rate_low.reshape(group, width)), blocks_n)
@@ -1007,9 +1006,10 @@
         inner_grad, fixed.astype(bf16)[None], (tp_size - 1, length - TILE, 0)
     ).reshape(group, width)
     in_full = product_left_t(inner_grad, normed).astype(bf16)
-    block_full = jnp.concatenate([rate_w, input_w]).astype(bf16)
-    block_sum = block_full + swap(block_full, "seq", 1)
+    ours, theirs = both_halves(rate_w.astype(bf16), input_w.astype(bf16), core)
+    block_sum = ours + swap(theirs, "seq", 1)
     normed_part = (product(inner_grad, in_t) + product(branch_pre_grad, branch_t)).astype(bf16)
+    rows_mine, normed_part, in_full = rows_spread(normed_part, in_full)
     rows_theirs = swap(rows_mine, "seq", 1)
     normed_part, in_full, pair_part, rows_mine, rows_theirs, block_sum, dense_part = tied(
         normed_part, in_full, pair_part, rows_mine, rows_theirs, block_sum, dense_part
@@ -1063,7 +1063,9 @@
     gate_sum, up_sum, down_sum = whole
     sums, gain_sum = small[:-2, :width], small[-2:, :gain_share]
     decay_sum = 8.0 * jax.nn.sigmoid(-decay_param) * sums[2]
-    rate_sum, input_sum = block_sum[:blocks_n].astype(f32), block_sum[blocks_n:].astype(f32)
+    rate_sum, input_sum = both_halves(block_sum, swap(block_sum, "seq", 1), core)
+    rate_sum, input_sum = rate_sum.astype(f32), input_sum.astype(f32)
+    in_sum, out_sum, branch_sum = tied(in_sum, out_sum, branch_sum)
     return (
         output,
         tokens_grad,

time: 577 us -> 581 us (level)
  starting transfers between devices: 58.5 us -> 65 us
    ppermute x43 -> x44, waiting for transfers between devices: 186 us -> 176 us  [swap(): return lax.ppermute(value, axis, [(i, i ^ bit) for i in range(count)])]
    reduce_scatter x1, waiting for transfers between devices: 0.01 us -> 7.59 us  [shards(): lax.psum_scatter(pair_full, 'seq', scatter_dimension=0, tiled=True)]
    ppermute x43 -> x44, starting transfers between devices: 53.8 us -> 57.2 us  [swap(): return lax.ppermute(value, axis, [(i, i ^ bit) for i in range(count)])]
    unnamed x91 -> x96, local copies, waits for them, and re-layouts: 12.8 us -> 13.5 us
  transfers between devices with their start and end apart: 55 -> 56, of which waited for: 25 -> 25; matrix products, arithmetic and copies ran while one was open for 15% -> 15% of each run, Pallas kernels for 36% -> 36%
where the time goes in v6:
time: 581 us; the launch traced here: 573 us
  Pallas kernels  204 us (35%)
  waiting for transfers between devices  185 us (32%)
  starting transfers between devices  65 us (11%)
  other arithmetic  44.5 us (8%)
  local copies, waits for them, and re-layouts  37.3 us (6%)
  matrix products  21.8 us (4%)
  between operations  15.5 us (3%)
    ppermute x44, waiting for transfers between devices, swap(): return lax.ppermute(value, axis, [(i, i ^ bit) for i in range(count)])  176 us
    pallas_call x1, Pallas kernels, dense_weight_grads(): pl.pallas_call(kernel, grid_spec=pltpu.PrefetchScalarGridSpec(num_scalar_...  94.6 us
    ppermute x44, starting transfers between devices, swap(): return lax.ppermute(value, axis, [(i, i ^ bit) for i in range(count)])  57.2 us
    pallas_call x1, Pallas kernels, dense_rows(): pl.pallas_call(kernel, grid_spec=pltpu.PrefetchScalarGridSpec(num_scalar_...  24.9 us
    pallas_call x3, Pallas kernels, joined(): pl.pallas_call(kernel, grid_spec=pltpu.PrefetchScalarGridSpec(num_scalar_...  24.2 us
    pallas_call x1, Pallas kernels, recur_backward(): pl.pallas_call(backward_kernel, grid_spec=pltpu.PrefetchScalarGridSpec(nu...  19.3 us
    pallas_call x1, Pallas kernels, recur_forward(): pl.pallas_call(forward_kernel, grid_spec=pltpu.PrefetchScalarGridSpec(num...  15.2 us
    unnamed x96, local copies, waits for them, and re-layouts  13.5 us
  transfers between devices with their start and end apart: 56, of which 25 were waited for; matrix products, arithmetic and copies ran while one was open for 15% of the time, Pallas kernels for 36%

profile of v6, /device:TPU:0, one launch (start us, length us, event | category | flops | bytes accessed | tf_op | source)
XLA Modules:
  0.0 573.0 jit_solution(8745651924307161642)
XLA Ops:
  13.9 10.3 %collective-permute-done.refs_1_ = bf16[128,2048]{1,0:T(8,128)(2,1)S(1)} collective-permute-done((bf16[128,2048]{1,0:T(8,128)(2,1)}, bf16[128,2048]{1,0:T(8,128)(2,1)S(1)}, u32[]{:S(2)}, u32[]{:S(2)}) %collective-permute-start) | collective-permute-done | bytes 524320 | tf_op jit(solution)/shard_map/ppermute | solution.py:39
  41.9 7.0 %norm_project.1 = (bf16[512,2048]{1,0:T(8,128)(2,1)}, f32[4,128,704]{2,1,0:T(8,128)S(1)}) custom-call(s32[1]{0:T(128)} %bitcast.place_ref, bf16[128,2048]{1,0:T(8,128)(2,1)S(1)} %copy-done.7, bf16[128,2048]{1,0:T(8,128)(2,1)S(1)} %collective-permute-done.refs_1_, bf16[128,2048]{1,0:T(8,128)(2,1)S(1)} %collective-permute-done.1.refs_2_, ...), custom_call_target="tpu_custom_call" | custom-call | tf_op jit(solution)/shard_map/norm_project/pallas_call | solution.py:725
  53.8 15.2 %recur_forward.1 = (f32[4,128,704]{2,1,0:T(8,128)}, bf16[4,128,704]{2,1,0:T(8,128)(2,1)S(1)}, f32[4,128,704]{2,1,0:T(8,128)}, f32[4,128,704]{2,1,0:T(8,128)}, f3...) custom-call(f32[4,128,704]{2,1,0:T(8,128)} %copy-done, ...), custom_call_target="tpu_custom_call" | custom-call | tf_op jit(solution)/shard_map/recur_forward/pallas_call | solution.py:750
  91.2 6.4 %mix_out.1 = (f32[4,128,704]{2,1,0:T(8,128)S(1)}, bf16[4,128,704]{2,1,0:T(8,128)(2,1)S(1)}, bf16[4,128,2048]{2,1,0:T(8,128)(2,1)}) custom-call(f32[4,128,704]{2,1,0:T(8,128)S(1)} %copy-done.14, f32[4,128,704]{2,1,0:T(8,128)} %get-tuple-element.120.keep_ref, f32[4,128,704]{2,1,0:T(8,128)} %bitcast.139, f32[1,704]{1,0:T(1,128)S(1)} %get-tuple-element.194.in_ref, ...), custom_call_target="tpu_custom_call" | custom-call | tf_op jit(solution)/shard_map/mix_out/pallas_call | solution.py:376
  103.2 23.4 %collective-permute-done.15 = bf16[128,2048]{1,0:T(8,128)(2,1)S(1)} collective-permute-done((bf16[128,2048]{1,0:T(8,128)(2,1)S(1)}, bf16[128,2048]{1,0:T(8,128)(2,1)S(1)}, u32[]{:S(2)}, u32[]{:S(2)}) %collective-permute-start.15) | collective-permute-done | bytes 524320 | tf_op jit(solution)/shard_map/ppermute | solution.py:39
  126.6 8.8 %collective-permute-done.14 = bf16[128,2048]{1,0:T(8,128)(2,1)S(1)} collective-permute-done((bf16[128,2048]{1,0:T(8,128)(2,1)S(1)}, bf16[128,2048]{1,0:T(8,128)(2,1)S(1)}, u32[]{:S(2)}, u32[]{:S(2)}) %collective-permute-start.14) | collective-permute-done | bytes 524320 | tf_op jit(solution)/shard_map/ppermute | solution.py:39
  148.1 11.1 %collective-permute-done.16 = bf16[128,2048]{1,0:T(8,128)(2,1)} collective-permute-done((bf16[128,2048]{1,0:T(8,128)(2,1)S(1)}, bf16[128,2048]{1,0:T(8,128)(2,1)}, u32[]{:S(2)}, u32[]{:S(2)}) %collective-permute-start.16) | collective-permute-done | bytes 524320 | tf_op jit(solution)/shard_map/ppermute | solution.py:39
  161.1 7.0 %collective-permute-done.17 = bf16[128,2048]{1,0:T(8,128)(2,1)} collective-permute-done((bf16[128,2048]{1,0:T(8,128)(2,1)S(1)}, bf16[128,2048]{1,0:T(8,128)(2,1)}, u32[]{:S(2)}, u32[]{:S(2)}) %collective-permute-start.17) | collective-permute-done | bytes 524320 | tf_op jit(solution)/shard_map/ppermute | solution.py:39
  171.9 24.9 %dense_rows.1 = (bf16[512,1536]{1,0:T(8,128)(2,1)S(1)}, bf16[512,2048]{1,0:T(8,128)(2,1)S(1)}) custom-call(s32[1]{0:T(128)} %bitcast.19.place_ref, bf16[512,2048]{1,0:T(8,128)(2,1)} %bitcast.24.x_ref, bf16[4096,2048]{1,0:T(8,128)(2,1)} %all-gather.5.cloned.1.call-done.c_ref, bf16[2048,1536]{1,0:T(8,128)(2,1)} %gate_ref.3, bf16[2048,1536]{1,0:T(8,128)(2,1)} %up_ref.3, ...), custom_call_target="tpu_custom_call" | custom-call | tf_op jit(solution)/shard_map/dense_rows/pallas_call | solution.py:307
  205.8 7.0 %collective-permute-done.21 = bf16[128,2048]{1,0:T(8,128)(2,1)S(1)} collective-permute-done((bf16[128,2048]{1,0:T(8,128)(2,1)S(1)}, bf16[128,2048]{1,0:T(8,128)(2,1)S(1)}, u32[]{:S(2)}, u32[]{:S(2)}) %collective-permute-start.21) | collective-permute-done | bytes 524320 | tf_op jit(solution)/shard_map/ppermute | solution.py:39
  212.8 7.7 %collective-permute-done.20 = bf16[128,2048]{1,0:T(8,128)(2,1)S(1)} collective-permute-done((bf16[128,2048]{1,0:T(8,128)(2,1)S(1)}, bf16[128,2048]{1,0:T(8,128)(2,1)S(1)}, u32[]{:S(2)}, u32[]{:S(2)}) %collective-permute-start.20) | collective-permute-done | bytes 524320 | tf_op jit(solution)/shard_map/ppermute | solution.py:39
  228.5 11.7 %collective-permute-done.22 = bf16[128,2048]{1,0:T(8,128)(2,1)} collective-permute-done((bf16[128,2048]{1,0:T(8,128)(2,1)}, bf16[128,2048]{1,0:T(8,128)(2,1)}, u32[]{:S(2)}, u32[]{:S(2)}) %collective-permute-start.22) | collective-permute-done | bytes 524320 | tf_op jit(solution)/shard_map/ppermute | solution.py:39
  242.0 9.5 %collective-permute-done.23 = bf16[128,2048]{1,0:T(8,128)(2,1)} collective-permute-done((bf16[128,2048]{1,0:T(8,128)(2,1)}, bf16[128,2048]{1,0:T(8,128)(2,1)}, u32[]{:S(2)}, u32[]{:S(2)}) %collective-permute-start.23) | collective-permute-done | bytes 524320 | tf_op jit(solution)/shard_map/ppermute | solution.py:39
  256.3 8.0 %mix_back.1 = (f32[4,128,704]{2,1,0:T(8,128)S(1)}, bf16[4,128,704]{2,1,0:T(8,128)(2,1)S(1)}, f32[1,704]{1,0:T(1,128)S(1)}) custom-call(bf16[4,128,2048]{2,1,0:T(8,128)(2,1)} %bitcast_dynamic-update-slice_fusion.mid_ref, bf16[704,2048]{1,0:T(8,128)(2,1)} %out_ref.3, f32[4,128,704]{2,1,0:T(8,128)S(1)} %bitcast.140, f32[4,128,704]{2,1,0:T(8,128)} %copy-done.1, ...), custom_call_target="tpu_custom_call" | custom-call | tf_op jit(solution)/shard_map/mix_back/pallas_call | solution.py:428
  282.1 19.3 %recur_backward.1 = (bf16[4,128,704]{2,1,0:T(8,128)(2,1)S(1)}, bf16[4,128,704]{2,1,0:T(8,128)(2,1)S(1)}, bf16[4,128,704]{2,1,0:T(8,128)(2,1)S(1)}, f32[8,704]{1,...) custom-call(f32[4,128,704]{2,1,0:T(8,128)} %copy-done.13, f32[4,128,704]{2,1,0:T(8,128)} %copy-done.1, ...), custom_call_target="tpu_custom_call" | custom-call | flops 1000 | bytes 1000 | tf_op jit(solution)/shard_map/recur_backward/pallas_call | solution.py:799
  321.0 19.1 %collective-permute-done.33 = bf16[256,2048]{1,0:T(8,128)(2,1)S(1)} collective-permute-done((bf16[256,2048]{1,0:T(8,128)(2,1)S(1)}, bf16[256,2048]{1,0:T(8,128)(2,1)S(1)}, u32[]{:S(2)}, u32[]{:S(2)}) %collective-permute-start.33) | collective-permute-done | bytes 1048608 | tf_op jit(solution)/shard_map/ppermute | solution.py:39
  353.3 10.1 %collective-permute-done.35 = bf16[4,176,176]{2,1,0:T(8,128)(2,1)S(1)} collective-permute-done((bf16[4,176,176]{2,1,0:T(8,128)(2,1)S(1)}, bf16[4,176,176]{2,1,0:T(8,128)(2,1)S(1)}, u32[]{:S(2)}, u32[]{:S(2)}) %collective-permute-start.35) | collective-permute-done | bytes 247840 | tf_op jit(solution)/shard_map/ppermute | solution.py:39
  363.7 7.6 %reduce-scatter.3.cloned.1.call-done = bf16[176,2048]{1,0:T(8,128)(2,1)} async-done(((bf16[1408,2048]{1,0:T(8,128)(2,1)}), bf16[176,2048]{1,0:T(8,128)(2,1)}) %reduce-scatter.3.cloned.1.call-update) | async-done | bytes 720912 | tf_op jit(solution)/shard_map/reduce_scatter | solution.py:983
  380.9 94.6 %dense_weight_grads.1 = (bf16[2048,768]{1,0:T(8,128)(2,1)}, bf16[2048,768]{1,0:T(8,128)(2,1)}, bf16[768,2048]{1,0:T(8,128)(2,1)}) custom-call(s32[2]{0:T(128)} %pad_add_fusion.2.core_ref, bf16[4,4,128,2048]{3,2,1,0:T(8,128)(2,1)} %bitcast.150, bf16[4,4,128,2048]{3,2,1,0:T(8,128)(2,1)} %bitcast.54.theirs_ref, bf16[4,2,4,128,2048]{4,3,2,1,0:T(8,128)(2,1)} %bitcast.149, ...), custom_call_target="tpu_custom_call" | custom-call | flops 1000 | bytes 1000 | tf_op jit(solution)/shard_map/dense_weight_grads/pallas_call | solution.py:197
  487.4 8.4 %joined.3 = f32[2048,1536]{1,0:T(8,128)} custom-call(s32[2]{0:T(128)S(1)} %copy-done.16, bf16[2048,768]{1,0:T(8,128)(2,1)S(1)} %copy-done.10, bf16[2048,768]{1,0:T(8,128)(2,1)} %collective-permute-done.40.theirs_ref), custom_call_target="tpu_custom_call" | custom-call | bytes 18874368 | tf_op jit(solution)/shard_map/joined/pallas_call | solution.py:261
  500.7 8.7 %joined.4 = f32[2048,1536]{1,0:T(8,128)} custom-call(s32[2]{0:T(128)S(1)} %copy-done.16, bf16[2048,768]{1,0:T(8,128)(2,1)S(1)} %copy-done.9, bf16[2048,768]{1,0:T(8,128)(2,1)} %collective-permute-done.42.theirs_ref), custom_call_target="tpu_custom_call" | custom-call | bytes 18874368 | tf_op jit(solution)/shard_map/joined/pallas_call | solution.py:261
  509.5 23.7 %collective-permute-done.48 = bf16[4,176,176]{2,1,0:T(8,128)(2,1)S(1)} collective-permute-done((bf16[4,176,176]{2,1,0:T(8,128)(2,1)S(1)}, bf16[4,176,176]{2,1,0:T(8,128)(2,1)S(1)}, u32[]{:S(2)}, u32[]{:S(2)}) %collective-permute-start.48) | collective-permute-done | bytes 247840 | tf_op jit(solution)/shard_map/ppermute | solution.py:39
  533.4 7.1 %joined.5 = f32[2,768,2048]{2,1,0:T(8,128)} custom-call(s32[2]{0:T(128)S(1)} %copy-done.16, bf16[768,2048]{1,0:T(8,128)(2,1)S(1)} %copy-done.8, bf16[768,2048]{1,0:T(8,128)(2,1)} %collective-permute-done.44.theirs_ref), custom_call_target="tpu_custom_call" | custom-call | bytes 18874368 | tf_op jit(solution)/shard_map/joined/pallas_call | solution.py:261
  552.2 8.7 %slice_convert_fusion = (f32[704,2048]{1,0:T(8,128)}, f32[704,2048]{1,0:T(8,128)}) fusion(bf16[1408,2048]{1,0:T(8,128)(2,1)} %all-gather.11.cloned.1.call-done), kind=kLoop, calls=%fused_computation.16 | loop fusion | flops 2883584 | bytes 17301504 | tf_op jit(solution)/shard_map/convert_element_type | solution.py:1044
  (321 shorter events, 192.3 us)
Async XLA Ops:
  7.2 164.7 %all-gather.5.cloned.1.call-start = ((), (), s32[]{:S(2)}) async-start(), calls=%async_computation.2 | async-start | bytes 17301504 | tf_op jit(solution)/shard_map/all_gather | solution.py:941
  7.9 246.3 %all-gather.7.cloned.1.call-start = ((), (), s32[]{:S(2)}) async-start(), calls=%async_computation.3 | async-start | bytes 2621440 | tf_op jit(solution)/shard_map/all_gather | solution.py:961
  11.0 26.8 %collective-permute-start.1 = (bf16[128,2048]{1,0:T(8,128)(2,1)}, bf16[128,2048]{1,0:T(8,128)(2,1)S(1)}, u32[]{:S(2)}, u32[]{:S(2)}) collective-permute-start(bf16[128,2048]{1,0:T(8,128)(2,1)} %refs_0_), channel_id=1, source_target_pairs={{0,2},{1,3},{2,0},{3,1},{4,6},{5,7},{6,4},{7,5},{8,10},{9,11},{10,... | collective-permute-start | bytes 1572872 | tf_op jit(solution)/shard_map/ppermute | solution.py:39
  12.5 26.9 %collective-permute-start.2 = (bf16[128,2048]{1,0:T(8,128)(2,1)}, bf16[128,2048]{1,0:T(8,128)(2,1)S(1)}, u32[]{:S(2)}, u32[]{:S(2)}) collective-permute-start(bf16[128,2048]{1,0:T(8,128)(2,1)} %refs_0_), channel_id=1, source_target_pairs={{0,3},{1,2},{2,1},{3,0},{4,7},{5,6},{6,5},{7,4},{8,11},{9,10},{10,... | collective-permute-start | bytes 1572872 | tf_op jit(solution)/shard_map/ppermute | solution.py:39
  99.6 27.0 %collective-permute-start.15 = (bf16[128,2048]{1,0:T(8,128)(2,1)S(1)}, bf16[128,2048]{1,0:T(8,128)(2,1)S(1)}, u32[]{:S(2)}, u32[]{:S(2)}) collective-permute-start(bf16[128,2048]{1,0:T(8,128)(2,1)S(1)} %get-tuple-element.212), channel_id=1, source_target_pairs={{0,3},{1,2},{2,1},{3,0},{4,7},{5,6},{6,5},{7,4},{8,11},{9,10},{10,... | collective-permute-start | bytes 1572872 | tf_op jit(solution)/shard_map/ppermute | solution.py:39
  99.7 35.7 %collective-permute-start.14 = (bf16[128,2048]{1,0:T(8,128)(2,1)S(1)}, bf16[128,2048]{1,0:T(8,128)(2,1)S(1)}, u32[]{:S(2)}, u32[]{:S(2)}) collective-permute-start(bf16[128,2048]{1,0:T(8,128)(2,1)S(1)} %get-tuple-element.213), channel_id=1, source_target_pairs={{0,2},{1,3},{2,0},{3,1},{4,6},{5,7},{6,4},{7,5},{8,10},{9,11},{10,... | collective-permute-start | bytes 1572872 | tf_op jit(solution)/shard_map/ppermute | solution.py:39
  100.0 40.0 %collective-permute-start.13 = (bf16[128,2048]{1,0:T(8,128)(2,1)S(1)}, bf16[128,2048]{1,0:T(8,128)(2,1)S(1)}, u32[]{:S(2)}, u32[]{:S(2)}) collective-permute-start(bf16[128,2048]{1,0:T(8,128)(2,1)S(1)} %get-tuple-element.211), channel_id=1, source_target_pairs={{0,1},{1,0},{2,3},{3,2},{4,5},{5,4},{6,7},{7,6},{8,9},{9,8},{10,11... | collective-permute-start | bytes 1572872 | tf_op jit(solution)/shard_map/ppermute | solution.py:39
  144.5 23.6 %collective-permute-start.17 = (bf16[128,2048]{1,0:T(8,128)(2,1)S(1)}, bf16[128,2048]{1,0:T(8,128)(2,1)}, u32[]{:S(2)}, u32[]{:S(2)}) collective-permute-start(bf16[128,2048]{1,0:T(8,128)(2,1)S(1)} %get-tuple-element.198), channel_id=1, source_target_pairs={{0,2},{1,3},{2,0},{3,1},{4,6},{5,7},{6,4},{7,5},{8,10},{9,11},{10,... | collective-permute-start | bytes 1572872 | tf_op jit(solution)/shard_map/ppermute | solution.py:39
  146.2 23.8 %collective-permute-start.18 = (bf16[128,2048]{1,0:T(8,128)(2,1)S(1)}, bf16[128,2048]{1,0:T(8,128)(2,1)}, u32[]{:S(2)}, u32[]{:S(2)}) collective-permute-start(bf16[128,2048]{1,0:T(8,128)(2,1)S(1)} %get-tuple-element.198), channel_id=1, source_target_pairs={{0,3},{1,2},{2,1},{3,0},{4,7},{5,6},{6,5},{7,4},{8,11},{9,10},{10,... | collective-permute-start | bytes 1572872 | tf_op jit(solution)/shard_map/ppermute | solution.py:39
  147.7 223.5 %reduce-scatter.3.cloned.1.call-start = ((), (), s32[]{:S(2)}) async-start(), calls=%async_computation.4 | async-start | bytes 6488064 | tf_op jit(solution)/shard_map/reduce_scatter | solution.py:983
  226.4 25.1 %collective-permute-start.23 = (bf16[128,2048]{1,0:T(8,128)(2,1)}, bf16[128,2048]{1,0:T(8,128)(2,1)}, u32[]{:S(2)}, u32[]{:S(2)}) collective-permute-start(bf16[128,2048]{1,0:T(8,128)(2,1)} %get-tuple-element.196), channel_id=1, source_target_pairs={{0,2},{1,3},{2,0},{3,1},{4,6},{5,7},{6,4},{7,5},{8,10},{9,11},{10,... | collective-permute-start | bytes 1572872 | tf_op jit(solution)/shard_map/ppermute | solution.py:39
  227.0 26.4 %collective-permute-start.24 = (bf16[128,2048]{1,0:T(8,128)(2,1)}, bf16[128,2048]{1,0:T(8,128)(2,1)S(1)}, u32[]{:S(2)}, u32[]{:S(2)}) collective-permute-start(bf16[128,2048]{1,0:T(8,128)(2,1)} %get-tuple-element.196), channel_id=1, source_target_pairs={{0,3},{1,2},{2,1},{3,0},{4,7},{5,6},{6,5},{7,4},{8,11},{9,10},{10,... | collective-permute-start | bytes 1572872 | tf_op jit(solution)/shard_map/ppermute | solution.py:39
  254.3 62.0 %collective-permute-start.25 = (bf16[512,2048]{1,0:T(8,128)(2,1)}, bf16[512,2048]{1,0:T(8,128)(2,1)}, u32[]{:S(2)}, u32[]{:S(2)}) collective-permute-start(bf16[512,2048]{1,0:T(8,128)(2,1)} %all-gather.7.cloned.1.call-done), channel_id=1, source_target_pairs={{0,1},{1,0},{2,3},{3,2},{4,5},{5,4},{6,7},{7,6},{8,9},{9,8},{10,11... | collective-permute-start | bytes 6291464 | tf_op jit(solution)/shard_map/ppermute | solution.py:39
  254.6 61.7 %collective-permute-start.26 = (bf16[512,2048]{1,0:T(8,128)(2,1)}, bf16[512,2048]{1,0:T(8,128)(2,1)}, u32[]{:S(2)}, u32[]{:S(2)}) collective-permute-start(bf16[512,2048]{1,0:T(8,128)(2,1)} %all-gather.7.cloned.1.call-done), channel_id=1, source_target_pairs={{0,2},{1,3},{2,0},{3,1},{4,6},{5,7},{6,4},{7,5},{8,10},{9,11},{10,... | collective-permute-start | bytes 6291464 | tf_op jit(solution)/shard_map/ppermute | solution.py:39
  305.5 174.0 %reduce-scatter.5.cloned.1.call-start = ((), (), s32[]{:S(2)}) async-start(), calls=%async_computation.5 | async-start | bytes 3244032 | tf_op jit(solution)/shard_map/reduce_scatter | solution.py:1018
  371.3 180.9 %all-gather.11.cloned.1.call-start = ((), (), s32[]{:S(2)}) async-start(), calls=%async_computation.7 | async-start | bytes 6488064 | tf_op jit(solution)/shard_map/all_gather | solution.py:1017
  371.9 189.0 %all-gather.9.cloned.1.call-start = ((), (), s32[]{:S(2)}) async-start(), calls=%async_computation.6 | async-start | bytes 3244032 | tf_op jit(solution)/shard_map/all_gather | solution.py:1037
  375.2 100.4 %collective-permute-start.38 = (bf16[256,2048]{1,0:T(8,128)(2,1)}, bf16[256,2048]{1,0:T(8,128)(2,1)S(1)}, u32[]{:S(2)}, u32[]{:S(2)}) collective-permute-start(bf16[256,2048]{1,0:T(8,128)(2,1)} %get-tuple-element.205), channel_id=1, source_target_pairs={{0,3},{1,2},{2,1},{3,0},{4,7},{5,6},{6,5},{7,4},{8,11},{9,10},{10,... | collective-permute-start | bytes 3145736 | tf_op jit(solution)/shard_map/ppermute | solution.py:39
  378.0 97.6 %collective-permute-start.37 = (bf16[256,2048]{1,0:T(8,128)(2,1)}, bf16[256,2048]{1,0:T(8,128)(2,1)}, u32[]{:S(2)}, u32[]{:S(2)}) collective-permute-start(bf16[256,2048]{1,0:T(8,128)(2,1)} %get-tuple-element.204), channel_id=1, source_target_pairs={{0,2},{1,3},{2,0},{3,1},{4,6},{5,7},{6,4},{7,5},{8,10},{9,11},{10,... | collective-permute-start | bytes 3145736 | tf_op jit(solution)/shard_map/ppermute | solution.py:39
  378.2 97.4 %collective-permute-start.36 = (bf16[256,2048]{1,0:T(8,128)(2,1)}, bf16[256,2048]{1,0:T(8,128)(2,1)}, u32[]{:S(2)}, u32[]{:S(2)}) collective-permute-start(bf16[256,2048]{1,0:T(8,128)(2,1)} %get-tuple-element.203), channel_id=1, source_target_pairs={{0,1},{1,0},{2,3},{3,2},{4,5},{5,4},{6,7},{7,6},{8,9},{9,8},{10,11... | collective-permute-start | bytes 3145736 | tf_op jit(solution)/shard_map/ppermute | solution.py:39
  379.3 100.2 %collective-permute-start.39 = (bf16[4,176,176]{2,1,0:T(8,128)(2,1)S(1)}, bf16[4,176,176]{2,1,0:T(8,128)(2,1)S(1)}, u32[]{:S(2)}, u32[]{:S(2)}) collective-permute-start(bf16[4,176,176]{2,1,0:T(8,128)(2,1)S(1)} %select_add_fusion), channel_id=1, source_target_pairs={{0,8},{4,12},{8,0},{12,4},{16,24},{20,28},{24,16},{28,20},{1,9},{5... | collective-permute-start | bytes 743432 | tf_op jit(solution)/shard_map/ppermute | solution.py:39
  480.0 53.4 %collective-permute-start.44 = (bf16[768,2048]{1,0:T(8,128)(2,1)}, bf16[768,2048]{1,0:T(8,128)(2,1)}, u32[]{:S(2)}, u32[]{:S(2)}) collective-permute-start(bf16[768,2048]{1,0:T(8,128)(2,1)} %get-tuple-element.174.mine_ref), channel_id=1, source_target_pairs={{0,4},{4,0},{8,12},{12,8},{16,20},{20,16},{24,28},{28,24},{1,5},{5... | collective-permute-start | bytes 9437192 | tf_op jit(solution)/shard_map/ppermute | solution.py:39
  497.5 35.7 %collective-permute-start.48 = (bf16[4,176,176]{2,1,0:T(8,128)(2,1)S(1)}, bf16[4,176,176]{2,1,0:T(8,128)(2,1)S(1)}, u32[]{:S(2)}, u32[]{:S(2)}) collective-permute-start(bf16[4,176,176]{2,1,0:T(8,128)(2,1)S(1)} %add.218), channel_id=1, source_target_pairs={{0,16},{4,20},{8,24},{12,28},{16,0},{20,4},{24,8},{28,12},{1,17},{... | collective-permute-start | bytes 743432 | tf_op jit(solution)/shard_map/ppermute | solution.py:39
  509.4 31.1 %collective-permute-start.45 = (f32[10,704]{1,0:T(8,128)S(1)}, f32[10,704]{1,0:T(8,128)S(1)}, u32[]{:S(2)}, u32[]{:S(2)}) collective-permute-start(f32[10,704]{1,0:T(8,128)S(1)} %select_maximum_fusion), channel_id=1, source_target_pairs={{0,4},{4,0},{8,12},{12,8},{16,20},{20,16},{24,28},{28,24},{1,5},{5... | collective-permute-start | bytes 84488 | tf_op jit(solution)/shard_map/ppermute | solution.py:39
  (78 other events, 897.0 us)
Sparse Core Ops, SparseCore 0:
  10.9 150.1 all-gather.4
  163.2 44.0 all-gather.6
  305.6 65.6 reduce-scatter.2
  374.0 45.2 reduce-scatter.4
  420.7 59.2 all-gather.10
  481.6 53.7 all-gather.8

commit v7 on v6

--- a/solution.py
+++ b/solution.py
@@ -53,16 +53,22 @@
     count = lax.axis_size("tp")
     if count != 4:
         whole = jnp.stack([rows] + [swap(rows, "tp", r) for r in range(1, count)])
-        return lambda *after: tied(whole, *after)
+        return lambda *after: after, lambda *after: tied(whole, *after)
     half = rows.shape[0] // 2
-    sides = swap(rows, "tp", 1), swap(rows, "tp", 2)
+    parts = []
+
+    def first(*after):
+        one, two, rest, *after = tied(swap(rows[:half], "tp", 1), swap(rows[:half], "tp", 2), rows[half:], *after)
+        parts.extend([one, two, swap(rest, "tp", 1), swap(rest, "tp", 2)])
+        return after
 
     def finish(*after):
-        one, two, *after = tied(*sides, *after)
-        far = jnp.concatenate([swap(two[:half], "tp", 1), swap(one[half:], "tp", 2)])
-        return (jnp.stack([rows, one, two, far]), *after)
-
-    return finish
+        one, two, one_rest, two_rest, *after = tied(*parts, *after)
+        far, far_rest = swap(two, "tp", 1), swap(one_rest, "tp", 2)
+        whole = jnp.concatenate([rows, one, one_rest, two, two_rest, far, far_rest])
+        return (whole.reshape((count,) + rows.shape), *after)
+
+    return first, finish
 
 
 def scatter_rows(blocks):
@@ -970,7 +976,7 @@
     mid_grad = cotangent.astype(f32) + mid_from_norm
     mid_blocks = gather_rows(mid_grad.astype(bf16))
     mid_blocks, dense_part, rows_z = tied(mid_blocks, dense_part, rows_z)
-    rows_spread = spread(rows_z)
+    spread_first, spread_finish = spread(rows_z)
 
     direct, branch_pre_grad, reach = mix_back(mid_blocks, out_proj, branch_pre, state, keep_prefix)
     branch_pre_grad = branch_pre_grad.reshape(group, width)
@@ -979,7 +985,7 @@
     after = carry_in(ends[0, 0], reach, True)
     out_full = product_left_t(mixed, mid_rows).astype(bf16)
     branch_full = product_left_t(branch_pre_grad, normed).astype(bf16)
-    after, pair_full = tied(after, jnp.concatenate([out_full, branch_full]))
+    after, pair_full = spread_first(*tied(after, jnp.concatenate([out_full, branch_full])))
     pair_part = lax.psum_scatter(pair_full, "seq", scatter_dimension=0, tiled=True)
     tile = lambda v: jnp.broadcast_to(v, (TILE, width))
     rate_low, input_low, inner_grad, tail, rim_grad, sums = recur_backward(
@@ -999,6 +1005,7 @@
         input_dense,
     )
     fixed = tail + from_neighbour(rim_grad, 1)
+    rows_mine, fixed = spread_finish(fixed)
     low_rows = conv_low.reshape(group, width)
     rate_w = diagonal_blocks(product_left_t(low_rows, rate_low.reshape(group, width)), blocks_n)
     input_w = diagonal_blocks(product_left_t(low_rows, input_low.reshape(group, width)), blocks_n)
@@ -1009,16 +1016,18 @@
     ours, theirs = both_halves(rate_w.astype(bf16), input_w.astype(bf16), core)
     block_sum = ours + swap(theirs, "seq", 1)
     normed_part = (product(inner_grad, in_t) + product(branch_pre_grad, branch_t)).astype(bf16)
-    rows_mine, normed_part, in_full = rows_spread(normed_part, in_full)
+    block_other = swap(block_sum, "seq", 2)
+    rows_mine, pair_part = tied(rows_mine, pair_part)
     rows_theirs = swap(rows_mine, "seq", 1)
-    normed_part, in_full, pair_part, rows_mine, rows_theirs, block_sum, dense_part = tied(
-        normed_part, in_full, pair_part, rows_mine, rows_theirs, block_sum, dense_part
-    )
+    normed_part, in_full, pair_part, rows_mine, rows_theirs, block_other, dense_part = tied(
+        normed_part, in_full, pair_part, rows_mine, rows_theirs, block_other, dense_part
+    )
+    block_sum = block_sum + block_other
     pair_sum = lax.all_gather(pair_part, "seq", axis=0, tiled=True)
     in_part = lax.psum_scatter(in_full, "seq", scatter_dimension=0, tiled=True)
     split = lambda rows: rows.reshape(tp_size, length, model)
     grad_and_out = scatter_rows(jnp.concatenate([split(normed_part), split(dense_part)], axis=1))
-    block_other = swap(block_sum, "seq", 2)
+    block_other = swap(block_sum, "seq", 4)
 
     places = jnp.stack([core, tp_place]).astype(jnp.int32)
     blocked = lambda rows: rows.reshape(tp_size, chips, length, model)
@@ -1030,7 +1039,7 @@
     )
     normed_grad, dense_out = grad_and_out[:length], grad_and_out[length:]
     block_sum = block_sum + block_other
-    bit = 4
+    bit = 8
     while bit < seq_size:
         block_sum = block_sum + swap(block_sum, "seq", bit)
         bit *= 2

time: 581 us -> 559 us (0.962)
  waiting for transfers between devices: 185 us -> 164 us
    ppermute x44 -> x46, waiting for transfers between devices: 176 us -> 151 us  [swap(): return lax.ppermute(value, axis, [(i, i ^ bit) for i in range(count)])]
    unnamed x96 -> x104, local copies, waits for them, and re-layouts: 13.5 us -> 22.3 us
    ppermute x44 -> x46, starting transfers between devices: 57.2 us -> 55.1 us  [swap(): return lax.ppermute(value, axis, [(i, i ^ bit) for i in range(count)])]
  transfers between devices with their start and end apart: 56 -> 58, of which waited for: 25 -> 28; matrix products, arithmetic and copies ran while one was open for 15% -> 15% of each run, Pallas kernels for 36% -> 37%
where the time goes in v7:
time: 559 us; the launch traced here: 551 us
  Pallas kernels  204 us (36%)
  waiting for transfers between devices  164 us (29%)
  starting transfers between devices  62.2 us (11%)
  local copies, waits for them, and re-layouts  42.5 us (8%)
  other arithmetic  41.6 us (7%)
  matrix products  21 us (4%)
  between operations  15.4 us (3%)
    ppermute x46, waiting for transfers between devices, swap(): return lax.ppermute(value, axis, [(i, i ^ bit) for i in range(count)])  151 us
    pallas_call x1, Pallas kernels, dense_weight_grads(): pl.pallas_call(kernel, grid_spec=pltpu.PrefetchScalarGridSpec(num_scalar_...  94.9 us
    ppermute x46, starting transfers between devices, swap(): return lax.ppermute(value, axis, [(i, i ^ bit) for i in range(count)])  55.1 us
    pallas_call x1, Pallas kernels, dense_rows(): pl.pallas_call(kernel, grid_spec=pltpu.PrefetchScalarGridSpec(num_scalar_...  24.9 us
    pallas_call x3, Pallas kernels, joined(): pl.pallas_call(kernel, grid_spec=pltpu.PrefetchScalarGridSpec(num_scalar_...  24.2 us
    unnamed x104, local copies, waits for them, and re-layouts  22.3 us
    pallas_call x1, Pallas kernels, recur_backward(): pl.pallas_call(backward_kernel, grid_spec=pltpu.PrefetchScalarGridSpec(nu...  19.5 us
    pallas_call x1, Pallas kernels, recur_forward(): pl.pallas_call(forward_kernel, grid_spec=pltpu.PrefetchScalarGridSpec(num...  15.2 us
  transfers between devices with their start and end apart: 58, of which 28 were waited for; matrix products, arithmetic and copies ran while one was open for 15% of the time, Pallas kernels for 37%

profile of v7, /device:TPU:0, one launch (start us, length us, event | category | flops | bytes accessed | tf_op | source)
XLA Modules:
  0.0 551.0 jit_solution(14355217074723659206)
XLA Ops:
  13.9 10.3 %collective-permute-done.refs_1_ = bf16[128,2048]{1,0:T(8,128)(2,1)S(1)} collective-permute-done((bf16[128,2048]{1,0:T(8,128)(2,1)}, bf16[128,2048]{1,0:T(8,128)(2,1)S(1)}, u32[]{:S(2)}, u32[]{:S(2)}) %collective-permute-start) | collective-permute-done | bytes 524320 | tf_op jit(solution)/shard_map/ppermute | solution.py:39
  41.9 7.0 %norm_project.1 = (bf16[512,2048]{1,0:T(8,128)(2,1)}, f32[4,128,704]{2,1,0:T(8,128)S(1)}) custom-call(s32[1]{0:T(128)} %bitcast.place_ref, bf16[128,2048]{1,0:T(8,128)(2,1)S(1)} %copy-done.7, bf16[128,2048]{1,0:T(8,128)(2,1)S(1)} %collective-permute-done.refs_1_, bf16[128,2048]{1,0:T(8,128)(2,1)S(1)} %collective-permute-done.1.refs_2_, ...), custom_call_target="tpu_custom_call" | custom-call | tf_op jit(solution)/shard_map/norm_project/pallas_call | solution.py:731
  53.8 15.2 %recur_forward.1 = (f32[4,128,704]{2,1,0:T(8,128)}, bf16[4,128,704]{2,1,0:T(8,128)(2,1)S(1)}, f32[4,128,704]{2,1,0:T(8,128)}, f32[4,128,704]{2,1,0:T(8,128)}, f3...) custom-call(f32[4,128,704]{2,1,0:T(8,128)} %copy-done, ...), custom_call_target="tpu_custom_call" | custom-call | tf_op jit(solution)/shard_map/recur_forward/pallas_call | solution.py:756
  69.0 6.4 %collective-permute-start.10 = (f32[2,704]{1,0:T(2,128)S(1)}, f32[2,704]{1,0:T(2,128)S(1)}, u32[]{:S(2)}, u32[]{:S(2)}) collective-permute-start(f32[2,704]{1,0:T(2,128)S(1)} %pad_maximum_fusion.6), channel_id=1, source_target_pairs={{0,4},{4,0},{8,12},{12,8},{16,20},{20,16},{24,28},{28,24},{1,5},{5... | collective-permute-start | bytes 16904 | tf_op jit(solution)/shard_map/ppermute | solution.py:39
  91.2 6.4 %mix_out.1 = (f32[4,128,704]{2,1,0:T(8,128)S(1)}, bf16[4,128,704]{2,1,0:T(8,128)(2,1)S(1)}, bf16[4,128,2048]{2,1,0:T(8,128)(2,1)}) custom-call(f32[4,128,704]{2,1,0:T(8,128)S(1)} %copy-done.14, f32[4,128,704]{2,1,0:T(8,128)} %get-tuple-element.128.keep_ref, f32[4,128,704]{2,1,0:T(8,128)} %bitcast.133, f32[1,704]{1,0:T(1,128)S(1)} %get-tuple-element.210.in_ref, ...), custom_call_target="tpu_custom_call" | custom-call | tf_op jit(solution)/shard_map/mix_out/pallas_call | solution.py:382
  103.5 23.4 %collective-permute-done.15 = bf16[128,2048]{1,0:T(8,128)(2,1)S(1)} collective-permute-done((bf16[128,2048]{1,0:T(8,128)(2,1)S(1)}, bf16[128,2048]{1,0:T(8,128)(2,1)S(1)}, u32[]{:S(2)}, u32[]{:S(2)}) %collective-permute-start.15) | collective-permute-done | bytes 524320 | tf_op jit(solution)/shard_map/ppermute | solution.py:39
  126.9 8.8 %collective-permute-done.14 = bf16[128,2048]{1,0:T(8,128)(2,1)S(1)} collective-permute-done((bf16[128,2048]{1,0:T(8,128)(2,1)S(1)}, bf16[128,2048]{1,0:T(8,128)(2,1)S(1)}, u32[]{:S(2)}, u32[]{:S(2)}) %collective-permute-start.14) | collective-permute-done | bytes 524320 | tf_op jit(solution)/shard_map/ppermute | solution.py:39
  147.9 11.1 %collective-permute-done.16 = bf16[128,2048]{1,0:T(8,128)(2,1)} collective-permute-done((bf16[128,2048]{1,0:T(8,128)(2,1)S(1)}, bf16[128,2048]{1,0:T(8,128)(2,1)}, u32[]{:S(2)}, u32[]{:S(2)}) %collective-permute-start.16) | collective-permute-done | bytes 524320 | tf_op jit(solution)/shard_map/ppermute | solution.py:39
  161.0 6.9 %collective-permute-done.17 = bf16[128,2048]{1,0:T(8,128)(2,1)S(1)} collective-permute-done((bf16[128,2048]{1,0:T(8,128)(2,1)S(1)}, bf16[128,2048]{1,0:T(8,128)(2,1)S(1)}, u32[]{:S(2)}, u32[]{:S(2)}) %collective-permute-start.17) | collective-permute-done | bytes 524320 | tf_op jit(solution)/shard_map/ppermute | solution.py:39
  169.9 24.9 %dense_rows.1 = (bf16[512,1536]{1,0:T(8,128)(2,1)S(1)}, bf16[512,2048]{1,0:T(8,128)(2,1)S(1)}) custom-call(s32[1]{0:T(128)} %bitcast.19.place_ref, bf16[512,2048]{1,0:T(8,128)(2,1)} %bitcast.148, bf16[4096,2048]{1,0:T(8,128)(2,1)} %all-gather.5.cloned.1.call-done.c_ref, bf16[2048,1536]{1,0:T(8,128)(2,1)} %gate_ref.3, bf16[2048,1536]{1,0:T(8,128)(2,1)} %up_ref.3, ...), custom_call_target="tpu_custom_call" | custom-call | tf_op jit(solution)/shard_map/dense_rows/pallas_call | solution.py:313
  203.4 7.4 %collective-permute-done.21 = bf16[128,2048]{1,0:T(8,128)(2,1)S(1)} collective-permute-done((bf16[128,2048]{1,0:T(8,128)(2,1)S(1)}, bf16[128,2048]{1,0:T(8,128)(2,1)S(1)}, u32[]{:S(2)}, u32[]{:S(2)}) %collective-permute-start.21) | collective-permute-done | bytes 524320 | tf_op jit(solution)/shard_map/ppermute | solution.py:39
  210.8 8.6 %collective-permute-done.20 = bf16[128,2048]{1,0:T(8,128)(2,1)S(1)} collective-permute-done((bf16[128,2048]{1,0:T(8,128)(2,1)S(1)}, bf16[128,2048]{1,0:T(8,128)(2,1)S(1)}, u32[]{:S(2)}, u32[]{:S(2)}) %collective-permute-start.20) | collective-permute-done | bytes 524320 | tf_op jit(solution)/shard_map/ppermute | solution.py:39
  227.4 11.5 %collective-permute-done.22 = bf16[128,2048]{1,0:T(8,128)(2,1)S(1)} collective-permute-done((bf16[128,2048]{1,0:T(8,128)(2,1)}, bf16[128,2048]{1,0:T(8,128)(2,1)S(1)}, u32[]{:S(2)}, u32[]{:S(2)}) %collective-permute-start.22) | collective-permute-done | bytes 524320 | tf_op jit(solution)/shard_map/ppermute | solution.py:39
  239.8 10.6 %collective-permute-done.23 = bf16[128,2048]{1,0:T(8,128)(2,1)S(1)} collective-permute-done((bf16[128,2048]{1,0:T(8,128)(2,1)}, bf16[128,2048]{1,0:T(8,128)(2,1)S(1)}, u32[]{:S(2)}, u32[]{:S(2)}) %collective-permute-start.23) | collective-permute-done | bytes 524320 | tf_op jit(solution)/shard_map/ppermute | solution.py:39
  257.3 8.0 %mix_back.1 = (f32[4,128,704]{2,1,0:T(8,128)S(1)}, bf16[4,128,704]{2,1,0:T(8,128)(2,1)S(1)}, f32[1,704]{1,0:T(1,128)S(1)}) custom-call(bf16[4,128,2048]{2,1,0:T(8,128)(2,1)} %bitcast_dynamic-update-slice_fusion.mid_ref, bf16[704,2048]{1,0:T(8,128)(2,1)} %out_ref.3, f32[4,128,704]{2,1,0:T(8,128)S(1)} %bitcast.134, f32[4,128,704]{2,1,0:T(8,128)} %copy-done.1, ...), custom_call_target="tpu_custom_call" | custom-call | tf_op jit(solution)/shard_map/mix_back/pallas_call | solution.py:434
  285.3 19.5 %recur_backward.1 = (bf16[4,128,704]{2,1,0:T(8,128)(2,1)S(1)}, bf16[4,128,704]{2,1,0:T(8,128)(2,1)S(1)}, bf16[4,128,704]{2,1,0:T(8,128)(2,1)S(1)}, f32[8,704]{1,...) custom-call(f32[4,128,704]{2,1,0:T(8,128)} %copy-done.13, f32[4,128,704]{2,1,0:T(8,128)} %copy-done.1, ...), custom_call_target="tpu_custom_call" | custom-call | flops 1000 | bytes 1000 | tf_op jit(solution)/shard_map/recur_backward/pallas_call | solution.py:805
  317.9 12.8 %collective-permute-done.34 = bf16[256,2048]{1,0:T(8,128)(2,1)S(1)} collective-permute-done((bf16[256,2048]{1,0:T(8,128)(2,1)}, bf16[256,2048]{1,0:T(8,128)(2,1)S(1)}, u32[]{:S(2)}, u32[]{:S(2)}) %collective-permute-start.34) | collective-permute-done | bytes 1048608 | tf_op jit(solution)/shard_map/ppermute | solution.py:39
  335.7 11.4 %reduce-scatter.3.cloned.1.call-done = bf16[176,2048]{1,0:T(8,128)(2,1)} async-done(((bf16[1408,2048]{1,0:T(8,128)(2,1)}), bf16[176,2048]{1,0:T(8,128)(2,1)}) %reduce-scatter.3.cloned.1.call-update) | async-done | bytes 720912 | tf_op jit(solution)/shard_map/reduce_scatter | solution.py:989
  350.9 9.9 %collective-permute-done.37 = bf16[4,176,176]{2,1,0:T(8,128)(2,1)S(1)} collective-permute-done((bf16[4,176,176]{2,1,0:T(8,128)(2,1)S(1)}, bf16[4,176,176]{2,1,0:T(8,128)(2,1)S(1)}, u32[]{:S(2)}, u32[]{:S(2)}) %collective-permute-start.37) | collective-permute-done | bytes 247840 | tf_op jit(solution)/shard_map/ppermute | solution.py:39
  381.6 94.9 %dense_weight_grads.1 = (bf16[2048,768]{1,0:T(8,128)(2,1)}, bf16[2048,768]{1,0:T(8,128)(2,1)}, bf16[768,2048]{1,0:T(8,128)(2,1)}) custom-call(s32[2]{0:T(128)} %pad_add_fusion.2.core_ref, bf16[4,4,128,2048]{3,2,1,0:T(8,128)(2,1)} %bitcast.50.mine_ref, bf16[4,4,128,2048]{3,2,1,0:T(8,128)(2,1)} %bitcast.51.theirs_ref, bf16[4,2,4,128,2048]{4,3,2,1,0:T(8,128)(2,1)} %bitcast.143, ...), custom_call_target="tpu_custom_call" | custom-call | flops 1000 | bytes 1000 | tf_op jit(solution)/shard_map/dense_weight_grads/pallas_call | solution.py:203
  488.3 8.4 %joined.3 = f32[2048,1536]{1,0:T(8,128)} custom-call(s32[2]{0:T(128)S(1)} %copy-done.16, bf16[2048,768]{1,0:T(8,128)(2,1)S(1)} %copy-done.10, bf16[2048,768]{1,0:T(8,128)(2,1)} %collective-permute-done.43.theirs_ref), custom_call_target="tpu_custom_call" | custom-call | bytes 18874368 | tf_op jit(solution)/shard_map/joined/pallas_call | solution.py:267
  500.2 8.7 %joined.4 = f32[2048,1536]{1,0:T(8,128)} custom-call(s32[2]{0:T(128)S(1)} %copy-done.16, bf16[2048,768]{1,0:T(8,128)(2,1)S(1)} %copy-done.9, bf16[2048,768]{1,0:T(8,128)(2,1)} %collective-permute-done.45.theirs_ref), custom_call_target="tpu_custom_call" | custom-call | bytes 18874368 | tf_op jit(solution)/shard_map/joined/pallas_call | solution.py:267
  509.7 7.0 %joined.5 = f32[2,768,2048]{2,1,0:T(8,128)} custom-call(s32[2]{0:T(128)S(1)} %copy-done.16, bf16[768,2048]{1,0:T(8,128)(2,1)S(1)} %copy-done.8, bf16[768,2048]{1,0:T(8,128)(2,1)} %collective-permute-done.47.theirs_ref), custom_call_target="tpu_custom_call" | custom-call | bytes 18874368 | tf_op jit(solution)/shard_map/joined/pallas_call | solution.py:267
  530.1 8.7 %slice_convert_fusion = (f32[704,2048]{1,0:T(8,128)}, f32[704,2048]{1,0:T(8,128)}) fusion(bf16[1408,2048]{1,0:T(8,128)(2,1)} %all-gather.11.cloned.1.call-done), kind=kLoop, calls=%fused_computation.15 | loop fusion | flops 2883584 | bytes 17301504 | tf_op jit(solution)/shard_map/convert_element_type | solution.py:1053
  (332 shorter events, 187.6 us)
Async XLA Ops:
  7.2 162.7 %all-gather.5.cloned.1.call-start = ((), (), s32[]{:S(2)}) async-start(), calls=%async_computation.2 | async-start | bytes 17301504 | tf_op jit(solution)/shard_map/all_gather | solution.py:947
  7.9 244.1 %all-gather.7.cloned.1.call-start = ((), (), s32[]{:S(2)}) async-start(), calls=%async_computation.3 | async-start | bytes 2621440 | tf_op jit(solution)/shard_map/all_gather | solution.py:967
  11.0 26.8 %collective-permute-start.1 = (bf16[128,2048]{1,0:T(8,128)(2,1)}, bf16[128,2048]{1,0:T(8,128)(2,1)S(1)}, u32[]{:S(2)}, u32[]{:S(2)}) collective-permute-start(bf16[128,2048]{1,0:T(8,128)(2,1)} %refs_0_), channel_id=1, source_target_pairs={{0,2},{1,3},{2,0},{3,1},{4,6},{5,7},{6,4},{7,5},{8,10},{9,11},{10,... | collective-permute-start | bytes 1572872 | tf_op jit(solution)/shard_map/ppermute | solution.py:39
  12.5 26.9 %collective-permute-start.2 = (bf16[128,2048]{1,0:T(8,128)(2,1)}, bf16[128,2048]{1,0:T(8,128)(2,1)S(1)}, u32[]{:S(2)}, u32[]{:S(2)}) collective-permute-start(bf16[128,2048]{1,0:T(8,128)(2,1)} %refs_0_), channel_id=1, source_target_pairs={{0,3},{1,2},{2,1},{3,0},{4,7},{5,6},{6,5},{7,4},{8,11},{9,10},{10,... | collective-permute-start | bytes 1572872 | tf_op jit(solution)/shard_map/ppermute | solution.py:39
  100.0 27.0 %collective-permute-start.15 = (bf16[128,2048]{1,0:T(8,128)(2,1)S(1)}, bf16[128,2048]{1,0:T(8,128)(2,1)S(1)}, u32[]{:S(2)}, u32[]{:S(2)}) collective-permute-start(bf16[128,2048]{1,0:T(8,128)(2,1)S(1)} %get-tuple-element.230), channel_id=1, source_target_pairs={{0,3},{1,2},{2,1},{3,0},{4,7},{5,6},{6,5},{7,4},{8,11},{9,10},{10,... | collective-permute-start | bytes 1572872 | tf_op jit(solution)/shard_map/ppermute | solution.py:39
  100.1 35.7 %collective-permute-start.14 = (bf16[128,2048]{1,0:T(8,128)(2,1)S(1)}, bf16[128,2048]{1,0:T(8,128)(2,1)S(1)}, u32[]{:S(2)}, u32[]{:S(2)}) collective-permute-start(bf16[128,2048]{1,0:T(8,128)(2,1)S(1)} %get-tuple-element.231), channel_id=1, source_target_pairs={{0,2},{1,3},{2,0},{3,1},{4,6},{5,7},{6,4},{7,5},{8,10},{9,11},{10,... | collective-permute-start | bytes 1572872 | tf_op jit(solution)/shard_map/ppermute | solution.py:39
  100.3 39.7 %collective-permute-start.13 = (bf16[128,2048]{1,0:T(8,128)(2,1)S(1)}, bf16[128,2048]{1,0:T(8,128)(2,1)S(1)}, u32[]{:S(2)}, u32[]{:S(2)}) collective-permute-start(bf16[128,2048]{1,0:T(8,128)(2,1)S(1)} %get-tuple-element.229), channel_id=1, source_target_pairs={{0,1},{1,0},{2,3},{3,2},{4,5},{5,4},{6,7},{7,6},{8,9},{9,8},{10,11... | collective-permute-start | bytes 1572872 | tf_op jit(solution)/shard_map/ppermute | solution.py:39
  147.6 199.5 %reduce-scatter.3.cloned.1.call-start = ((), (), s32[]{:S(2)}) async-start(), calls=%async_computation.4 | async-start | bytes 6488064 | tf_op jit(solution)/shard_map/reduce_scatter | solution.py:989
  225.3 25.0 %collective-permute-start.23 = (bf16[128,2048]{1,0:T(8,128)(2,1)}, bf16[128,2048]{1,0:T(8,128)(2,1)S(1)}, u32[]{:S(2)}, u32[]{:S(2)}) collective-permute-start(bf16[128,2048]{1,0:T(8,128)(2,1)} %get-tuple-element.212), channel_id=1, source_target_pairs={{0,2},{1,3},{2,0},{3,1},{4,6},{5,7},{6,4},{7,5},{8,10},{9,11},{10,... | collective-permute-start | bytes 1572872 | tf_op jit(solution)/shard_map/ppermute | solution.py:39
  225.9 25.2 %collective-permute-start.24 = (bf16[128,2048]{1,0:T(8,128)(2,1)}, bf16[128,2048]{1,0:T(8,128)(2,1)S(1)}, u32[]{:S(2)}, u32[]{:S(2)}) collective-permute-start(bf16[128,2048]{1,0:T(8,128)(2,1)} %get-tuple-element.212), channel_id=1, source_target_pairs={{0,3},{1,2},{2,1},{3,0},{4,7},{5,6},{6,5},{7,4},{8,11},{9,10},{10,... | collective-permute-start | bytes 1572872 | tf_op jit(solution)/shard_map/ppermute | solution.py:39
  255.2 27.8 %collective-permute-start.25 = (bf16[256,2048]{1,0:T(8,128)(2,1)}, bf16[256,2048]{1,0:T(8,128)(2,1)}, u32[]{:S(2)}, u32[]{:S(2)}) collective-permute-start(bf16[256,2048]{1,0:T(8,128)(2,1)} %get-tuple-element.225), channel_id=1, source_target_pairs={{0,1},{1,0},{2,3},{3,2},{4,5},{5,4},{6,7},{7,6},{8,9},{9,8},{10,11... | collective-permute-start | bytes 3145736 | tf_op jit(solution)/shard_map/ppermute | solution.py:39
  255.6 27.5 %collective-permute-start.26 = (bf16[256,2048]{1,0:T(8,128)(2,1)}, bf16[256,2048]{1,0:T(8,128)(2,1)}, u32[]{:S(2)}, u32[]{:S(2)}) collective-permute-start(bf16[256,2048]{1,0:T(8,128)(2,1)} %get-tuple-element.225), channel_id=1, source_target_pairs={{0,2},{1,3},{2,0},{3,1},{4,6},{5,7},{6,4},{7,5},{8,10},{9,11},{10,... | collective-permute-start | bytes 3145736 | tf_op jit(solution)/shard_map/ppermute | solution.py:39
  283.1 197.3 %reduce-scatter.5.cloned.1.call-start = ((), (), s32[]{:S(2)}) async-start(), calls=%async_computation.5 | async-start | bytes 3244032 | tf_op jit(solution)/shard_map/reduce_scatter | solution.py:1027
  283.2 24.3 %collective-permute-start.30 = (bf16[256,2048]{1,0:T(8,128)(2,1)}, bf16[256,2048]{1,0:T(8,128)(2,1)S(1)}, u32[]{:S(2)}, u32[]{:S(2)}) collective-permute-start(bf16[256,2048]{1,0:T(8,128)(2,1)} %get-tuple-element.160), channel_id=1, source_target_pairs={{0,1},{1,0},{2,3},{3,2},{4,5},{5,4},{6,7},{7,6},{8,9},{9,8},{10,11... | collective-permute-start | bytes 3145736 | tf_op jit(solution)/shard_map/ppermute | solution.py:39
  283.2 24.3 %collective-permute-start.31 = (bf16[256,2048]{1,0:T(8,128)(2,1)}, bf16[256,2048]{1,0:T(8,128)(2,1)S(1)}, u32[]{:S(2)}, u32[]{:S(2)}) collective-permute-start(bf16[256,2048]{1,0:T(8,128)(2,1)} %get-tuple-element.160), channel_id=1, source_target_pairs={{0,2},{1,3},{2,0},{3,1},{4,6},{5,7},{6,4},{7,5},{8,10},{9,11},{10,... | collective-permute-start | bytes 3145736 | tf_op jit(solution)/shard_map/ppermute | solution.py:39
  310.6 24.0 %collective-permute-start.35 = (bf16[256,2048]{1,0:T(8,128)(2,1)S(1)}, bf16[256,2048]{1,0:T(8,128)(2,1)S(1)}, u32[]{:S(2)}, u32[]{:S(2)}) collective-permute-start(bf16[256,2048]{1,0:T(8,128)(2,1)S(1)} %collective-permute-done.30), channel_id=1, source_target_pairs={{0,2},{1,3},{2,0},{3,1},{4,6},{5,7},{6,4},{7,5},{8,10},{9,11},{10,... | collective-permute-start | bytes 3145736 | tf_op jit(solution)/shard_map/ppermute | solution.py:39
  347.1 24.4 %collective-permute-start.36 = (bf16[4,512,2048]{2,1,0:T(8,128)(2,1)}, bf16[4,512,2048]{2,1,0:T(8,128)(2,1)}, u32[]{:S(2)}, u32[]{:S(2)}) collective-permute-start(bf16[4,512,2048]{2,1,0:T(8,128)(2,1)} %bitcast.39), channel_id=1, source_target_pairs={{0,4},{4,0},{8,12},{12,8},{16,20},{20,16},{24,28},{28,24},{1,5},{5... | collective-permute-start | bytes 25165832 | tf_op jit(solution)/shard_map/ppermute | solution.py:39
  371.6 158.6 %all-gather.11.cloned.1.call-start = ((), (), s32[]{:S(2)}) async-start(), calls=%async_computation.7 | async-start | bytes 6488064 | tf_op jit(solution)/shard_map/all_gather | solution.py:1026
  372.1 166.7 %all-gather.9.cloned.1.call-start = ((), (), s32[]{:S(2)}) async-start(), calls=%async_computation.6 | async-start | bytes 3244032 | tf_op jit(solution)/shard_map/all_gather | solution.py:1046
  375.8 100.7 %collective-permute-start.41 = (bf16[256,2048]{1,0:T(8,128)(2,1)}, bf16[256,2048]{1,0:T(8,128)(2,1)S(1)}, u32[]{:S(2)}, u32[]{:S(2)}) collective-permute-start(bf16[256,2048]{1,0:T(8,128)(2,1)} %get-tuple-element.221), channel_id=1, source_target_pairs={{0,3},{1,2},{2,1},{3,0},{4,7},{5,6},{6,5},{7,4},{8,11},{9,10},{10,... | collective-permute-start | bytes 3145736 | tf_op jit(solution)/shard_map/ppermute | solution.py:39
  378.1 98.4 %collective-permute-start.40 = (bf16[256,2048]{1,0:T(8,128)(2,1)}, bf16[256,2048]{1,0:T(8,128)(2,1)}, u32[]{:S(2)}, u32[]{:S(2)}) collective-permute-start(bf16[256,2048]{1,0:T(8,128)(2,1)} %get-tuple-element.220), channel_id=1, source_target_pairs={{0,2},{1,3},{2,0},{3,1},{4,6},{5,7},{6,4},{7,5},{8,10},{9,11},{10,... | collective-permute-start | bytes 3145736 | tf_op jit(solution)/shard_map/ppermute | solution.py:39
  378.7 97.8 %collective-permute-start.39 = (bf16[256,2048]{1,0:T(8,128)(2,1)}, bf16[256,2048]{1,0:T(8,128)(2,1)}, u32[]{:S(2)}, u32[]{:S(2)}) collective-permute-start(bf16[256,2048]{1,0:T(8,128)(2,1)} %get-tuple-element.219), channel_id=1, source_target_pairs={{0,1},{1,0},{2,3},{3,2},{4,5},{5,4},{6,7},{7,6},{8,9},{9,8},{10,11... | collective-permute-start | bytes 3145736 | tf_op jit(solution)/shard_map/ppermute | solution.py:39
  381.1 99.3 %collective-permute-start.42 = (bf16[4,176,176]{2,1,0:T(8,128)(2,1)S(1)}, bf16[4,176,176]{2,1,0:T(8,128)(2,1)S(1)}, u32[]{:S(2)}, u32[]{:S(2)}) collective-permute-start(bf16[4,176,176]{2,1,0:T(8,128)(2,1)S(1)} %fusion.57), channel_id=1, source_target_pairs={{0,16},{4,20},{8,24},{12,28},{16,0},{20,4},{24,8},{28,12},{1,17},{... | collective-permute-start | bytes 743432 | tf_op jit(solution)/shard_map/ppermute | solution.py:39
  480.9 28.8 %collective-permute-start.47 = (bf16[768,2048]{1,0:T(8,128)(2,1)}, bf16[768,2048]{1,0:T(8,128)(2,1)}, u32[]{:S(2)}, u32[]{:S(2)}) collective-permute-start(bf16[768,2048]{1,0:T(8,128)(2,1)} %get-tuple-element.190.mine_ref), channel_id=1, source_target_pairs={{0,4},{4,0},{8,12},{12,8},{16,20},{20,16},{24,28},{28,24},{1,5},{5... | collective-permute-start | bytes 9437192 | tf_op jit(solution)/shard_map/ppermute | solution.py:39
  (81 other events, 873.5 us)
Sparse Core Ops, SparseCore 0:
  10.9 150.1 all-gather.4
  163.2 44.0 all-gather.6
  283.2 63.8 reduce-scatter.2
  371.7 49.1 reduce-scatter.4
  422.3 64.1 all-gather.10
  488.0 35.5 all-gather.8

commit v8 on v7

--- a/solution.py
+++ b/solution.py
@@ -1016,8 +1016,8 @@
     ours, theirs = both_halves(rate_w.astype(bf16), input_w.astype(bf16), core)
     block_sum = ours + swap(theirs, "seq", 1)
     normed_part = (product(inner_grad, in_t) + product(branch_pre_grad, branch_t)).astype(bf16)
+    in_full, normed_part, block_sum, pair_part = tied(in_full, normed_part, block_sum, pair_part)
     block_other = swap(block_sum, "seq", 2)
-    rows_mine, pair_part = tied(rows_mine, pair_part)
     rows_theirs = swap(rows_mine, "seq", 1)
     normed_part, in_full, pair_part, rows_mine, rows_theirs, block_other, dense_part = tied(
         normed_part, in_full, pair_part, rows_mine, rows_theirs, block_other, dense_part
@@ -1044,13 +1044,14 @@
         block_sum = block_sum + swap(block_sum, "seq", bit)
         bit *= 2
     in_sum = lax.all_gather(in_part, "seq", axis=0, tiled=True)
-    halves = [(gate_w, swap(gate_w, "seq", 1), 1), (up_w, swap(up_w, "seq", 1), 1), (down_w, swap(down_w, "seq", 1), 0)]
+    out_sum, branch_sum = pair_sum[:width].astype(f32), pair_sum[width:].astype(f32)
+    gate_other, out_sum, branch_sum = tied(swap(gate_w, "seq", 1), out_sum, branch_sum)
+    halves = [(gate_w, gate_other, 1), (up_w, swap(up_w, "seq", 1), 1), (down_w, swap(down_w, "seq", 1), 0)]
     output = (mid + dense_out).astype(bf16)
     own = tokens.astype(f32)
     own_root = rms(own)
     rows_grad, mixer_gain_part = norm_back(normed_grad, own * own_root, mixer_scale, own_root)
     tokens_grad = mid_grad + rows_grad
-    out_sum, branch_sum = pair_sum[:width].astype(f32), pair_sum[width:].astype(f32)
 
     small = jnp.stack([mixer_gain_part, dense_gain_part])
     whole = []
@@ -1074,7 +1075,6 @@
     decay_sum = 8.0 * jax.nn.sigmoid(-decay_param) * sums[2]
     rate_sum, input_sum = both_halves(block_sum, swap(block_sum, "seq", 1), core)
     rate_sum, input_sum = rate_sum.astype(f32), input_sum.astype(f32)
-    in_sum, out_sum, branch_sum = tied(in_sum, out_sum, branch_sum)
     return (
         output,
         tokens_grad,

time: 559 us -> 560 us (level)
    reduce_scatter x1, waiting for transfers between devices: 11.4 us -> 0.01 us  [shards(): lax.psum_scatter(pair_full, 'seq', scatter_dimension=0, tiled=True)]
    unnamed x104 -> x92, local copies, waits for them, and re-layouts: 22.3 us -> 21.2 us
  transfers between devices with their start and end apart: 58 -> 58, of which waited for: 28 -> 26; matrix products, arithmetic and copies ran while one was open for 15% -> 15% of each run, Pallas kernels for 37% -> 37%
where the time goes in v8:
time: 560 us; the launch traced here: 552 us
  Pallas kernels  204 us (36%)
  waiting for transfers between devices  161 us (29%)
  starting transfers between devices  67.7 us (12%)
  local copies, waits for them, and re-layouts  41.4 us (7%)
  other arithmetic  40.6 us (7%)
  matrix products  22.1 us (4%)
  between operations  15.4 us (3%)
    ppermute x46, waiting for transfers between devices, swap(): return lax.ppermute(value, axis, [(i, i ^ bit) for i in range(count)])  156 us
    pallas_call x1, Pallas kernels, dense_weight_grads(): pl.pallas_call(kernel, grid_spec=pltpu.PrefetchScalarGridSpec(num_scalar_...  94.8 us
    ppermute x46, starting transfers between devices, swap(): return lax.ppermute(value, axis, [(i, i ^ bit) for i in range(count)])  60.5 us
    pallas_call x1, Pallas kernels, dense_rows(): pl.pallas_call(kernel, grid_spec=pltpu.PrefetchScalarGridSpec(num_scalar_...  24.9 us
    pallas_call x3, Pallas kernels, joined(): pl.pallas_call(kernel, grid_spec=pltpu.PrefetchScalarGridSpec(num_scalar_...  24.2 us
    unnamed x92, local copies, waits for them, and re-layouts  21.2 us
    pallas_call x1, Pallas kernels, recur_backward(): pl.pallas_call(backward_kernel, grid_spec=pltpu.PrefetchScalarGridSpec(nu...  19.4 us
    pallas_call x1, Pallas kernels, recur_forward(): pl.pallas_call(forward_kernel, grid_spec=pltpu.PrefetchScalarGridSpec(num...  15.2 us
  transfers between devices with their start and end apart: 58, of which 26 were waited for; matrix products, arithmetic and copies ran while one was open for 15% of the time, Pallas kernels for 37%

profile of v8, /device:TPU:0, one launch (start us, length us, event | category | flops | bytes accessed | tf_op | source)
XLA Modules:
  0.0 552.3 jit_solution(3713392510265658430)
XLA Ops:
  13.9 10.3 %collective-permute-done.refs_1_ = bf16[128,2048]{1,0:T(8,128)(2,1)S(1)} collective-permute-done((bf16[128,2048]{1,0:T(8,128)(2,1)}, bf16[128,2048]{1,0:T(8,128)(2,1)S(1)}, u32[]{:S(2)}, u32[]{:S(2)}) %collective-permute-start) | collective-permute-done | bytes 524320 | tf_op jit(solution)/shard_map/ppermute | solution.py:39
  41.9 7.0 %norm_project.1 = (bf16[512,2048]{1,0:T(8,128)(2,1)}, f32[4,128,704]{2,1,0:T(8,128)S(1)}) custom-call(s32[1]{0:T(128)} %bitcast.place_ref, bf16[128,2048]{1,0:T(8,128)(2,1)S(1)} %copy-done.7, bf16[128,2048]{1,0:T(8,128)(2,1)S(1)} %collective-permute-done.refs_1_, bf16[128,2048]{1,0:T(8,128)(2,1)S(1)} %collective-permute-done.1.refs_2_, ...), custom_call_target="tpu_custom_call" | custom-call | tf_op jit(solution)/shard_map/norm_project/pallas_call | solution.py:731
  53.8 15.2 %recur_forward.1 = (f32[4,128,704]{2,1,0:T(8,128)}, bf16[4,128,704]{2,1,0:T(8,128)(2,1)S(1)}, f32[4,128,704]{2,1,0:T(8,128)}, f32[4,128,704]{2,1,0:T(8,128)}, f3...) custom-call(f32[4,128,704]{2,1,0:T(8,128)} %copy-done, ...), custom_call_target="tpu_custom_call" | custom-call | tf_op jit(solution)/shard_map/recur_forward/pallas_call | solution.py:756
  69.0 6.4 %collective-permute-start.10 = (f32[2,704]{1,0:T(2,128)S(1)}, f32[2,704]{1,0:T(2,128)S(1)}, u32[]{:S(2)}, u32[]{:S(2)}) collective-permute-start(f32[2,704]{1,0:T(2,128)S(1)} %pad_maximum_fusion.6), channel_id=1, source_target_pairs={{0,4},{4,0},{8,12},{12,8},{16,20},{20,16},{24,28},{28,24},{1,5},{5... | collective-permute-start | bytes 16904 | tf_op jit(solution)/shard_map/ppermute | solution.py:39
  91.2 6.4 %mix_out.1 = (f32[4,128,704]{2,1,0:T(8,128)S(1)}, bf16[4,128,704]{2,1,0:T(8,128)(2,1)S(1)}, bf16[4,128,2048]{2,1,0:T(8,128)(2,1)}) custom-call(f32[4,128,704]{2,1,0:T(8,128)S(1)} %copy-done.14, f32[4,128,704]{2,1,0:T(8,128)} %get-tuple-element.130.keep_ref, f32[4,128,704]{2,1,0:T(8,128)} %bitcast.133, f32[1,704]{1,0:T(1,128)S(1)} %get-tuple-element.214.in_ref, ...), custom_call_target="tpu_custom_call" | custom-call | tf_op jit(solution)/shard_map/mix_out/pallas_call | solution.py:382
  103.5 23.4 %collective-permute-done.15 = bf16[128,2048]{1,0:T(8,128)(2,1)S(1)} collective-permute-done((bf16[128,2048]{1,0:T(8,128)(2,1)S(1)}, bf16[128,2048]{1,0:T(8,128)(2,1)S(1)}, u32[]{:S(2)}, u32[]{:S(2)}) %collective-permute-start.15) | collective-permute-done | bytes 524320 | tf_op jit(solution)/shard_map/ppermute | solution.py:39
  126.9 8.8 %collective-permute-done.14 = bf16[128,2048]{1,0:T(8,128)(2,1)S(1)} collective-permute-done((bf16[128,2048]{1,0:T(8,128)(2,1)S(1)}, bf16[128,2048]{1,0:T(8,128)(2,1)S(1)}, u32[]{:S(2)}, u32[]{:S(2)}) %collective-permute-start.14) | collective-permute-done | bytes 524320 | tf_op jit(solution)/shard_map/ppermute | solution.py:39
  147.9 11.1 %collective-permute-done.16 = bf16[128,2048]{1,0:T(8,128)(2,1)} collective-permute-done((bf16[128,2048]{1,0:T(8,128)(2,1)S(1)}, bf16[128,2048]{1,0:T(8,128)(2,1)}, u32[]{:S(2)}, u32[]{:S(2)}) %collective-permute-start.16) | collective-permute-done | bytes 524320 | tf_op jit(solution)/shard_map/ppermute | solution.py:39
  161.8 7.2 %collective-permute-done.18 = bf16[128,2048]{1,0:T(8,128)(2,1)S(1)} collective-permute-done((bf16[128,2048]{1,0:T(8,128)(2,1)S(1)}, bf16[128,2048]{1,0:T(8,128)(2,1)S(1)}, u32[]{:S(2)}, u32[]{:S(2)}) %collective-permute-start.18) | collective-permute-done | bytes 524320 | tf_op jit(solution)/shard_map/ppermute | solution.py:39
  169.8 24.9 %dense_rows.1 = (bf16[512,1536]{1,0:T(8,128)(2,1)S(1)}, bf16[512,2048]{1,0:T(8,128)(2,1)S(1)}) custom-call(s32[1]{0:T(128)} %bitcast.19.place_ref, bf16[512,2048]{1,0:T(8,128)(2,1)} %bitcast.148, bf16[4096,2048]{1,0:T(8,128)(2,1)} %all-gather.5.cloned.1.call-done.c_ref, bf16[2048,1536]{1,0:T(8,128)(2,1)} %gate_ref.3, bf16[2048,1536]{1,0:T(8,128)(2,1)} %up_ref.3, ...), custom_call_target="tpu_custom_call" | custom-call | tf_op jit(solution)/shard_map/dense_rows/pallas_call | solution.py:313
  203.4 7.3 %collective-permute-done.21 = bf16[128,2048]{1,0:T(8,128)(2,1)S(1)} collective-permute-done((bf16[128,2048]{1,0:T(8,128)(2,1)S(1)}, bf16[128,2048]{1,0:T(8,128)(2,1)S(1)}, u32[]{:S(2)}, u32[]{:S(2)}) %collective-permute-start.21) | collective-permute-done | bytes 524320 | tf_op jit(solution)/shard_map/ppermute | solution.py:39
  210.7 8.6 %collective-permute-done.20 = bf16[128,2048]{1,0:T(8,128)(2,1)S(1)} collective-permute-done((bf16[128,2048]{1,0:T(8,128)(2,1)S(1)}, bf16[128,2048]{1,0:T(8,128)(2,1)S(1)}, u32[]{:S(2)}, u32[]{:S(2)}) %collective-permute-start.20) | collective-permute-done | bytes 524320 | tf_op jit(solution)/shard_map/ppermute | solution.py:39
  227.4 11.5 %collective-permute-done.22 = bf16[128,2048]{1,0:T(8,128)(2,1)S(1)} collective-permute-done((bf16[128,2048]{1,0:T(8,128)(2,1)}, bf16[128,2048]{1,0:T(8,128)(2,1)S(1)}, u32[]{:S(2)}, u32[]{:S(2)}) %collective-permute-start.22) | collective-permute-done | bytes 524320 | tf_op jit(solution)/shard_map/ppermute | solution.py:39
  239.8 10.5 %collective-permute-done.23 = bf16[128,2048]{1,0:T(8,128)(2,1)S(1)} collective-permute-done((bf16[128,2048]{1,0:T(8,128)(2,1)}, bf16[128,2048]{1,0:T(8,128)(2,1)S(1)}, u32[]{:S(2)}, u32[]{:S(2)}) %collective-permute-start.23) | collective-permute-done | bytes 524320 | tf_op jit(solution)/shard_map/ppermute | solution.py:39
  257.3 8.0 %mix_back.1 = (f32[4,128,704]{2,1,0:T(8,128)S(1)}, bf16[4,128,704]{2,1,0:T(8,128)(2,1)S(1)}, f32[1,704]{1,0:T(1,128)S(1)}) custom-call(bf16[4,128,2048]{2,1,0:T(8,128)(2,1)} %bitcast_dynamic-update-slice_fusion.mid_ref, bf16[704,2048]{1,0:T(8,128)(2,1)} %out_ref.3, f32[4,128,704]{2,1,0:T(8,128)S(1)} %bitcast.134, f32[4,128,704]{2,1,0:T(8,128)} %copy-done.1, ...), custom_call_target="tpu_custom_call" | custom-call | tf_op jit(solution)/shard_map/mix_back/pallas_call | solution.py:434
  285.4 19.4 %recur_backward.1 = (bf16[4,128,704]{2,1,0:T(8,128)(2,1)S(1)}, bf16[4,128,704]{2,1,0:T(8,128)(2,1)S(1)}, bf16[4,128,704]{2,1,0:T(8,128)(2,1)S(1)}, f32[8,704]{1,...) custom-call(f32[4,128,704]{2,1,0:T(8,128)} %copy-done.13, f32[4,128,704]{2,1,0:T(8,128)} %copy-done.1, ...), custom_call_target="tpu_custom_call" | custom-call | flops 1000 | bytes 1000 | tf_op jit(solution)/shard_map/recur_backward/pallas_call | solution.py:805
  318.4 12.1 %collective-permute-done.35 = bf16[256,2048]{1,0:T(8,128)(2,1)S(1)} collective-permute-done((bf16[256,2048]{1,0:T(8,128)(2,1)}, bf16[256,2048]{1,0:T(8,128)(2,1)S(1)}, u32[]{:S(2)}, u32[]{:S(2)}) %collective-permute-start.35) | collective-permute-done | bytes 1048608 | tf_op jit(solution)/shard_map/ppermute | solution.py:39
  340.1 11.0 %collective-permute-done.34 = bf16[4,176,176]{2,1,0:T(8,128)(2,1)S(1)} collective-permute-done((bf16[4,176,176]{2,1,0:T(8,128)(2,1)S(1)}, bf16[4,176,176]{2,1,0:T(8,128)(2,1)S(1)}, u32[]{:S(2)}, u32[]{:S(2)}) %collective-permute-start.34) | collective-permute-done | bytes 247840 | tf_op jit(solution)/shard_map/ppermute | solution.py:39
  365.6 8.9 %collective-permute-done.38 = bf16[4,176,176]{2,1,0:T(8,128)(2,1)S(1)} collective-permute-done((bf16[4,176,176]{2,1,0:T(8,128)(2,1)S(1)}, bf16[4,176,176]{2,1,0:T(8,128)(2,1)S(1)}, u32[]{:S(2)}, u32[]{:S(2)}) %collective-permute-start.38) | collective-permute-done | bytes 247840 | tf_op jit(solution)/shard_map/ppermute | solution.py:39
  387.0 94.8 %dense_weight_grads.1 = (bf16[2048,768]{1,0:T(8,128)(2,1)}, bf16[2048,768]{1,0:T(8,128)(2,1)}, bf16[768,2048]{1,0:T(8,128)(2,1)}) custom-call(s32[2]{0:T(128)} %pad_add_fusion.2.core_ref, bf16[4,4,128,2048]{3,2,1,0:T(8,128)(2,1)} %bitcast.50.mine_ref, bf16[4,4,128,2048]{3,2,1,0:T(8,128)(2,1)} %bitcast.51.theirs_ref, bf16[4,2,4,128,2048]{4,3,2,1,0:T(8,128)(2,1)} %bitcast.143, ...), custom_call_target="tpu_custom_call" | custom-call | flops 1000 | bytes 1000 | tf_op jit(solution)/shard_map/dense_weight_grads/pallas_call | solution.py:203
  491.7 8.8 %slice_convert_fusion = (f32[704,2048]{1,0:T(8,128)}, f32[704,2048]{1,0:T(8,128)}) fusion(bf16[1408,2048]{1,0:T(8,128)(2,1)} %all-gather.9.cloned.1.call-done), kind=kLoop, calls=%fused_computation.15 | loop fusion | flops 2883584 | bytes 17301504 | tf_op jit(solution)/shard_map/convert_element_type | solution.py:1047
  500.5 8.5 %joined.3 = f32[2048,1536]{1,0:T(8,128)} custom-call(s32[2]{0:T(128)S(1)} %copy-done.16, bf16[2048,768]{1,0:T(8,128)(2,1)S(1)} %copy-done.10, bf16[2048,768]{1,0:T(8,128)(2,1)} %collective-permute-done.43.theirs_ref), custom_call_target="tpu_custom_call" | custom-call | bytes 18874368 | tf_op jit(solution)/shard_map/joined/pallas_call | solution.py:267
  511.4 8.7 %joined.4 = f32[2048,1536]{1,0:T(8,128)} custom-call(s32[2]{0:T(128)S(1)} %copy-done.16, bf16[2048,768]{1,0:T(8,128)(2,1)S(1)} %copy-done.9, bf16[2048,768]{1,0:T(8,128)(2,1)} %collective-permute-done.45.theirs_ref), custom_call_target="tpu_custom_call" | custom-call | bytes 18874368 | tf_op jit(solution)/shard_map/joined/pallas_call | solution.py:267
  521.0 7.0 %joined.5 = f32[2,768,2048]{2,1,0:T(8,128)} custom-call(s32[2]{0:T(128)S(1)} %copy-done.16, bf16[768,2048]{1,0:T(8,128)(2,1)S(1)} %copy-done.8, bf16[768,2048]{1,0:T(8,128)(2,1)} %collective-permute-done.47.theirs_ref), custom_call_target="tpu_custom_call" | custom-call | bytes 18874368 | tf_op jit(solution)/shard_map/joined/pallas_call | solution.py:267
  (320 shorter events, 190.9 us)
Async XLA Ops:
  7.2 162.6 %all-gather.5.cloned.1.call-start = ((), (), s32[]{:S(2)}) async-start(), calls=%async_computation.2 | async-start | bytes 17301504 | tf_op jit(solution)/shard_map/all_gather | solution.py:947
  7.9 244.0 %all-gather.7.cloned.1.call-start = ((), (), s32[]{:S(2)}) async-start(), calls=%async_computation.3 | async-start | bytes 2621440 | tf_op jit(solution)/shard_map/all_gather | solution.py:967
  11.0 26.8 %collective-permute-start.1 = (bf16[128,2048]{1,0:T(8,128)(2,1)}, bf16[128,2048]{1,0:T(8,128)(2,1)S(1)}, u32[]{:S(2)}, u32[]{:S(2)}) collective-permute-start(bf16[128,2048]{1,0:T(8,128)(2,1)} %refs_0_), channel_id=1, source_target_pairs={{0,2},{1,3},{2,0},{3,1},{4,6},{5,7},{6,4},{7,5},{8,10},{9,11},{10,... | collective-permute-start | bytes 1572872 | tf_op jit(solution)/shard_map/ppermute | solution.py:39
  12.5 26.9 %collective-permute-start.2 = (bf16[128,2048]{1,0:T(8,128)(2,1)}, bf16[128,2048]{1,0:T(8,128)(2,1)S(1)}, u32[]{:S(2)}, u32[]{:S(2)}) collective-permute-start(bf16[128,2048]{1,0:T(8,128)(2,1)} %refs_0_), channel_id=1, source_target_pairs={{0,3},{1,2},{2,1},{3,0},{4,7},{5,6},{6,5},{7,4},{8,11},{9,10},{10,... | collective-permute-start | bytes 1572872 | tf_op jit(solution)/shard_map/ppermute | solution.py:39
  100.0 27.0 %collective-permute-start.15 = (bf16[128,2048]{1,0:T(8,128)(2,1)S(1)}, bf16[128,2048]{1,0:T(8,128)(2,1)S(1)}, u32[]{:S(2)}, u32[]{:S(2)}) collective-permute-start(bf16[128,2048]{1,0:T(8,128)(2,1)S(1)} %get-tuple-element.234), channel_id=1, source_target_pairs={{0,3},{1,2},{2,1},{3,0},{4,7},{5,6},{6,5},{7,4},{8,11},{9,10},{10,... | collective-permute-start | bytes 1572872 | tf_op jit(solution)/shard_map/ppermute | solution.py:39
  100.0 35.7 %collective-permute-start.14 = (bf16[128,2048]{1,0:T(8,128)(2,1)S(1)}, bf16[128,2048]{1,0:T(8,128)(2,1)S(1)}, u32[]{:S(2)}, u32[]{:S(2)}) collective-permute-start(bf16[128,2048]{1,0:T(8,128)(2,1)S(1)} %get-tuple-element.235), channel_id=1, source_target_pairs={{0,2},{1,3},{2,0},{3,1},{4,6},{5,7},{6,4},{7,5},{8,10},{9,11},{10,... | collective-permute-start | bytes 1572872 | tf_op jit(solution)/shard_map/ppermute | solution.py:39
  100.3 39.7 %collective-permute-start.13 = (bf16[128,2048]{1,0:T(8,128)(2,1)S(1)}, bf16[128,2048]{1,0:T(8,128)(2,1)S(1)}, u32[]{:S(2)}, u32[]{:S(2)}) collective-permute-start(bf16[128,2048]{1,0:T(8,128)(2,1)S(1)} %get-tuple-element.233), channel_id=1, source_target_pairs={{0,1},{1,0},{2,3},{3,2},{4,5},{5,4},{6,7},{7,6},{8,9},{9,8},{10,11... | collective-permute-start | bytes 1572872 | tf_op jit(solution)/shard_map/ppermute | solution.py:39
  147.5 215.2 %reduce-scatter.3.cloned.1.call-start = ((), (), s32[]{:S(2)}) async-start(), calls=%async_computation.4 | async-start | bytes 6488064 | tf_op jit(solution)/shard_map/reduce_scatter | solution.py:989
  225.3 25.0 %collective-permute-start.23 = (bf16[128,2048]{1,0:T(8,128)(2,1)}, bf16[128,2048]{1,0:T(8,128)(2,1)S(1)}, u32[]{:S(2)}, u32[]{:S(2)}) collective-permute-start(bf16[128,2048]{1,0:T(8,128)(2,1)} %get-tuple-element.216), channel_id=1, source_target_pairs={{0,2},{1,3},{2,0},{3,1},{4,6},{5,7},{6,4},{7,5},{8,10},{9,11},{10,... | collective-permute-start | bytes 1572872 | tf_op jit(solution)/shard_map/ppermute | solution.py:39
  225.9 25.2 %collective-permute-start.24 = (bf16[128,2048]{1,0:T(8,128)(2,1)}, bf16[128,2048]{1,0:T(8,128)(2,1)S(1)}, u32[]{:S(2)}, u32[]{:S(2)}) collective-permute-start(bf16[128,2048]{1,0:T(8,128)(2,1)} %get-tuple-element.216), channel_id=1, source_target_pairs={{0,3},{1,2},{2,1},{3,0},{4,7},{5,6},{6,5},{7,4},{8,11},{9,10},{10,... | collective-permute-start | bytes 1572872 | tf_op jit(solution)/shard_map/ppermute | solution.py:39
  255.2 27.9 %collective-permute-start.25 = (bf16[256,2048]{1,0:T(8,128)(2,1)}, bf16[256,2048]{1,0:T(8,128)(2,1)}, u32[]{:S(2)}, u32[]{:S(2)}) collective-permute-start(bf16[256,2048]{1,0:T(8,128)(2,1)} %get-tuple-element.229), channel_id=1, source_target_pairs={{0,1},{1,0},{2,3},{3,2},{4,5},{5,4},{6,7},{7,6},{8,9},{9,8},{10,11... | collective-permute-start | bytes 3145736 | tf_op jit(solution)/shard_map/ppermute | solution.py:39
  255.6 27.5 %collective-permute-start.26 = (bf16[256,2048]{1,0:T(8,128)(2,1)}, bf16[256,2048]{1,0:T(8,128)(2,1)}, u32[]{:S(2)}, u32[]{:S(2)}) collective-permute-start(bf16[256,2048]{1,0:T(8,128)(2,1)} %get-tuple-element.229), channel_id=1, source_target_pairs={{0,2},{1,3},{2,0},{3,1},{4,6},{5,7},{6,4},{7,5},{8,10},{9,11},{10,... | collective-permute-start | bytes 3145736 | tf_op jit(solution)/shard_map/ppermute | solution.py:39
  283.1 202.5 %reduce-scatter.5.cloned.1.call-start = ((), (), s32[]{:S(2)}) async-start(), calls=%async_computation.5 | async-start | bytes 3244032 | tf_op jit(solution)/shard_map/reduce_scatter | solution.py:1027
  283.2 24.3 %collective-permute-start.30 = (bf16[256,2048]{1,0:T(8,128)(2,1)}, bf16[256,2048]{1,0:T(8,128)(2,1)S(1)}, u32[]{:S(2)}, u32[]{:S(2)}) collective-permute-start(bf16[256,2048]{1,0:T(8,128)(2,1)} %get-tuple-element.162), channel_id=1, source_target_pairs={{0,1},{1,0},{2,3},{3,2},{4,5},{5,4},{6,7},{7,6},{8,9},{9,8},{10,11... | collective-permute-start | bytes 3145736 | tf_op jit(solution)/shard_map/ppermute | solution.py:39
  283.3 24.2 %collective-permute-start.31 = (bf16[256,2048]{1,0:T(8,128)(2,1)}, bf16[256,2048]{1,0:T(8,128)(2,1)S(1)}, u32[]{:S(2)}, u32[]{:S(2)}) collective-permute-start(bf16[256,2048]{1,0:T(8,128)(2,1)} %get-tuple-element.162), channel_id=1, source_target_pairs={{0,2},{1,3},{2,0},{3,1},{4,6},{5,7},{6,4},{7,5},{8,10},{9,11},{10,... | collective-permute-start | bytes 3145736 | tf_op jit(solution)/shard_map/ppermute | solution.py:39
  335.5 30.1 %collective-permute-start.37 = (bf16[4,512,2048]{2,1,0:T(8,128)(2,1)}, bf16[4,512,2048]{2,1,0:T(8,128)(2,1)}, u32[]{:S(2)}, u32[]{:S(2)}) collective-permute-start(bf16[4,512,2048]{2,1,0:T(8,128)(2,1)} %bitcast.49), channel_id=1, source_target_pairs={{0,4},{4,0},{8,12},{12,8},{16,20},{20,16},{24,28},{28,24},{1,5},{5... | collective-permute-start | bytes 25165832 | tf_op jit(solution)/shard_map/ppermute | solution.py:39
  374.5 117.2 %all-gather.9.cloned.1.call-start = ((), (), s32[]{:S(2)}) async-start(), calls=%async_computation.6 | async-start | bytes 6488064 | tf_op jit(solution)/shard_map/all_gather | solution.py:1026
  375.1 165.0 %all-gather.11.cloned.1.call-start = ((), (), s32[]{:S(2)}) async-start(), calls=%async_computation.7 | async-start | bytes 3244032 | tf_op jit(solution)/shard_map/all_gather | solution.py:1046
  378.9 102.9 %collective-permute-start.41 = (bf16[256,2048]{1,0:T(8,128)(2,1)}, bf16[256,2048]{1,0:T(8,128)(2,1)S(1)}, u32[]{:S(2)}, u32[]{:S(2)}) collective-permute-start(bf16[256,2048]{1,0:T(8,128)(2,1)} %get-tuple-element.225), channel_id=1, source_target_pairs={{0,3},{1,2},{2,1},{3,0},{4,7},{5,6},{6,5},{7,4},{8,11},{9,10},{10,... | collective-permute-start | bytes 3145736 | tf_op jit(solution)/shard_map/ppermute | solution.py:39
  379.7 102.1 %collective-permute-start.40 = (bf16[256,2048]{1,0:T(8,128)(2,1)}, bf16[256,2048]{1,0:T(8,128)(2,1)}, u32[]{:S(2)}, u32[]{:S(2)}) collective-permute-start(bf16[256,2048]{1,0:T(8,128)(2,1)} %get-tuple-element.224), channel_id=1, source_target_pairs={{0,2},{1,3},{2,0},{3,1},{4,6},{5,7},{6,4},{7,5},{8,10},{9,11},{10,... | collective-permute-start | bytes 3145736 | tf_op jit(solution)/shard_map/ppermute | solution.py:39
  381.6 100.3 %collective-permute-start.39 = (bf16[256,2048]{1,0:T(8,128)(2,1)}, bf16[256,2048]{1,0:T(8,128)(2,1)}, u32[]{:S(2)}, u32[]{:S(2)}) collective-permute-start(bf16[256,2048]{1,0:T(8,128)(2,1)} %get-tuple-element.223), channel_id=1, source_target_pairs={{0,1},{1,0},{2,3},{3,2},{4,5},{5,4},{6,7},{7,6},{8,9},{9,8},{10,11... | collective-permute-start | bytes 3145736 | tf_op jit(solution)/shard_map/ppermute | solution.py:39
  383.1 102.5 %collective-permute-start.42 = (bf16[4,176,176]{2,1,0:T(8,128)(2,1)S(1)}, bf16[4,176,176]{2,1,0:T(8,128)(2,1)S(1)}, u32[]{:S(2)}, u32[]{:S(2)}) collective-permute-start(bf16[4,176,176]{2,1,0:T(8,128)(2,1)S(1)} %add.209), channel_id=1, source_target_pairs={{0,16},{4,20},{8,24},{12,28},{16,0},{20,4},{24,8},{28,12},{1,17},{... | collective-permute-start | bytes 743432 | tf_op jit(solution)/shard_map/ppermute | solution.py:39
  485.7 23.8 %collective-permute-start.45 = (bf16[2048,768]{1,0:T(8,128)(2,1)}, bf16[2048,768]{1,0:T(8,128)(2,1)}, u32[]{:S(2)}, u32[]{:S(2)}) collective-permute-start(bf16[2048,768]{1,0:T(8,128)(2,1)} %get-tuple-element.194.mine_ref), channel_id=1, source_target_pairs={{0,4},{4,0},{8,12},{12,8},{16,20},{20,16},{24,28},{28,24},{1,5},{5... | collective-permute-start | bytes 9437192 | tf_op jit(solution)/shard_map/ppermute | solution.py:39
  486.2 34.8 %collective-permute-start.47 = (bf16[768,2048]{1,0:T(8,128)(2,1)}, bf16[768,2048]{1,0:T(8,128)(2,1)}, u32[]{:S(2)}, u32[]{:S(2)}) collective-permute-start(bf16[768,2048]{1,0:T(8,128)(2,1)} %get-tuple-element.196.mine_ref), channel_id=1, source_target_pairs={{0,4},{4,0},{8,12},{12,8},{16,20},{20,16},{24,28},{28,24},{1,5},{5... | collective-permute-start | bytes 9437192 | tf_op jit(solution)/shard_map/ppermute | solution.py:39
  (75 other events, 839.3 us)
Sparse Core Ops, SparseCore 0:
  10.9 150.0 all-gather.4
  163.2 44.1 all-gather.6
  283.3 64.1 reduce-scatter.2
  374.6 50.2 reduce-scatter.4
  426.5 65.2 all-gather.8
  493.2 36.2 all-gather.10
